TPU v7x, 512 devices: a whole 4x4x16 slice. The times are simulated.
512 devices in a mesh: segment: 8 (over y, core), seq: 16 (over x, z_hi), tp: 4 (over z_lo).
Axes of the slice: x: 4, y: 4, z: 16 (z_hi: 4, z_lo: 4; z = z_hi * 4 + z_lo), core: 2. Of those that a mesh axis runs over, the one named last changes fastest.
Arguments:
- queries: bfloat16 [8, 3072, 4096], P('segment', 'seq', 'tp'), may hold values from -64 to 64
- nb_keys: bfloat16 [8, 48, 256, 4096], P('segment', 'seq', None, 'tp'), may hold values from -24 to 24
- nb_values: bfloat16 [8, 48, 256, 4096], P('segment', 'seq', None, 'tp'), may hold values from -6 to 6
- nb_lengths: int32 [8, 48, 2], P('segment', 'seq'), may hold values from 1 to 128
- slot_stretch: int32 [8, 48], P('segment', 'seq'), may hold values from 0 to 47, as said below
- out_weight: bfloat16 [8, 4096, 4096], P('segment', 'tp', 'seq'), may hold values from -0.09375 to 0.09375
- residual: bfloat16 [8, 3072, 4096], P('segment', 'seq', 'tp'), may hold values from -6 to 6
Outputs:
- mixed: bfloat16 [8, 3072, 4096], P('segment', 'seq', 'tp')
Inputs may be any that keep to these rules, and one draw needn't show every extreme that they name: Each row slot_stretch[e] is a permutation of the 48 stretches. The 3 stretches of one decoder device (stretches i * 3 to i * 3 + 2) are served by slots on 3 different encoder devices, so one decoder device sends at most one stretch to one encoder device.
All inputs are finite; a program needn't handle non-finite values.
Results may differ from a plain program's by a relative error of at most 0.0034.
Values may be sent and summed in bfloat16 or wider, within the bound.
No kernel may reach another device: no remote copies, remote signals or barrier semaphores. Data moves between devices by JAX's collectives and lax.ppermute only.
A program may use at most 64 MiB of HBM per device.

v0:
```python
import math

import jax
import jax.numpy as jnp
from jax import lax
from jax.sharding import PartitionSpec as P

HD = 128
STRETCH = 64
NR = 128


def shifted(value, axis, by):
    size = lax.axis_size(axis)
    return lax.ppermute(value, axis, [(i, (i + by) % size) for i in range(size)])


def attend(query_rows, key_rows, value_rows, lengths):
    count, width, feats = query_rows.shape
    heads = feats // HD
    span = key_rows.shape[1]
    query_heads = query_rows.reshape(count, width, heads, HD)
    key_heads = key_rows.reshape(count, span, heads, HD)
    value_heads = value_rows.reshape(count, span, heads, HD)
    scores = jnp.einsum(
        "cqhd,clhd->chql", query_heads, key_heads, preferred_element_type=jnp.float32
    ) * (1.0 / math.sqrt(HD))
    position = jnp.arange(span, dtype=jnp.int32)
    limits = jnp.take(lengths, position // NR, axis=1)
    valid = ((position % NR)[None, :] < limits)[:, None, None, :]
    highest = jnp.max(jnp.where(valid, scores, -1e30), axis=-1, keepdims=True)
    expo = jnp.exp(jnp.where(valid, scores - highest, -1e30))
    weights = (expo / jnp.sum(expo, axis=-1, keepdims=True)).astype(jnp.bfloat16)
    mixed = jnp.einsum("chql,clhd->cqhd", weights, value_heads, preferred_element_type=jnp.float32)
    return mixed.astype(jnp.bfloat16).reshape(count, width, feats)


def holders_for(table_row, owner_index, per_dev):
    wanted = owner_index * per_dev + jnp.arange(per_dev, dtype=jnp.int32)
    slot_ids = jnp.arange(table_row.shape[0], dtype=jnp.int32)
    matched = table_row[None, :] == wanted[:, None]
    return jnp.sum(jnp.where(matched, slot_ids[None, :] // per_dev, 0), axis=1)


def anchors_for(table_row, holder_index, per_dev):
    return lax.dynamic_slice_in_dim(table_row, holder_index * per_dev, per_dev) // per_dev


def place(blocks_in, targets, count_dev):
    selector = (targets[:, None] == jnp.arange(count_dev, dtype=jnp.int32)[None, :]).astype(
        jnp.bfloat16
    )
    return jnp.einsum(
        "kd,kqf->dqf", selector, blocks_in, preferred_element_type=jnp.float32
    ).astype(jnp.bfloat16)


def local(queries, nb_keys, nb_values, nb_lengths, slot_stretch, out_weight, residual):
    count_dev = lax.axis_size("seq")
    seq_index = lax.axis_index("seq")
    per_dev = slot_stretch.shape[1]
    feats = queries.shape[2]
    key_local = nb_keys[0]
    value_local = nb_values[0]
    length_local = nb_lengths[0]
    blocks = queries[0].reshape(per_dev, STRETCH, feats)
    table_row = lax.all_gather(slot_stretch, "seq", axis=1, tiled=True)[0]
    lowered = shifted(blocks, "segment", -1)
    targets = holders_for(table_row, seq_index, per_dev)
    anchors = anchors_for(table_row, seq_index, per_dev)
    outgoing = place(lowered, targets, count_dev)
    picked = jnp.take(
        lax.all_to_all(outgoing, "seq", split_axis=0, concat_axis=0, tiled=True), anchors, axis=0
    )
    answer = attend(picked, key_local, value_local, length_local)
    returned = lax.all_to_all(
        place(answer, anchors, count_dev), "seq", split_axis=0, concat_axis=0, tiled=True
    )
    gathered = jnp.take(returned, targets, axis=0)
    cca_blocks = shifted(gathered, "segment", 1)
    cca_rows = cca_blocks.reshape(per_dev * STRETCH, feats)
    partial_out = jnp.dot(
        cca_rows,
        lax.all_gather(out_weight[0], "seq", axis=1, tiled=True),
        preferred_element_type=jnp.float32,
    )
    summed = lax.psum_scatter(partial_out, "tp", scatter_dimension=1, tiled=True)
    mixed = (residual[0].astype(jnp.float32) + summed).astype(jnp.bfloat16)
    return mixed[None]


def solution(mesh):
    in_specs = (
        P("segment", "seq", "tp"),
        P("segment", "seq", None, "tp"),
        P("segment", "seq", None, "tp"),
        P("segment", "seq", None),
        P("segment", "seq"),
        P("segment", "tp", "seq"),
        P("segment", "seq", "tp"),
    )
    out_specs = P("segment", "seq", "tp")
    return jax.shard_map(local, mesh=mesh, in_specs=in_specs, out_specs=out_specs, check_vma=False)
```

profile of v0, /device:TPU:1, one launch (start us, length us, event | category | flops | bytes accessed | tf_op | source)
XLA Modules:
  0.0 513.7 jit_solution(2113023838081756587)
XLA Ops:
  6.5 0.0 copy-start
  6.5 1.3 copy.31
  7.9 6.9 %collective-permute-start = (bf16[3,64,1024]{2,0,1:T(4,128)(2,1)S(1)}, bf16[3,64,1024]{2,0,1:T(4,128)(2,1)S(1)}, u32[]{:S(2)}, u32[]{:S(2)}) collective-permute-start(bf16[3,64,1024]{2,0,1:T(4,128)(2,1)S(1)} %copy.31), channel_id=1, source_target_pairs={{0,448},{64,0},{128,64},{192,128},{256,192},{320,256},{384,320},{4... | collective-permute-start | bytes 1179656 | tf_op jit(solution)/shard_map/ppermute | solution.py:15
  14.8 1.3 dynamic-slice.1
  16.7 0.8 bitcast_dynamic-update-slice_fusion
  17.5 22.1 %all-reduce = s32[48]{0:T(128)S(1)} all-reduce(s32[48]{0:T(128)S(1)} %bitcast_dynamic-update-slice_fusion), channel_id=1, replica_groups=mesh['segment'=8,'seq'=16,'tp'=4] {'seq'}, use_global_device_ids=true, to_apply=%add | all-reduce | flops 48 | bytes 384
  39.6 0.2 select_reduce_fusion.1
  39.8 0.0 collective-permute-done
  39.8 0.9 convolution_convert_fusion.1
  40.7 2.5 copy.32
  43.1 0.0 copy-start.1
  43.1 5.6 %all-to-all-start = ((bf16[16,64,1024]{2,1,0:T(8,128)(2,1)}), bf16[16,64,1024]{2,1,0:T(8,128)(2,1)}, u32[]{:S(2)}, u32[]{:S(2)}) async-start(bf16[16,64,1024]{2,1,0:T(8,128)(2,1)} %copy.32), calls=%async_computation | async-start | bytes 4194304 | tf_op jit(solution)/shard_map/all_to_all | solution.py:73
  48.8 0.0 all-gather.3.cloned.1.call-start
  48.8 0.7 all-gather.3.cloned.1.call-update
  49.5 0.0 copy-done.1
  49.5 0.4 copy.42
  50.0 0.0 copy-done
  50.0 0.7 gather_fusion
  50.7 0.1 fusion.26
  50.9 0.1 copy.30
  51.0 1.9 copy.43
  52.8 0.6 compare_and_fusion.1
  53.4 0.0 copy-start.3
  53.5 0.5 copy-done.3
  54.0 109.8 %all-to-all-done = bf16[16,64,1024]{2,1,0:T(8,128)(2,1)} async-done(((bf16[16,64,1024]{2,1,0:T(8,128)(2,1)}), bf16[16,64,1024]{2,1,0:T(8,128)(2,1)}, u32[]{:S(2)}, u32[]{:S(2)}) %all-to-all-start) | async-done | bytes 2097184 | tf_op jit(solution)/shard_map/all_to_all | solution.py:73
  163.7 2.2 gather_fusion.1
  165.9 1.4 fusion.10
  167.3 0.8 fusion.35
  168.1 0.5 fusion.16
  168.6 0.0 copy-start.4
  168.6 0.3 copy.39
  168.8 0.1 reshape.212
  168.9 0.2 copy-done.4
  169.2 0.9 convolution_convert_fusion
  170.0 2.5 copy.38
  172.5 10.6 %all-to-all-start.1 = ((bf16[16,64,1024]{2,1,0:T(8,128)(2,1)}), bf16[16,64,1024]{2,1,0:T(8,128)(2,1)S(1)}, u32[]{:S(2)}, u32[]{:S(2)}) async-start(bf16[16,64,1024]{2,1,0:T(8,128)(2,1)} %copy.38), calls=%async_computation.1 | async-start | bytes 4194304 | tf_op jit(solution)/shard_map/all_to_all | solution.py:76
  183.2 0.0 reduce-scatter.2.cloned.1.call-start
  183.2 134.9 %all-to-all-done.1 = bf16[16,64,1024]{2,1,0:T(8,128)(2,1)S(1)} async-done(((bf16[16,64,1024]{2,1,0:T(8,128)(2,1)}), bf16[16,64,1024]{2,1,0:T(8,128)(2,1)S(1)}, u32[]{:S(2)}, u32[]{:S(2)}) %all-to-all-start.1) | async-done | bytes 2097184 | tf_op jit(solution)/shard_map/all_to_all | solution.py:76
  318.2 0.6 gather_fusion.2
  318.8 0.1 broadcast_select_fusion
  318.9 8.3 %collective-permute-start.1 = (bf16[3,64,1024]{2,1,0:T(8,128)(2,1)S(1)}, bf16[3,64,1024]{2,1,0:T(8,128)(2,1)S(1)}, u32[]{:S(2)}, u32[]{:S(2)}) collective-permute-start(bf16[3,64,1024]{2,1,0:T(8,128)(2,1)S(1)} %broadcast_select_fusion), channel_id=1, source_target_pairs={{0,64},{64,128},{128,192},{192,256},{256,320},{320,384},{384,448},... | collective-permute-start | bytes 1179656 | tf_op jit(solution)/shard_map/ppermute | solution.py:15
  327.1 45.8 %all-gather.3.cloned.1.call-done = bf16[1,1024,4096]{2,1,0:T(8,128)(2,1)} async-done(((bf16[1,1024,256]{2,1,0:T(8,128)(2,1)}), bf16[1,1024,4096]{2,1,0:T(8,128)(2,1)}) %all-gather.3.cloned.1.call-update) | async-done | bytes 8388624 | tf_op jit(solution)/shard_map/all_gather | solution.py:84
  372.9 0.0 collective-permute-done.1
  372.9 6.9 %fusion.1 = f32[192,4096]{1,0:T(8,128)} fusion(bf16[192,1024]{1,0:T(8,128)(2,1)S(1)} %bitcast.54, bf16[1,1024,4096]{2,1,0:T(8,128)(2,1)} %all-gather.3.cloned.1.call-done), kind=kOutput, calls=%fused_computation.4 | convolution fusion | flops 1610612736 | bytes 11927552 | tf_op jit(solution)/shard_map/dot_general | solution.py:82
  379.9 0.0 copy-start.2
  379.9 0.0 reduce-scatter.2.cloned.1.call-update
  379.9 124.9 %reduce-scatter.2.cloned.1.call-done = f32[192,1024]{1,0:T(8,128)} async-done(((f32[192,4096]{1,0:T(8,128)}), f32[192,1024]{1,0:T(8,128)}) %reduce-scatter.2.cloned.1.call-update) | async-done | bytes 786448 | tf_op jit(solution)/shard_map/reduce_scatter | solution.py:87
  504.8 0.0 copy-done.2
  504.8 2.0 fusion.23
  (12 shorter events, 0.1 us)
Async XLA Ops:
  6.5 43.5 %copy-start = (s32[1,3,2]{1,2,0:T(2,128)S(1)}, s32[1,3,2]{1,2,0:T(2,128)}, u32[]{:S(2)}) copy-start(s32[1,3,2]{1,2,0:T(2,128)} %param.12) | copy-start | bytes 76
  7.9 31.9 %collective-permute-start = (bf16[3,64,1024]{2,0,1:T(4,128)(2,1)S(1)}, bf16[3,64,1024]{2,0,1:T(4,128)(2,1)S(1)}, u32[]{:S(2)}, u32[]{:S(2)}) collective-permute-start(bf16[3,64,1024]{2,0,1:T(4,128)(2,1)S(1)} %copy.31), channel_id=1, source_target_pairs={{0,448},{64,0},{128,64},{192,128},{256,192},{320,256},{384,320},{4... | collective-permute-start | bytes 1179656 | tf_op jit(solution)/shard_map/ppermute | solution.py:15
  43.1 6.4 %copy-start.1 = (bf16[1,3,256,1024]{3,2,1,0:T(8,128)(2,1)S(1)}, bf16[1,3,256,1024]{3,2,1,0:T(8,128)(2,1)}, u32[]{:S(2)}) copy-start(bf16[1,3,256,1024]{3,2,1,0:T(8,128)(2,1)} %param.10) | copy-start | bytes 4718596
  43.1 120.6 %all-to-all-start = ((bf16[16,64,1024]{2,1,0:T(8,128)(2,1)}), bf16[16,64,1024]{2,1,0:T(8,128)(2,1)}, u32[]{:S(2)}, u32[]{:S(2)}) async-start(bf16[16,64,1024]{2,1,0:T(8,128)(2,1)} %copy.32), calls=%async_computation | async-start | bytes 4194304 | tf_op jit(solution)/shard_map/all_to_all | solution.py:73
  48.8 324.2 %all-gather.3.cloned.1.call-start = ((), (), s32[]{:S(2)}) async-start(), calls=%async_computation.4 | async-start | bytes 8912896 | tf_op jit(solution)/shard_map/all_gather | solution.py:84
  53.4 0.5 copy-start.3
  168.6 0.6 copy-start.4
  172.5 145.6 %all-to-all-start.1 = ((bf16[16,64,1024]{2,1,0:T(8,128)(2,1)}), bf16[16,64,1024]{2,1,0:T(8,128)(2,1)S(1)}, u32[]{:S(2)}, u32[]{:S(2)}) async-start(bf16[16,64,1024]{2,1,0:T(8,128)(2,1)} %copy.38), calls=%async_computation.1 | async-start | bytes 4194304 | tf_op jit(solution)/shard_map/all_to_all | solution.py:76
  183.2 321.7 %reduce-scatter.2.cloned.1.call-start = ((), (), s32[]{:S(2)}) async-start(), calls=%async_computation.3 | async-start | bytes 3932160 | tf_op jit(solution)/shard_map/reduce_scatter | solution.py:87
  318.9 54.1 %collective-permute-start.1 = (bf16[3,64,1024]{2,1,0:T(8,128)(2,1)S(1)}, bf16[3,64,1024]{2,1,0:T(8,128)(2,1)S(1)}, u32[]{:S(2)}, u32[]{:S(2)}) collective-permute-start(bf16[3,64,1024]{2,1,0:T(8,128)(2,1)S(1)} %broadcast_select_fusion), channel_id=1, source_target_pairs={{0,64},{64,128},{128,192},{192,256},{256,320},{320,384},{384,448},... | collective-permute-start | bytes 1179656 | tf_op jit(solution)/shard_map/ppermute | solution.py:15
  379.9 125.0 %copy-start.2 = (bf16[1,192,1024]{2,1,0:T(8,128)(2,1)S(1)}, bf16[1,192,1024]{2,1,0:T(8,128)(2,1)}, u32[]{:S(2)}) copy-start(bf16[1,192,1024]{2,1,0:T(8,128)(2,1)} %param.15) | copy-start | bytes 1179652
Sparse Core Ops, SparseCore 0:
  52.6 320.2 all-gather.2
  380.0 124.7 reduce-scatter.1
where the time goes:
time: 514 us
  waiting for transfers between devices  416 us (81%)
  starting transfers between devices  31.5 us (6%)
  blocking collectives  22.1 us (4%)
  local copies, waits for them, and re-layouts  15.3 us (3%)
  between operations  14.3 us (3%)
  matrix products  10.5 us (2%)
    all_to_all x1, waiting for transfers between devices, local(): lax.all_to_all(place(answer, anchors, count_dev), 'seq', split_axis=0, co...  135 us
    reduce_scatter x1, waiting for transfers between devices, local(): lax.psum_scatter(partial_out, 'tp', scatter_dimension=1, tiled=True)  125 us
    all_to_all x1, waiting for transfers between devices, local(): lax.all_to_all(outgoing, 'seq', split_axis=0, concat_axis=0, tiled=True)  110 us
    all_gather x1, waiting for transfers between devices, local(): lax.all_gather(out_weight[0], 'seq', axis=1, tiled=True)  45.8 us
    unnamed x1, blocking collectives  22.1 us
    ppermute x2, starting transfers between devices, shifted(): lax.ppermute(value, axis, [(i, (i + by) % size) for i in range(size)])  15.2 us
    all_to_all x1, starting transfers between devices, local(): lax.all_to_all(place(answer, anchors, count_dev), 'seq', split_axis=0, co...  10.6 us
  transfers between devices with their start and end apart: 6, of which 4 were waited for; matrix products, arithmetic and copies ran while one was open for 3% of the time, Pallas kernels for 0%

commit v1 on v0

v1 whole, which is shorter than its diff:
```python
import functools
import math

import jax
import jax.numpy as jnp
from jax import lax
from jax.experimental import pallas as pl
from jax.experimental.pallas import tpu as pltpu
from jax.sharding import Mesh
from jax.sharding import PartitionSpec as P

HD = 128
STRETCH = 64
NR = 128
G = 4
ROWS = STRETCH // G
VMEM = pl.BlockSpec(memory_space=pltpu.VMEM)
SMEM = pl.BlockSpec(memory_space=pltpu.SMEM)
PARAMS = pltpu.CompilerParams(vmem_limit_bytes=40 * 1024 * 1024)
SEQ = ("x", "zh")


def cost(flops, moved, trans=0):
    return pl.CostEstimate(flops=flops, bytes_accessed=moved, transcendentals=trans)


def permute_kernel(order_ref, in_ref, out_ref):
    for slot in range(in_ref.shape[0]):
        out_ref[slot] = in_ref[order_ref[slot]]


def permute_blocks(blocks, order):
    return pl.pallas_call(
        permute_kernel,
        out_shape=jax.ShapeDtypeStruct(blocks.shape, blocks.dtype),
        in_specs=[SMEM, VMEM],
        out_specs=VMEM,
        compiler_params=PARAMS,
        cost_estimate=cost(0, 4 * blocks.size),
        name="permute_blocks",
    )(order, blocks)


def attend_kernel(len_ref, q_ref, k_ref, v_ref, out_ref):
    slot = pl.program_id(0)
    span = k_ref.shape[1]
    heads = k_ref.shape[2] // HD
    per_group = heads // G
    position = lax.broadcasted_iota(jnp.int32, (1, span), 1)
    limit = jnp.where(position < NR, len_ref[slot, 0], len_ref[slot, 1] + NR)
    valid = position < limit
    for head in range(heads):
        lanes = slice(head * HD, (head + 1) * HD)
        part = slice((head % per_group) * HD, (head % per_group + 1) * HD)
        q = q_ref[:, head // per_group, 0, :, part].reshape(STRETCH, HD)
        scores = lax.dot_general(
            q, k_ref[0, :, lanes], (((1,), (1,)), ((), ())), preferred_element_type=jnp.float32
        ) * (1.0 / math.sqrt(HD))
        highest = jnp.max(jnp.where(valid, scores, -1e30), axis=-1, keepdims=True)
        expo = jnp.exp(jnp.where(valid, scores - highest, -1e30))
        weights = (expo / jnp.sum(expo, axis=-1, keepdims=True)).astype(jnp.bfloat16)
        mixed = jnp.dot(weights, v_ref[0, :, lanes], preferred_element_type=jnp.float32)
        out_ref[:, 0, :, lanes] = mixed.astype(jnp.bfloat16).reshape(G, ROWS, HD)


def attend(picked, keys, values, lengths):
    slots, span, feats = keys.shape
    return pl.pallas_call(
        attend_kernel,
        out_shape=jax.ShapeDtypeStruct((G, slots, ROWS, feats), jnp.bfloat16),
        grid=(slots,),
        in_specs=[
            SMEM,
            pl.BlockSpec((G, G, 1, ROWS, feats // G), lambda s: (0, 0, s, 0, 0)),
            pl.BlockSpec((1, span, feats), lambda s: (s, 0, 0)),
            pl.BlockSpec((1, span, feats), lambda s: (s, 0, 0)),
        ],
        out_specs=pl.BlockSpec((G, 1, ROWS, feats), lambda s: (0, s, 0, 0)),
        compiler_params=PARAMS,
        cost_estimate=cost(4 * slots * STRETCH * span * feats, 4 * slots * span * feats),
        name="attend",
    )(lengths, picked, keys, values)


def project_kernel(a_ref, w_ref, out_ref):
    out_ref[0] = jnp.dot(a_ref[...], w_ref[...], preferred_element_type=jnp.float32).astype(
        jnp.bfloat16
    )


def project(rows, weight):
    m, k = rows.shape
    n = weight.shape[1]
    return pl.pallas_call(
        project_kernel,
        out_shape=jax.ShapeDtypeStruct((G, m, n // G), jnp.bfloat16),
        grid=(G,),
        in_specs=[
            pl.BlockSpec((m, k), lambda c: (0, 0)),
            pl.BlockSpec((k, n // G), lambda c: (0, c)),
        ],
        out_specs=pl.BlockSpec((1, m, n // G), lambda c: (c, 0, 0)),
        compiler_params=PARAMS,
        cost_estimate=cost(2 * m * n * k, 2 * (m * k + n * k + m * n)),
        name="project",
    )(rows, weight)


def sum_permute_kernel(order_ref, in_ref, out_ref):
    for place in range(out_ref.shape[0]):
        taken = order_ref[place]
        total = in_ref[0, taken].astype(jnp.float32)
        for part in range(1, in_ref.shape[0]):
            total = total + in_ref[part, taken].astype(jnp.float32)
        out_ref[place] = total.astype(out_ref.dtype)


def sum_permute(parts, order):
    return pl.pallas_call(
        sum_permute_kernel,
        out_shape=jax.ShapeDtypeStruct(parts.shape[1:], parts.dtype),
        in_specs=[SMEM, VMEM],
        out_specs=VMEM,
        compiler_params=PARAMS,
        cost_estimate=cost(parts.size, 3 * parts.size),
        name="sum_permute",
    )(order, parts)


def exchange(value, axes):
    return lax.all_to_all(value, axes, split_axis=0, concat_axis=0, tiled=True)


def local(queries, nb_keys, nb_values, nb_lengths, slot_stretch, out_weight, residual):
    per_dev = slot_stretch.shape[1]
    feats = queries.shape[2]
    part = feats // G
    sections = lax.axis_size("segment")
    count = per_dev * G * G
    back = [(i, (i - 1) % sections) for i in range(sections)]

    weight = lax.ppermute(out_weight[0], "segment", back)
    weight = lax.all_gather(weight, "zh", axis=1, tiled=True)

    table = lax.all_gather(slot_stretch[0], SEQ, axis=0, tiled=True)
    ids = jnp.arange(count, dtype=jnp.int32)
    inverse = jnp.sum(jnp.where(table[None, :] == ids[:, None], ids[None, :], 0), axis=1)

    pieces = queries[0].reshape(per_dev, G, ROWS, G, part).transpose(1, 3, 0, 2, 4)
    pieces = lax.ppermute(pieces, "segment", back)
    spread = exchange(pieces.reshape(G * G, per_dev, ROWS, part), SEQ)
    ordered = permute_blocks(spread.reshape(count, ROWS, part), table)
    picked = exchange(ordered.reshape(G * G, per_dev, ROWS, part), SEQ)

    answer = attend(
        picked.reshape(G, G, per_dev, ROWS, part), nb_keys[0], nb_values[0], nb_lengths[0]
    )
    banded = exchange(answer, "zh")
    everywhere = jnp.broadcast_to(banded[None], (G,) + banded.shape)
    gathered = exchange(everywhere, "x")

    partial = project(gathered.reshape(count * ROWS, feats), weight)
    partial = exchange(partial, "tp").reshape(G, count, ROWS, part)
    summed = sum_permute(partial, inverse)

    moves = []
    for s in range(sections):
        for x in range(G):
            for zh in range(G):
                for t in range(G):
                    source = ((s * G + x) * G + zh) * G + t
                    target = ((((s + 1) % sections) * G + t) * G + zh) * G + x
                    moves.append((source, target))
    turned = lax.ppermute(summed, ("segment", "x", "zh", "tp"), moves)
    owned = exchange(turned.reshape(G * G, per_dev, ROWS, part), SEQ)
    owned = owned.reshape(G, G, per_dev, ROWS, part).transpose(2, 1, 3, 0, 4)
    projected = owned.reshape(per_dev * STRETCH, feats).astype(jnp.float32)
    return (residual[0].astype(jnp.float32) + projected).astype(jnp.bfloat16)[None]


def solution(mesh):
    sections, _, tp = mesh.devices.shape
    inner = Mesh(mesh.devices.reshape(sections, G, G, tp), ("segment", "x", "zh", "tp"))
    in_specs = (
        P("segment", SEQ, "tp"),
        P("segment", SEQ, None, "tp"),
        P("segment", SEQ, None, "tp"),
        P("segment", SEQ, None),
        P("segment", SEQ),
        P("segment", "tp", SEQ),
        P("segment", SEQ, "tp"),
    )
    out_specs = P("segment", SEQ, "tp")
    return jax.shard_map(local, mesh=inner, in_specs=in_specs, out_specs=out_specs, check_vma=False)
```

time: 514 us -> 325 us (0.63)
  waiting for transfers between devices: 416 us -> 108 us
  blocking collectives: 22.1 us -> 130 us
  starting transfers between devices: 31.5 us -> 48.7 us
  Pallas kernels: 0 us -> 13.6 us
  matrix products: 10.5 us -> 0 us
  local copies, waits for them, and re-layouts: 15.3 us -> 8.31 us
    all_to_all x2 -> x4, waiting for transfers between devices: 245 us -> 45 us  [exchange(): return lax.all_to_all(value, axes, split_axis=0, concat_axis=0, tiled=True)]
    reduce_scatter x1 -> x0, waiting for transfers between devices: 125 us -> none  [local(): lax.psum_scatter(partial_out, 'tp', scatter_dimension=1, tiled=True)]
    all_to_all x0 -> x2, blocking collectives: none -> 99 us  [exchange(): return lax.all_to_all(value, axes, split_axis=0, concat_axis=0, tiled=True)]
    all_gather x0 -> x1, blocking collectives: none -> 31.5 us  [local(): table = lax.all_gather(slot_stretch[0], SEQ, axis=0, tiled=True)]
    unnamed x1 -> x0, blocking collectives: 22.1 us -> none
    all_to_all x2 -> x4, starting transfers between devices: 16.2 us -> 34.4 us  [exchange(): return lax.all_to_all(value, axes, split_axis=0, concat_axis=0, tiled=True)]
    pallas_call x0 -> x4, Pallas kernels: none -> 13.6 us  [the longest x1 8.77 us: attend(): pl.pallas_call(attend_kernel, out_shape=jax.ShapeDtypeStruct((G, slots, R...]
    ppermute x2 -> x3, waiting for transfers between devices: 0.01 us -> 13 us  [the longest x1 6.91 us: local(): weight = lax.ppermute(out_weight[0], 'segment', back)]
  transfers between devices with their start and end apart: 6 -> 8, of which waited for: 4 -> 6; matrix products, arithmetic and copies ran while one was open for 3% -> 1% of each run, Pallas kernels for 0% -> 3%
where the time goes in v1:
time: 325 us; the launch traced here: 324 us
  blocking collectives  130 us (40%)
  waiting for transfers between devices  108 us (33%)
  starting transfers between devices  48.7 us (15%)
  between operations  14.1 us (4%)
  Pallas kernels  13.6 us (4%)
  local copies, waits for them, and re-layouts  8.31 us (3%)
    all_to_all x2, blocking collectives, exchange(): return lax.all_to_all(value, axes, split_axis=0, concat_axis=0, tiled=True)  99 us
    all_gather x1, waiting for transfers between devices, local(): weight = lax.all_gather(weight, 'zh', axis=1, tiled=True)  49.8 us
    all_to_all x4, waiting for transfers between devices, exchange(): return lax.all_to_all(value, axes, split_axis=0, concat_axis=0, tiled=True)  45 us
    all_to_all x4, starting transfers between devices, exchange(): return lax.all_to_all(value, axes, split_axis=0, concat_axis=0, tiled=True)  34.4 us
    all_gather x1, blocking collectives, local(): table = lax.all_gather(slot_stretch[0], SEQ, axis=0, tiled=True)  31.5 us
    pallas_call x1, Pallas kernels, attend(): pl.pallas_call(attend_kernel, out_shape=jax.ShapeDtypeStruct((G, slots, R...  8.77 us
    ppermute x1, waiting for transfers between devices, local(): weight = lax.ppermute(out_weight[0], 'segment', back)  6.91 us
    ppermute x1, starting transfers between devices, local(): pieces = lax.ppermute(pieces, 'segment', back)  6.89 us
  transfers between devices with their start and end apart: 8, of which 6 were waited for; matrix products, arithmetic and copies ran while one was open for 1% of the time, Pallas kernels for 3%

profile of v1, /device:TPU:1, one launch (start us, length us, event | category | flops | bytes accessed | tf_op | source)
XLA Modules:
  0.0 323.9 jit_solution(4570513772742633659)
XLA Ops:
  6.5 0.0 copy-start.6
  6.5 1.3 reshape_squeeze.3
  7.8 6.9 %collective-permute-start = (bf16[4,4,3,16,256]{4,1,3,0,2:T(4,128)(2,1)S(1)}, bf16[4,4,3,16,256]{4,1,3,0,2:T(4,128)(2,1)S(1)}, u32[]{:S(2)}, u32[]{:S(2)}) collective-permute-start(bf16[4,4,3,16,256]{4,1,3,0,2:T(4,128)(2,1)S(1)} %bitcast.31), channel_id=1, source_target_pairs={{0,448},{64,0},{128,64},{192,128},{256,192},{320,256},{384,320},{4... | collective-permute-start | bytes 1179656 | tf_op jit(solution)/shard_map/ppermute | solution.py:150
  14.7 1.3 collective-permute-done
  16.1 0.0 copy-start.1
  16.1 0.8 copy.11
  16.9 0.0 copy-start.5
  16.9 0.0 copy-start
  16.9 17.4 %all-to-all-start = ((bf16[16,3,16,256]{3,2,1,0:T(8,128)(2,1)}), bf16[16,3,16,256]{3,2,1,0:T(8,128)(2,1)S(1)}, u32[]{:S(2)}, u32[]{:S(2)}) async-start(bf16[16,3,16,256]{3,2,1,0:T(8,128)(2,1)} %bitcast.28), calls=%async_computation | async-start | bytes 786432 | tf_op jit(solution)/shard_map/all_to_all | solution.py:131
  34.3 1.3 dynamic-slice
  36.3 0.0 copy-done.6
  36.3 0.1 bitcast_dynamic-update-slice_fusion
  36.4 31.5 %all-reduce.order_ref = s32[48]{0:T(128)S(1)} all-reduce(s32[48]{0:T(128)S(1)} %bitcast_dynamic-update-slice_fusion), channel_id=2, replica_groups=mesh['segment'=8,'x'=4,'zh'=4,'tp'=4] {'x','zh'}, use_global_device_ids=true, to_apply=%add | all-reduce | flops 48 | bytes 384 | tf_op jit(solution)/shard_map/all_gather | solution.py:145
  67.9 0.0 all-to-all-done
  67.9 0.6 permute_blocks.1
  68.5 0.0 copy-start.2
  68.5 0.7 copy-done.2
  69.2 6.7 %all-to-all-start.1 = ((bf16[16,3,16,256]{3,2,1,0:T(8,128)(2,1)}), bf16[16,3,16,256]{3,2,1,0:T(8,128)(2,1)S(1)}, u32[]{:S(2)}, u32[]{:S(2)}) async-start(bf16[16,3,16,256]{3,2,1,0:T(8,128)(2,1)} %bitcast.26), calls=%async_computation.1 | async-start | bytes 786432 | tf_op jit(solution)/shard_map/all_to_all | solution.py:131
  75.9 0.0 all-gather.3.cloned.1.call-start
  76.0 4.5 %collective-permute-start.1 = (bf16[1024,256]{1,0:T(8,128)(2,1)}, bf16[1024,256]{1,0:T(8,128)(2,1)}, u32[]{:S(2)}, u32[]{:S(2)}) collective-permute-start(bf16[1024,256]{1,0:T(8,128)(2,1)} %bitcast.33), channel_id=1, source_target_pairs={{0,448},{64,0},{128,64},{192,128},{256,192},{320,256},{384,320},{4... | collective-permute-start | bytes 1572872 | tf_op jit(solution)/shard_map/ppermute | solution.py:142
  80.4 6.9 %collective-permute-done.1 = bf16[1024,256]{1,0:T(8,128)(2,1)} collective-permute-done((bf16[1024,256]{1,0:T(8,128)(2,1)}, bf16[1024,256]{1,0:T(8,128)(2,1)}, u32[]{:S(2)}, u32[]{:S(2)}) %collective-permute-start.1) | collective-permute-done | bytes 524320 | tf_op jit(solution)/shard_map/ppermute | solution.py:142
  87.3 0.0 all-gather.3.cloned.1.call-update
  87.4 0.0 copy-done.5
  87.4 0.1 copy.12.len_ref
  87.5 8.6 %all-to-all-done.1 = bf16[16,3,16,256]{3,2,1,0:T(8,128)(2,1)S(1)} async-done(((bf16[16,3,16,256]{3,2,1,0:T(8,128)(2,1)}), bf16[16,3,16,256]{3,2,1,0:T(8,128)(2,1)S(1)}, u32[]{:S(2)}, u32[]{:S(2)}) %all-to-all-start.1) | async-done | bytes 393248 | tf_op jit(solution)/shard_map/all_to_all | solution.py:131
  96.1 0.0 copy-done.1
  96.1 0.0 copy-done
  96.1 8.8 %attend.1 = bf16[4,3,16,1024]{3,2,1,0:T(8,128)(2,1)S(1)} custom-call(s32[3,2]{1,0:T(4,128)S(1)} %copy.12.len_ref, bf16[4,4,3,16,256]{4,3,2,1,0:T(8,128)(2,1)S(1)} %bitcast.24, bf16[3,256,1024]{2,1,0:T(8,128)(2,1)S(1)} %bitcast.21, bf16[3,256,1024]{2,1,0:T(8,128)(2,1)S(1)} %bitcast.22), custom_call_target="tpu_custom_call" | custom-call | flops 201326592 | bytes 3145728 | tf_op jit(solution)/shard_map/attend/pallas_call | solution.py:68
  104.9 44.9 %all_to_all.30 = bf16[4,3,16,1024]{3,2,1,0:T(8,128)(2,1)S(1)} all-to-all(bf16[4,3,16,1024]{3,2,1,0:T(8,128)(2,1)S(1)} %attend.1), channel_id=1, replica_groups=mesh['segment'=8,'x'=4,'zh'=4,'tp'=4] {'zh'}, dimensions={0} | all-to-all | bytes 786432 | tf_op jit(solution)/shard_map/all_to_all | solution.py:131
  149.8 1.4 broadcast_in_dim.24
  151.1 4.8 %all-to-all-start.3 = ((bf16[4,4,3,16,1024]{4,3,2,1,0:T(8,128)(2,1)}), bf16[4,4,3,16,1024]{4,3,2,1,0:T(8,128)(2,1)S(1)}, u32[]{:S(2)}, u32[]{:S(2)}) async-start(bf16[4,4,3,16,1024]{4,3,2,1,0:T(8,128)(2,1)} %broadcast_in_dim.24), calls=%async_computation.3 | async-start | bytes 3145728 | tf_op jit(solution)/shard_map/all_to_all | solution.py:131
  155.9 49.8 %all-gather.3.cloned.1.call-done.w_ref = bf16[1024,1024]{1,0:T(8,128)(2,1)} async-done(((bf16[1024,256]{1,0:T(8,128)(2,1)}), bf16[1024,1024]{1,0:T(8,128)(2,1)}) %all-gather.3.cloned.1.call-update) | async-done | bytes 2097168 | tf_op jit(solution)/shard_map/all_gather | solution.py:143
  205.7 0.0 all-to-all-done.3
  205.7 0.0 copy-start.3
  205.7 1.6 copy-done.3
  207.3 3.5 %project.1 = bf16[4,768,256]{2,1,0:T(8,128)(2,1)} custom-call(bf16[768,1024]{1,0:T(8,128)(2,1)S(1)} %bitcast.23, bf16[1024,1024]{1,0:T(8,128)(2,1)S(1)} %copy-done.3), custom_call_target="tpu_custom_call" | custom-call | flops 1610612736 | bytes 5242880 | tf_op jit(solution)/shard_map/project/pallas_call | solution.py:94
  210.8 5.6 %all-to-all-start.4 = ((bf16[4,768,256]{2,1,0:T(8,128)(2,1)}), bf16[4,768,256]{2,1,0:T(8,128)(2,1)S(1)}, u32[]{:S(2)}, u32[]{:S(2)}) async-start(bf16[4,768,256]{2,1,0:T(8,128)(2,1)} %project.1), calls=%async_computation.4 | async-start | bytes 3145728 | tf_op jit(solution)/shard_map/all_to_all | solution.py:131
  216.3 0.1 select_reduce_fusion.order_ref
  216.5 36.3 %all-to-all-done.4 = bf16[4,768,256]{2,1,0:T(8,128)(2,1)S(1)} async-done(((bf16[4,768,256]{2,1,0:T(8,128)(2,1)}), bf16[4,768,256]{2,1,0:T(8,128)(2,1)S(1)}, u32[]{:S(2)}, u32[]{:S(2)}) %all-to-all-start.4) | async-done | bytes 1572896 | tf_op jit(solution)/shard_map/all_to_all | solution.py:131
  252.8 0.7 sum_permute.1
  253.5 2.9 collective-permute-start.2
  256.5 4.7 %collective-permute-done.2 = bf16[48,16,256]{2,1,0:T(8,128)(2,1)S(1)} collective-permute-done((bf16[48,16,256]{2,1,0:T(8,128)(2,1)S(1)}, bf16[48,16,256]{2,1,0:T(8,128)(2,1)S(1)}, u32[]{:S(2)}, u32[]{:S(2)}) %collective-permute-start.2) | collective-permute-done | bytes 393248 | tf_op jit(solution)/shard_map/ppermute | solution.py:174
  261.2 54.1 %all_to_all.31 = bf16[16,3,16,256]{3,2,1,0:T(8,128)(2,1)S(1)} all-to-all(bf16[16,3,16,256]{3,2,1,0:T(8,128)(2,1)S(1)} %bitcast.30), channel_id=1, replica_groups=mesh['segment'=8,'x'=4,'zh'=4,'tp'=4] {'x','zh'}, dimensions={0} | all-to-all | bytes 786432 | tf_op jit(solution)/shard_map/all_to_all | solution.py:131
  315.2 0.0 copy-start.4
  315.2 0.3 copy.15
  315.5 0.4 reshape.46
  315.9 0.3 copy-done.4
  316.2 0.8 add_convert_fusion
  (1 shorter events, 0.0 us)
Async XLA Ops:
  6.5 29.8 %copy-start.6 = (s32[1,3]{1,0:T(1,128)S(1)}, s32[1,3]{1,0:T(1,128)}, u32[]{:S(2)}) copy-start(s32[1,3]{1,0:T(1,128)} %param.11) | copy-start | bytes 40
  7.8 8.2 %collective-permute-start = (bf16[4,4,3,16,256]{4,1,3,0,2:T(4,128)(2,1)S(1)}, bf16[4,4,3,16,256]{4,1,3,0,2:T(4,128)(2,1)S(1)}, u32[]{:S(2)}, u32[]{:S(2)}) collective-permute-start(bf16[4,4,3,16,256]{4,1,3,0,2:T(4,128)(2,1)S(1)} %bitcast.31), channel_id=1, source_target_pairs={{0,448},{64,0},{128,64},{192,128},{256,192},{320,256},{384,320},{4... | collective-permute-start | bytes 1179656 | tf_op jit(solution)/shard_map/ppermute | solution.py:150
  16.1 80.0 %copy-start.1 = (bf16[1,3,256,1024]{3,2,1,0:T(8,128)(2,1)S(1)}, bf16[1,3,256,1024]{3,2,1,0:T(8,128)(2,1)}, u32[]{:S(2)}) copy-start(bf16[1,3,256,1024]{3,2,1,0:T(8,128)(2,1)} %param.9) | copy-start | bytes 4718596
  16.9 70.5 %copy-start.5 = (s32[1,3,2]{1,2,0:T(2,128)S(1)}, s32[1,3,2]{1,2,0:T(2,128)}, u32[]{:S(2)}) copy-start(s32[1,3,2]{1,2,0:T(2,128)} %param.10) | copy-start | bytes 76
  16.9 79.2 %copy-start = (bf16[1,3,256,1024]{3,2,1,0:T(8,128)(2,1)S(1)}, bf16[1,3,256,1024]{3,2,1,0:T(8,128)(2,1)}, u32[]{:S(2)}) copy-start(bf16[1,3,256,1024]{3,2,1,0:T(8,128)(2,1)} %param.8) | copy-start | bytes 4718596
  16.9 51.0 %all-to-all-start = ((bf16[16,3,16,256]{3,2,1,0:T(8,128)(2,1)}), bf16[16,3,16,256]{3,2,1,0:T(8,128)(2,1)S(1)}, u32[]{:S(2)}, u32[]{:S(2)}) async-start(bf16[16,3,16,256]{3,2,1,0:T(8,128)(2,1)} %bitcast.28), calls=%async_computation | async-start | bytes 786432 | tf_op jit(solution)/shard_map/all_to_all | solution.py:131
  68.5 0.7 copy-start.2
  69.2 26.9 %all-to-all-start.1 = ((bf16[16,3,16,256]{3,2,1,0:T(8,128)(2,1)}), bf16[16,3,16,256]{3,2,1,0:T(8,128)(2,1)S(1)}, u32[]{:S(2)}, u32[]{:S(2)}) async-start(bf16[16,3,16,256]{3,2,1,0:T(8,128)(2,1)} %bitcast.26), calls=%async_computation.1 | async-start | bytes 786432 | tf_op jit(solution)/shard_map/all_to_all | solution.py:131
  75.9 129.8 %all-gather.3.cloned.1.call-start = ((), (), s32[]{:S(2)}) async-start(), calls=%async_computation.6 | async-start | bytes 2621440 | tf_op jit(solution)/shard_map/all_gather | solution.py:143
  76.0 11.4 %collective-permute-start.1 = (bf16[1024,256]{1,0:T(8,128)(2,1)}, bf16[1024,256]{1,0:T(8,128)(2,1)}, u32[]{:S(2)}, u32[]{:S(2)}) collective-permute-start(bf16[1024,256]{1,0:T(8,128)(2,1)} %bitcast.33), channel_id=1, source_target_pairs={{0,448},{64,0},{128,64},{192,128},{256,192},{320,256},{384,320},{4... | collective-permute-start | bytes 1572872 | tf_op jit(solution)/shard_map/ppermute | solution.py:142
  151.1 54.6 %all-to-all-start.3 = ((bf16[4,4,3,16,1024]{4,3,2,1,0:T(8,128)(2,1)}), bf16[4,4,3,16,1024]{4,3,2,1,0:T(8,128)(2,1)S(1)}, u32[]{:S(2)}, u32[]{:S(2)}) async-start(bf16[4,4,3,16,1024]{4,3,2,1,0:T(8,128)(2,1)} %broadcast_in_dim.24), calls=%async_computation.3 | async-start | bytes 3145728 | tf_op jit(solution)/shard_map/all_to_all | solution.py:131
  205.7 1.6 copy-start.3
  210.8 42.0 %all-to-all-start.4 = ((bf16[4,768,256]{2,1,0:T(8,128)(2,1)}), bf16[4,768,256]{2,1,0:T(8,128)(2,1)S(1)}, u32[]{:S(2)}, u32[]{:S(2)}) async-start(bf16[4,768,256]{2,1,0:T(8,128)(2,1)} %project.1), calls=%async_computation.4 | async-start | bytes 3145728 | tf_op jit(solution)/shard_map/all_to_all | solution.py:131
  253.5 7.6 %collective-permute-start.2 = (bf16[48,16,256]{2,1,0:T(8,128)(2,1)S(1)}, bf16[48,16,256]{2,1,0:T(8,128)(2,1)S(1)}, u32[]{:S(2)}, u32[]{:S(2)}) collective-permute-start(bf16[48,16,256]{2,1,0:T(8,128)(2,1)S(1)} %sum_permute.1), channel_id=1, source_target_pairs={{0,64},{1,80},{2,96},{3,112},{4,68},{5,84},{6,100},{7,116},{8,72},... | collective-permute-start | bytes 1179656 | tf_op jit(solution)/shard_map/ppermute | solution.py:174
  315.2 1.0 copy-start.4
Sparse Core Ops, SparseCore 0:
  87.5 118.2 all-gather.2

commit v2 on v1

--- a/solution.py
+++ b/solution.py
@@ -24,21 +24,24 @@
     return pl.CostEstimate(flops=flops, bytes_accessed=moved, transcendentals=trans)
 
 
-def permute_kernel(order_ref, in_ref, out_ref):
-    for slot in range(in_ref.shape[0]):
-        out_ref[slot] = in_ref[order_ref[slot]]
-
-
-def permute_blocks(blocks, order):
-    return pl.pallas_call(
-        permute_kernel,
-        out_shape=jax.ShapeDtypeStruct(blocks.shape, blocks.dtype),
+def permute_kernel(per_dev, order_ref, in_ref, out_ref):
+    for slot in range(out_ref.shape[0]):
+        taken = order_ref[slot]
+        start = pl.multiple_of(lax.rem(taken, per_dev) * ROWS, ROWS)
+        out_ref[slot] = in_ref[lax.div(taken, per_dev), pl.ds(start, ROWS), :]
+
+
+def permute_blocks(spread, order, per_dev):
+    sources, _, part = spread.shape
+    return pl.pallas_call(
+        functools.partial(permute_kernel, per_dev),
+        out_shape=jax.ShapeDtypeStruct((sources * per_dev, ROWS, part), spread.dtype),
         in_specs=[SMEM, VMEM],
         out_specs=VMEM,
         compiler_params=PARAMS,
-        cost_estimate=cost(0, 4 * blocks.size),
+        cost_estimate=cost(0, 4 * spread.size),
         name="permute_blocks",
-    )(order, blocks)
+    )(order, spread)
 
 
 def attend_kernel(len_ref, q_ref, k_ref, v_ref, out_ref):
@@ -140,16 +143,25 @@
     back = [(i, (i - 1) % sections) for i in range(sections)]
 
     weight = lax.ppermute(out_weight[0], "segment", back)
+    weight, first = lax.optimization_barrier((weight, queries[0]))
     weight = lax.all_gather(weight, "zh", axis=1, tiled=True)
 
-    table = lax.all_gather(slot_stretch[0], SEQ, axis=0, tiled=True)
+    moved = lax.ppermute(first, "segment", back)
+    pieces = moved.reshape(per_dev, G, ROWS, G, part).transpose(1, 3, 0, 2, 4)
+    note = jnp.pad(slot_stretch.astype(jnp.bfloat16), ((0, 7), (0, part - per_dev)))
+    pieces = jnp.concatenate(
+        [
+            pieces.reshape(G * G, per_dev * ROWS, part),
+            jnp.broadcast_to(note[None], (G * G,) + note.shape),
+        ],
+        axis=1,
+    )
+    spread = exchange(pieces, SEQ)
+
+    table = spread[:, per_dev * ROWS, :per_dev].astype(jnp.int32).reshape(count)
     ids = jnp.arange(count, dtype=jnp.int32)
     inverse = jnp.sum(jnp.where(table[None, :] == ids[:, None], ids[None, :], 0), axis=1)
-
-    pieces = queries[0].reshape(per_dev, G, ROWS, G, part).transpose(1, 3, 0, 2, 4)
-    pieces = lax.ppermute(pieces, "segment", back)
-    spread = exchange(pieces.reshape(G * G, per_dev, ROWS, part), SEQ)
-    ordered = permute_blocks(spread.reshape(count, ROWS, part), table)
+    ordered = permute_blocks(spread, table, per_dev)
     picked = exchange(ordered.reshape(G * G, per_dev, ROWS, part), SEQ)
 
     answer = attend(

time: 325 us -> 317 us (0.975)
  blocking collectives: 130 us -> 141 us
  starting transfers between devices: 48.7 us -> 37.8 us
  waiting for transfers between devices: 108 us -> 102 us
    all_to_all x2 -> x3, blocking collectives: 99 us -> 141 us  [exchange(): return lax.all_to_all(value, axes, split_axis=0, concat_axis=0, tiled=True)]
    all_gather x1 -> x0, blocking collectives: 31.5 us -> none  [local(): table = lax.all_gather(slot_stretch[0], SEQ, axis=0, tiled=True)]
    all_gather x1, waiting for transfers between devices: 49.8 us -> 35.2 us  [local(): weight = lax.all_gather(weight, 'zh', axis=1, tiled=True)]
    all_to_all x4 -> x3, starting transfers between devices: 34.4 us -> 23 us  [exchange(): return lax.all_to_all(value, axes, split_axis=0, concat_axis=0, tiled=True)]
    all_to_all x4 -> x3, waiting for transfers between devices: 45 us -> 55.5 us  [exchange(): return lax.all_to_all(value, axes, split_axis=0, concat_axis=0, tiled=True)]
    ppermute x1, waiting for transfers between devices: 6.91 us -> 2.88 us  [local(): weight = lax.ppermute(out_weight[0], 'segment', back)]
  transfers between devices with their start and end apart: 8 -> 7, of which waited for: 6 -> 6; matrix products, arithmetic and copies ran while one was open for 1% -> 1% of each run, Pallas kernels for 3% -> 3%
where the time goes in v2:
time: 317 us; the launch traced here: 316 us
  blocking collectives  141 us (44%)
  waiting for transfers between devices  102 us (32%)
  starting transfers between devices  37.8 us (12%)
  Pallas kernels  14.5 us (5%)
  between operations  13.5 us (4%)
  local copies, waits for them, and re-layouts  5.87 us (2%)
    all_to_all x3, blocking collectives, exchange(): return lax.all_to_all(value, axes, split_axis=0, concat_axis=0, tiled=True)  141 us
    all_to_all x3, waiting for transfers between devices, exchange(): return lax.all_to_all(value, axes, split_axis=0, concat_axis=0, tiled=True)  55.5 us
    all_gather x1, waiting for transfers between devices, local(): weight = lax.all_gather(weight, 'zh', axis=1, tiled=True)  35.2 us
    all_to_all x3, starting transfers between devices, exchange(): return lax.all_to_all(value, axes, split_axis=0, concat_axis=0, tiled=True)  23 us
    pallas_call x1, Pallas kernels, attend(): pl.pallas_call(attend_kernel, out_shape=jax.ShapeDtypeStruct((G, slots, R...  8.77 us
    ppermute x1, starting transfers between devices, local(): weight = lax.ppermute(out_weight[0], 'segment', back)  6.88 us
  transfers between devices with their start and end apart: 7, of which 6 were waited for; matrix products, arithmetic and copies ran while one was open for 1% of the time, Pallas kernels for 3%

profile of v2, /device:TPU:1, one launch (start us, length us, event | category | flops | bytes accessed | tf_op | source)
XLA Modules:
  0.0 316.1 jit_solution(16708623489685244938)
XLA Ops:
  6.5 6.9 %collective-permute-start = (bf16[1024,256]{1,0:T(8,128)(2,1)}, bf16[1024,256]{1,0:T(8,128)(2,1)S(1)}, u32[]{:S(2)}, u32[]{:S(2)}) collective-permute-start(bf16[1024,256]{1,0:T(8,128)(2,1)} %bitcast.28), channel_id=1, source_target_pairs={{0,448},{64,0},{128,64},{192,128},{256,192},{320,256},{384,320},{4... | collective-permute-start | bytes 1572872 | tf_op jit(solution)/shard_map/ppermute | solution.py:145
  13.4 2.9 collective-permute-done
  16.3 0.0 copy-start.3
  16.3 4.1 %collective-permute-start.1 = (bf16[192,1024]{1,0:T(8,128)(2,1)}, bf16[192,1024]{1,0:T(8,128)(2,1)S(1)}, u32[]{:S(2)}, u32[]{:S(2)}) collective-permute-start(bf16[192,1024]{1,0:T(8,128)(2,1)} %bitcast.29), channel_id=1, source_target_pairs={{0,448},{64,0},{128,64},{192,128},{256,192},{320,256},{384,320},{4... | collective-permute-start | bytes 1179656 | tf_op jit(solution)/shard_map/ppermute | solution.py:149
  20.4 0.7 convert_element_type.44
  21.1 2.6 collective-permute-done.1
  23.7 0.3 reshape.48
  24.1 0.0 copy-start.5
  24.1 0.0 copy-start
  24.1 39.5 %all_to_all.30.in_ref = bf16[16,56,256]{2,1,0:T(8,128)(2,1)S(1)} all-to-all(bf16[16,56,256]{2,1,0:T(8,128)(2,1)S(1)} %pad_maximum_fusion), channel_id=1, replica_groups=mesh['segment'=8,'x'=4,'zh'=4,'tp'=4] {'x','zh'}, dimensions={0} | all-to-all | bytes 917504 | tf_op jit(solution)/shard_map/all_to_all | solution.py:134
  63.6 0.0 copy-done.3
  63.7 0.1 reshape.55.order_ref
  63.8 1.5 permute_blocks.1
  65.3 9.6 %all-to-all-start.1 = ((bf16[16,3,16,256]{3,2,1,0:T(8,128)(2,1)}), bf16[16,3,16,256]{3,2,1,0:T(8,128)(2,1)S(1)}, u32[]{:S(2)}, u32[]{:S(2)}) async-start(bf16[16,3,16,256]{3,2,1,0:T(8,128)(2,1)} %bitcast.5), calls=%async_computation.1 | async-start | bytes 786432 | tf_op jit(solution)/shard_map/all_to_all | solution.py:134
  74.9 0.0 all-gather.2.cloned.1.call-start
  75.0 0.7 all-gather.2.cloned.1.call-update
  75.6 0.0 copy-done.5
  75.7 0.1 copy.15.len_ref
  75.7 19.2 %all-to-all-done.1 = bf16[16,3,16,256]{3,2,1,0:T(8,128)(2,1)S(1)} async-done(((bf16[16,3,16,256]{3,2,1,0:T(8,128)(2,1)}), bf16[16,3,16,256]{3,2,1,0:T(8,128)(2,1)S(1)}, u32[]{:S(2)}, u32[]{:S(2)}) %all-to-all-start.1) | async-done | bytes 393248 | tf_op jit(solution)/shard_map/all_to_all | solution.py:134
  94.9 0.0 copy-done
  94.9 0.0 copy-start.1
  95.0 1.4 copy-done.1
  96.4 8.8 %attend.1 = bf16[4,3,16,1024]{3,2,1,0:T(8,128)(2,1)S(1)} custom-call(s32[3,2]{1,0:T(4,128)S(1)} %copy.15.len_ref, bf16[4,4,3,16,256]{4,3,2,1,0:T(8,128)(2,1)S(1)} %bitcast.22, bf16[3,256,1024]{2,1,0:T(8,128)(2,1)S(1)} %bitcast.19, bf16[3,256,1024]{2,1,0:T(8,128)(2,1)S(1)} %bitcast.20), custom_call_target="tpu_custom_call" | custom-call | flops 201326592 | bytes 3145728 | tf_op jit(solution)/shard_map/attend/pallas_call | solution.py:71
  105.1 46.9 %all_to_all.31 = bf16[4,3,16,1024]{3,2,1,0:T(8,128)(2,1)S(1)} all-to-all(bf16[4,3,16,1024]{3,2,1,0:T(8,128)(2,1)S(1)} %attend.1), channel_id=1, replica_groups=mesh['segment'=8,'x'=4,'zh'=4,'tp'=4] {'zh'}, dimensions={0} | all-to-all | bytes 786432 | tf_op jit(solution)/shard_map/all_to_all | solution.py:134
  152.0 1.4 broadcast_in_dim.30
  153.4 3.6 %all-to-all-start.3 = ((bf16[4,4,3,16,1024]{4,3,2,1,0:T(8,128)(2,1)}), bf16[4,4,3,16,1024]{4,3,2,1,0:T(8,128)(2,1)S(1)}, u32[]{:S(2)}, u32[]{:S(2)}) async-start(bf16[4,4,3,16,1024]{4,3,2,1,0:T(8,128)(2,1)} %broadcast_in_dim.30), calls=%async_computation.3 | async-start | bytes 3145728 | tf_op jit(solution)/shard_map/all_to_all | solution.py:134
  156.9 35.2 %all-gather.2.cloned.1.call-done.w_ref = bf16[1024,1024]{1,0:T(8,128)(2,1)} async-done(((bf16[1024,256]{1,0:T(8,128)(2,1)}), bf16[1024,1024]{1,0:T(8,128)(2,1)}) %all-gather.2.cloned.1.call-update) | async-done | bytes 2097168 | tf_op jit(solution)/shard_map/all_gather | solution.py:147
  192.1 0.0 all-to-all-done.3
  192.1 0.0 copy-start.2
  192.1 1.6 copy-done.2
  193.7 3.5 %project.1 = bf16[4,768,256]{2,1,0:T(8,128)(2,1)} custom-call(bf16[768,1024]{1,0:T(8,128)(2,1)S(1)} %bitcast.21, bf16[1024,1024]{1,0:T(8,128)(2,1)S(1)} %copy-done.2), custom_call_target="tpu_custom_call" | custom-call | flops 1610612736 | bytes 5242880 | tf_op jit(solution)/shard_map/project/pallas_call | solution.py:97
  197.2 9.8 %all-to-all-start.4 = ((bf16[4,768,256]{2,1,0:T(8,128)(2,1)}), bf16[4,768,256]{2,1,0:T(8,128)(2,1)S(1)}, u32[]{:S(2)}, u32[]{:S(2)}) async-start(bf16[4,768,256]{2,1,0:T(8,128)(2,1)} %project.1), calls=%async_computation.4 | async-start | bytes 3145728 | tf_op jit(solution)/shard_map/all_to_all | solution.py:134
  207.0 0.1 select_reduce_fusion.order_ref
  207.1 36.3 %all-to-all-done.4 = bf16[4,768,256]{2,1,0:T(8,128)(2,1)S(1)} async-done(((bf16[4,768,256]{2,1,0:T(8,128)(2,1)}), bf16[4,768,256]{2,1,0:T(8,128)(2,1)S(1)}, u32[]{:S(2)}, u32[]{:S(2)}) %all-to-all-start.4) | async-done | bytes 1572896 | tf_op jit(solution)/shard_map/all_to_all | solution.py:134
  243.5 0.7 sum_permute.1
  244.2 3.8 %collective-permute-start.2 = (bf16[48,16,256]{2,1,0:T(8,128)(2,1)S(1)}, bf16[48,16,256]{2,1,0:T(8,128)(2,1)S(1)}, u32[]{:S(2)}, u32[]{:S(2)}) collective-permute-start(bf16[48,16,256]{2,1,0:T(8,128)(2,1)S(1)} %sum_permute.1), channel_id=1, source_target_pairs={{0,64},{1,80},{2,96},{3,112},{4,68},{5,84},{6,100},{7,116},{8,72},... | collective-permute-start | bytes 1179656 | tf_op jit(solution)/shard_map/ppermute | solution.py:186
  248.0 4.7 %collective-permute-done.2 = bf16[48,16,256]{2,1,0:T(8,128)(2,1)S(1)} collective-permute-done((bf16[48,16,256]{2,1,0:T(8,128)(2,1)S(1)}, bf16[48,16,256]{2,1,0:T(8,128)(2,1)S(1)}, u32[]{:S(2)}, u32[]{:S(2)}) %collective-permute-start.2) | collective-permute-done | bytes 393248 | tf_op jit(solution)/shard_map/ppermute | solution.py:186
  252.7 54.7 %all_to_all.32 = bf16[16,3,16,256]{3,2,1,0:T(8,128)(2,1)S(1)} all-to-all(bf16[16,3,16,256]{3,2,1,0:T(8,128)(2,1)S(1)} %bitcast.26), channel_id=1, replica_groups=mesh['segment'=8,'x'=4,'zh'=4,'tp'=4] {'x','zh'}, dimensions={0} | all-to-all | bytes 786432 | tf_op jit(solution)/shard_map/all_to_all | solution.py:134
  307.4 0.0 copy-start.4
  307.4 0.3 copy.18
  307.7 0.4 reshape.56
  308.1 0.3 copy-done.4
  308.4 0.8 add_convert_fusion
  (5 shorter events, 0.1 us)
Async XLA Ops:
  6.5 9.8 %collective-permute-start = (bf16[1024,256]{1,0:T(8,128)(2,1)}, bf16[1024,256]{1,0:T(8,128)(2,1)S(1)}, u32[]{:S(2)}, u32[]{:S(2)}) collective-permute-start(bf16[1024,256]{1,0:T(8,128)(2,1)} %bitcast.28), channel_id=1, source_target_pairs={{0,448},{64,0},{128,64},{192,128},{256,192},{320,256},{384,320},{4... | collective-permute-start | bytes 1572872 | tf_op jit(solution)/shard_map/ppermute | solution.py:145
  16.3 47.3 %copy-start.3 = (bf16[1024,256]{1,0:T(8,128)(2,1)}, bf16[1024,256]{1,0:T(8,128)(2,1)S(1)}, u32[]{:S(2)}) copy-start(bf16[1024,256]{1,0:T(8,128)(2,1)S(1)} %collective-permute-done) | copy-start | bytes 1572868
  16.3 7.4 %collective-permute-start.1 = (bf16[192,1024]{1,0:T(8,128)(2,1)}, bf16[192,1024]{1,0:T(8,128)(2,1)S(1)}, u32[]{:S(2)}, u32[]{:S(2)}) collective-permute-start(bf16[192,1024]{1,0:T(8,128)(2,1)} %bitcast.29), channel_id=1, source_target_pairs={{0,448},{64,0},{128,64},{192,128},{256,192},{320,256},{384,320},{4... | collective-permute-start | bytes 1179656 | tf_op jit(solution)/shard_map/ppermute | solution.py:149
  24.1 51.5 %copy-start.5 = (s32[1,3,2]{1,2,0:T(2,128)S(1)}, s32[1,3,2]{1,2,0:T(2,128)}, u32[]{:S(2)}) copy-start(s32[1,3,2]{1,2,0:T(2,128)} %param.10) | copy-start | bytes 76
  24.1 70.8 %copy-start = (bf16[1,3,256,1024]{3,2,1,0:T(8,128)(2,1)S(1)}, bf16[1,3,256,1024]{3,2,1,0:T(8,128)(2,1)}, u32[]{:S(2)}) copy-start(bf16[1,3,256,1024]{3,2,1,0:T(8,128)(2,1)} %param.8) | copy-start | bytes 4718596
  65.3 29.7 %all-to-all-start.1 = ((bf16[16,3,16,256]{3,2,1,0:T(8,128)(2,1)}), bf16[16,3,16,256]{3,2,1,0:T(8,128)(2,1)S(1)}, u32[]{:S(2)}, u32[]{:S(2)}) async-start(bf16[16,3,16,256]{3,2,1,0:T(8,128)(2,1)} %bitcast.5), calls=%async_computation.1 | async-start | bytes 786432 | tf_op jit(solution)/shard_map/all_to_all | solution.py:134
  74.9 117.2 %all-gather.2.cloned.1.call-start = ((), (), s32[]{:S(2)}) async-start(), calls=%async_computation.6 | async-start | bytes 2621440 | tf_op jit(solution)/shard_map/all_gather | solution.py:147
  94.9 1.4 copy-start.1
  153.4 38.8 %all-to-all-start.3 = ((bf16[4,4,3,16,1024]{4,3,2,1,0:T(8,128)(2,1)}), bf16[4,4,3,16,1024]{4,3,2,1,0:T(8,128)(2,1)S(1)}, u32[]{:S(2)}, u32[]{:S(2)}) async-start(bf16[4,4,3,16,1024]{4,3,2,1,0:T(8,128)(2,1)} %broadcast_in_dim.30), calls=%async_computation.3 | async-start | bytes 3145728 | tf_op jit(solution)/shard_map/all_to_all | solution.py:134
  192.1 1.6 copy-start.2
  197.2 46.3 %all-to-all-start.4 = ((bf16[4,768,256]{2,1,0:T(8,128)(2,1)}), bf16[4,768,256]{2,1,0:T(8,128)(2,1)S(1)}, u32[]{:S(2)}, u32[]{:S(2)}) async-start(bf16[4,768,256]{2,1,0:T(8,128)(2,1)} %project.1), calls=%async_computation.4 | async-start | bytes 3145728 | tf_op jit(solution)/shard_map/all_to_all | solution.py:134
  244.2 8.5 %collective-permute-start.2 = (bf16[48,16,256]{2,1,0:T(8,128)(2,1)S(1)}, bf16[48,16,256]{2,1,0:T(8,128)(2,1)S(1)}, u32[]{:S(2)}, u32[]{:S(2)}) collective-permute-start(bf16[48,16,256]{2,1,0:T(8,128)(2,1)S(1)} %sum_permute.1), channel_id=1, source_target_pairs={{0,64},{1,80},{2,96},{3,112},{4,68},{5,84},{6,100},{7,116},{8,72},... | collective-permute-start | bytes 1179656 | tf_op jit(solution)/shard_map/ppermute | solution.py:186
  307.4 1.0 copy-start.4
Sparse Core Ops, SparseCore 0:
  77.8 114.2 all-gather.1

commit v3 on v2

v3 whole, which is shorter than its diff:
```python
import functools
import math

import jax
import jax.numpy as jnp
from jax import lax
from jax.experimental import pallas as pl
from jax.experimental.pallas import tpu as pltpu
from jax.sharding import Mesh
from jax.sharding import PartitionSpec as P

HD = 128
STRETCH = 64
NR = 128
G = 4
ROWS = STRETCH // G
VMEM = pl.BlockSpec(memory_space=pltpu.VMEM)
SMEM = pl.BlockSpec(memory_space=pltpu.SMEM)
PARAMS = pltpu.CompilerParams(vmem_limit_bytes=40 * 1024 * 1024)
SEQ = ("x", "zh")
CHUNKS = 2


def cost(flops, moved, trans=0):
    return pl.CostEstimate(flops=flops, bytes_accessed=moved, transcendentals=trans)


def permute_kernel(per_dev, order_ref, in_ref, out_ref):
    for slot in range(out_ref.shape[0]):
        taken = order_ref[slot]
        start = pl.multiple_of(lax.rem(taken, per_dev) * ROWS, ROWS)
        out_ref[slot] = in_ref[lax.div(taken, per_dev), pl.ds(start, ROWS), :]


def permute_blocks(spread, order, per_dev):
    sources, _, part = spread.shape
    return pl.pallas_call(
        functools.partial(permute_kernel, per_dev),
        out_shape=jax.ShapeDtypeStruct((sources * per_dev, ROWS, part), spread.dtype),
        in_specs=[SMEM, VMEM],
        out_specs=VMEM,
        compiler_params=PARAMS,
        cost_estimate=cost(0, 4 * spread.size),
        name="permute_blocks",
    )(order, spread)


def attend_kernel(len_ref, q_ref, k_ref, v_ref, out_ref):
    slot = pl.program_id(0)
    span = k_ref.shape[1]
    heads = k_ref.shape[2] // HD
    groups = q_ref.shape[1]
    per_group = heads // groups
    position = lax.broadcasted_iota(jnp.int32, (1, span), 1)
    limit = jnp.where(position < NR, len_ref[slot, 0], len_ref[slot, 1] + NR)
    valid = position < limit
    lanes = [slice(head * HD, (head + 1) * HD) for head in range(heads)]
    scores = []
    for head in range(heads):
        part = slice((head % per_group) * HD, (head % per_group + 1) * HD)
        q = q_ref[:, head // per_group, 0, :, part].reshape(STRETCH, HD)
        scores.append(
            lax.dot_general(
                q,
                k_ref[0, :, lanes[head]],
                (((1,), (1,)), ((), ())),
                preferred_element_type=jnp.float32,
            )
        )
    weights = []
    for head in range(heads):
        masked = jnp.where(valid, scores[head] * (1.0 / math.sqrt(HD)), -1e30)
        expo = jnp.exp(masked - jnp.max(masked, axis=-1, keepdims=True))
        weights.append((expo / jnp.sum(expo, axis=-1, keepdims=True)).astype(jnp.bfloat16))
    for head in range(heads):
        mixed = jnp.dot(
            weights[head], v_ref[0, :, lanes[head]], preferred_element_type=jnp.float32
        )
        out_ref[:, 0, :, lanes[head]] = mixed.astype(jnp.bfloat16).reshape(G, ROWS, HD)


def attend(picked, keys, values, lengths, chunk, chunks):
    slots, span, feats = keys.shape
    wide = feats // chunks
    groups = G // chunks
    return pl.pallas_call(
        attend_kernel,
        out_shape=jax.ShapeDtypeStruct((G, slots, ROWS, wide), jnp.bfloat16),
        grid=(slots,),
        in_specs=[
            SMEM,
            pl.BlockSpec((G, groups, 1, ROWS, feats // G), lambda s: (0, chunk, s, 0, 0)),
            pl.BlockSpec((1, span, wide), lambda s: (s, 0, chunk)),
            pl.BlockSpec((1, span, wide), lambda s: (s, 0, chunk)),
        ],
        out_specs=pl.BlockSpec((G, 1, ROWS, wide), lambda s: (0, s, 0, 0)),
        compiler_params=PARAMS,
        cost_estimate=cost(4 * slots * STRETCH * span * wide, 4 * slots * span * wide),
        name="attend",
    )(lengths, picked, keys, values)


def project_kernel(chunks, order_ref, *refs):
    parts = len(refs[:-G - 1]) // chunks
    w_ref, outs = refs[-G - 1], refs[-G:]
    wide = refs[0].shape[1]
    for out, group in zip(outs, range(G)):
        taken = order_ref[group]
        start = 0
        for part in range(parts):
            rows = refs[part].shape[0]
            total = None
            for chunk in range(chunks):
                product = jnp.dot(
                    refs[chunk * parts + part][...],
                    w_ref[taken, chunk * wide : (chunk + 1) * wide, :],
                    preferred_element_type=jnp.float32,
                )
                total = product if total is None else total + product
            out[start : start + rows, :] = total.astype(jnp.bfloat16)
            start += rows


def project(parts, weight, order):
    chunks = len(parts)
    m = sum(p.shape[0] for p in parts[0])
    _, k, n = weight.shape
    flat = [p for chunk in parts for p in chunk]
    return pl.pallas_call(
        functools.partial(project_kernel, chunks),
        out_shape=[jax.ShapeDtypeStruct((m, n), jnp.bfloat16)] * G,
        in_specs=[SMEM] + [VMEM] * (len(flat) + 1),
        out_specs=[VMEM] * G,
        compiler_params=PARAMS,
        cost_estimate=cost(2 * m * n * k * G, 2 * (m * k + G * n * k + G * m * n)),
        name="project",
    )(order, *flat, weight)


def sum_permute_kernel(order_ref, *refs):
    out_ref = refs[-1]
    for place in range(out_ref.shape[0]):
        start = pl.multiple_of(order_ref[place] * ROWS, ROWS)
        total = None
        for ref in refs[:-1]:
            term = ref[pl.ds(start, ROWS), :].astype(jnp.float32)
            total = term if total is None else total + term
        out_ref[place] = total.astype(out_ref.dtype)


def sum_permute(parts, order):
    m, n = parts[0].shape
    return pl.pallas_call(
        sum_permute_kernel,
        out_shape=jax.ShapeDtypeStruct((m // ROWS, ROWS, n), parts[0].dtype),
        in_specs=[SMEM] + [VMEM] * len(parts),
        out_specs=VMEM,
        compiler_params=PARAMS,
        cost_estimate=cost(4 * m * n, 10 * m * n),
        name="sum_permute",
    )(order, *parts)


def exchange(value, axes):
    return lax.all_to_all(value, axes, split_axis=0, concat_axis=0, tiled=True)


def turn(value, axis, by):
    return lax.ppermute(value, axis, [(i, (i + by) % G) for i in range(G)])


def gather_ring(value):
    half = value.shape[0] // 2
    below = turn(value, "zh", 1)
    above = turn(value, "zh", -1)
    return [value, below, above, turn(below[:half], "zh", 1), turn(above[half:], "zh", -1)]


def local(queries, nb_keys, nb_values, nb_lengths, slot_stretch, out_weight, residual):
    per_dev = slot_stretch.shape[1]
    feats = queries.shape[2]
    part = feats // G
    sections = lax.axis_size("segment")
    count = per_dev * G * G
    back = [(i, (i - 1) % sections) for i in range(sections)]
    onward = [(i, (i + 1) % sections) for i in range(sections)]
    x, zh, t = lax.axis_index("x"), lax.axis_index("zh"), lax.axis_index("tp")

    moved = lax.ppermute(queries[0], "segment", back)
    pieces = moved.reshape(per_dev, G, ROWS, G, part).transpose(1, 3, 0, 2, 4)
    note = jnp.pad(slot_stretch.astype(jnp.bfloat16), ((0, 7), (0, part - per_dev)))
    pieces = jnp.concatenate(
        [
            pieces.reshape(G * G, per_dev * ROWS, part),
            jnp.broadcast_to(note[None], (G * G,) + note.shape),
        ],
        axis=1,
    )
    spread = exchange(pieces, SEQ)

    own = lax.ppermute(out_weight[0], "segment", back)
    weight = jnp.stack([own, turn(own, "x", -1), turn(own, "x", 2), turn(own, "x", 1)])

    table = spread[:, per_dev * ROWS, :per_dev].astype(jnp.int32).reshape(count)
    ids = jnp.arange(count, dtype=jnp.int32)
    holder, within = ids // per_dev, ids % per_dev
    apart = (holder % G - zh) % G
    rank = jnp.where(apart == 3, 1, jnp.where(apart == 1, 2, jnp.where(apart == 2, 3, 0)))
    place = (rank * G + holder // G) * per_dev + within
    places = jnp.sum(jnp.where(table[None, :] == ids[:, None], place[None, :], 0), axis=1)
    places = lax.ppermute(places, "segment", onward)

    ordered = permute_blocks(spread, table, per_dev)
    picked = exchange(ordered.reshape(G * G, per_dev, ROWS, part), SEQ)
    picked = picked.reshape(G, G, per_dev, ROWS, part)

    parts = []
    for chunk in range(CHUNKS):
        answer = attend(picked, nb_keys[0], nb_values[0], nb_lengths[0], chunk, CHUNKS)
        banded = exchange(answer, "x")
        parts.append(gather_ring(banded.reshape(-1, feats // CHUNKS)))

    order = (t + jnp.arange(G, dtype=jnp.int32) - x) % G
    partial = project(parts, weight, order)
    arrived = []
    for ahead, block in enumerate(partial):
        moves = []
        for s in range(sections):
            for i in range(G):
                moves.append((s * G + i, (s + 1) % sections * G + (i + ahead) % G))
        arrived.append(lax.ppermute(block, ("segment", "tp"), moves))
    summed = sum_permute(arrived, places)
    owned = exchange(summed.reshape(G * G, per_dev, ROWS, part), SEQ)
    owned = owned.reshape(G, G, per_dev, ROWS, part).transpose(2, 0, 3, 1, 4)
    projected = owned.reshape(per_dev * STRETCH, feats).astype(jnp.float32)
    return (residual[0].astype(jnp.float32) + projected).astype(jnp.bfloat16)[None]


def solution(mesh):
    sections, _, tp = mesh.devices.shape
    inner = Mesh(mesh.devices.reshape(sections, G, G, tp), ("segment", "x", "zh", "tp"))
    in_specs = (
        P("segment", SEQ, "tp"),
        P("segment", SEQ, None, "tp"),
        P("segment", SEQ, None, "tp"),
        P("segment", SEQ, None),
        P("segment", SEQ),
        P("segment", "tp", SEQ),
        P("segment", SEQ, "tp"),
    )
    out_specs = P("segment", SEQ, "tp")
    return jax.shard_map(local, mesh=inner, in_specs=in_specs, out_specs=out_specs, check_vma=False)
```

time: 317 us -> 263 us (0.83)
  the two profiles are of different devices: /device:TPU:1 before, /device:TPU:49 now
where the time goes in v3:
time: 263 us; the launch traced here: 262 us
  blocking collectives  100 us (38%)
  waiting for transfers between devices  71.7 us (27%)
  starting transfers between devices  70.1 us (27%)
  Pallas kernels  8.95 us (3%)
  local copies, waits for them, and re-layouts  6.84 us (3%)
  other arithmetic  3.54 us (1%)
    all_to_all x3, blocking collectives, exchange(): return lax.all_to_all(value, axes, split_axis=0, concat_axis=0, tiled=True)  100 us
    ppermute x11, starting transfers between devices, turn(): return lax.ppermute(value, axis, [(i, (i + by) % G) for i in range(G)])  46.2 us
    all_to_all x2, waiting for transfers between devices, exchange(): return lax.all_to_all(value, axes, split_axis=0, concat_axis=0, tiled=True)  28.5 us
    ppermute x4, waiting for transfers between devices, local(): arrived.append(lax.ppermute(block, ('segment', 'tp'), moves))  22.8 us
    ppermute x4, starting transfers between devices, local(): arrived.append(lax.ppermute(block, ('segment', 'tp'), moves))  15.2 us
    ppermute x11, waiting for transfers between devices, turn(): return lax.ppermute(value, axis, [(i, (i + by) % G) for i in range(G)])  8.96 us
    all_to_all x2, starting transfers between devices, exchange(): return lax.all_to_all(value, axes, split_axis=0, concat_axis=0, tiled=True)  7.55 us
    ppermute x1, waiting for transfers between devices, local(): moved = lax.ppermute(queries[0], 'segment', back)  6.07 us
  transfers between devices with their start and end apart: 20, of which 7 were waited for; matrix products, arithmetic and copies ran while one was open for 2% of the time, Pallas kernels for 2%

profile of v3, /device:TPU:49, one launch (start us, length us, event | category | flops | bytes accessed | tf_op | source)
XLA Modules:
  0.0 261.8 jit_solution(14490784481418162764)
XLA Ops:
  0.0 0.7 collective-permute-start
  0.7 0.7 convert_element_type.44
  1.3 6.1 %collective-permute-done = bf16[192,1024]{1,0:T(8,128)(2,1)S(1)} collective-permute-done((bf16[192,1024]{1,0:T(8,128)(2,1)}, bf16[192,1024]{1,0:T(8,128)(2,1)S(1)}, u32[]{:S(2)}, u32[]{:S(2)}) %collective-permute-start) | collective-permute-done | bytes 393248 | tf_op jit(solution)/shard_map/ppermute | solution.py:189
  7.4 0.3 reshape.112
  7.7 0.0 copy-start
  7.7 0.0 copy-start.1
  7.8 48.3 %all_to_all.25.in_ref = bf16[16,56,256]{2,1,0:T(8,128)(2,1)S(1)} all-to-all(bf16[16,56,256]{2,1,0:T(8,128)(2,1)S(1)} %pad_maximum_fusion.1), channel_id=1, replica_groups=mesh['segment'=8,'x'=4,'zh'=4,'tp'=4] {'x','zh'}, dimensions={0} | all-to-all | bytes 917504 | tf_op jit(solution)/shard_map/all_to_all | solution.py:165
  56.2 0.8 copy-done.2
  57.0 0.1 reshape.119.order_ref
  57.1 1.0 copy-done.3
  58.1 0.8 permute_blocks.1
  58.9 0.0 copy-start.4
  58.9 0.7 copy-done.4
  59.6 3.6 %all-to-all-start.1 = ((bf16[16,3,16,256]{3,2,1,0:T(8,128)(2,1)}), bf16[16,3,16,256]{3,2,1,0:T(8,128)(2,1)S(1)}, u32[]{:S(2)}, u32[]{:S(2)}) async-start(bf16[16,3,16,256]{3,2,1,0:T(8,128)(2,1)} %bitcast.28), calls=%async_computation.1 | async-start | bytes 786432 | tf_op jit(solution)/shard_map/all_to_all | solution.py:165
  63.2 0.4 collective-permute-start.10
  63.6 0.1 copy.17.len_ref
  63.7 28.5 %all-to-all-done.1 = bf16[16,3,16,256]{3,2,1,0:T(8,128)(2,1)S(1)} async-done(((bf16[16,3,16,256]{3,2,1,0:T(8,128)(2,1)}), bf16[16,3,16,256]{3,2,1,0:T(8,128)(2,1)S(1)}, u32[]{:S(2)}, u32[]{:S(2)}) %all-to-all-start.1) | async-done | bytes 393248 | tf_op jit(solution)/shard_map/all_to_all | solution.py:165
  92.2 2.2 attend.3
  94.4 0.0 copy-start.5
  94.4 0.7 copy-done.5
  95.1 4.0 %all-to-all-start.3 = ((bf16[4,3,16,512]{3,2,1,0:T(8,128)(2,1)}), bf16[4,3,16,512]{3,2,1,0:T(8,128)(2,1)}, u32[]{:S(2)}, u32[]{:S(2)}) async-start(bf16[4,3,16,512]{3,2,1,0:T(8,128)(2,1)} %copy-done.5), calls=%async_computation.3 | async-start | bytes 393216 | tf_op jit(solution)/shard_map/all_to_all | solution.py:165
  99.1 4.5 %collective-permute-start.11 = (bf16[1024,256]{1,0:T(8,128)(2,1)}, bf16[1024,256]{1,0:T(8,128)(2,1)}, u32[]{:S(2)}, u32[]{:S(2)}) collective-permute-start(bf16[1024,256]{1,0:T(8,128)(2,1)} %collective-permute-done.10), channel_id=1, source_target_pairs={{0,48},{16,0},{32,16},{48,32},{1,49},{17,1},{33,17},{49,33},{2,50}... | collective-permute-start | bytes 1572872 | tf_op jit(solution)/shard_map/ppermute | solution.py:169
  103.6 2.5 collective-permute-start.12
  106.1 2.5 collective-permute-start.13
  108.6 0.0 all-to-all-done.3
  108.6 2.8 %collective-permute-start.6 = (bf16[192,512]{1,0:T(8,128)(2,1)}, bf16[192,512]{1,0:T(8,128)(2,1)S(1)}, u32[]{:S(2)}, u32[]{:S(2)}) collective-permute-start(bf16[192,512]{1,0:T(8,128)(2,1)} %bitcast.9.refs_5_), channel_id=1, source_target_pairs={{0,4},{4,8},{8,12},{12,0},{1,5},{5,9},{9,13},{13,1},{2,6},{6,10},{... | collective-permute-start | bytes 589832 | tf_op jit(solution)/shard_map/ppermute | solution.py:169
  111.4 6.4 %collective-permute-start.7 = (bf16[192,512]{1,0:T(8,128)(2,1)}, bf16[192,512]{1,0:T(8,128)(2,1)S(1)}, u32[]{:S(2)}, u32[]{:S(2)}) collective-permute-start(bf16[192,512]{1,0:T(8,128)(2,1)} %bitcast.9.refs_5_), channel_id=1, source_target_pairs={{0,12},{4,0},{8,4},{12,8},{1,13},{5,1},{9,5},{13,9},{2,14},{6,2},{... | collective-permute-start | bytes 589832 | tf_op jit(solution)/shard_map/ppermute | solution.py:169
  117.8 2.3 attend.2
  120.1 13.8 %all_to_all.26 = bf16[4,3,16,512]{3,2,1,0:T(8,128)(2,1)S(1)} all-to-all(bf16[4,3,16,512]{3,2,1,0:T(8,128)(2,1)S(1)} %attend.2), channel_id=1, replica_groups=mesh['segment'=8,'x'=4,'zh'=4,'tp'=4] {'x'}, dimensions={0} | all-to-all | bytes 393216 | tf_op jit(solution)/shard_map/all_to_all | solution.py:165
  133.9 2.8 %collective-permute-start.2 = (bf16[192,512]{1,0:T(8,128)(2,1)S(1)}, bf16[192,512]{1,0:T(8,128)(2,1)S(1)}, u32[]{:S(2)}, u32[]{:S(2)}) collective-permute-start(bf16[192,512]{1,0:T(8,128)(2,1)S(1)} %bitcast.30), channel_id=1, source_target_pairs={{0,4},{4,8},{8,12},{12,0},{1,5},{5,9},{9,13},{13,1},{2,6},{6,10},{... | collective-permute-start | bytes 589832 | tf_op jit(solution)/shard_map/ppermute | solution.py:169
  136.7 0.0 collective-permute-done.7.refs_7_
  136.7 0.7 copy-done.8
  137.4 6.4 %collective-permute-start.3 = (bf16[192,512]{1,0:T(8,128)(2,1)S(1)}, bf16[192,512]{1,0:T(8,128)(2,1)S(1)}, u32[]{:S(2)}, u32[]{:S(2)}) collective-permute-start(bf16[192,512]{1,0:T(8,128)(2,1)S(1)} %bitcast.31), channel_id=1, source_target_pairs={{0,12},{4,0},{8,4},{12,8},{1,13},{5,1},{9,5},{13,9},{2,14},{6,2},{... | collective-permute-start | bytes 589832 | tf_op jit(solution)/shard_map/ppermute | solution.py:169
  143.8 0.9 slice.23
  144.7 0.9 slice.24
  145.6 7.6 %collective-permute-done.2.refs_1_ = bf16[192,512]{1,0:T(8,128)(2,1)S(1)} collective-permute-done((bf16[192,512]{1,0:T(8,128)(2,1)S(1)}, bf16[192,512]{1,0:T(8,128)(2,1)S(1)}, u32[]{:S(2)}, u32[]{:S(2)}) %collective-permute-start.2) | collective-permute-done | bytes 196640 | tf_op jit(solution)/shard_map/ppermute | solution.py:169
  153.2 2.8 %collective-permute-start.8 = (bf16[96,512]{1,0:T(8,128)(2,1)S(1)}, bf16[96,512]{1,0:T(8,128)(2,1)S(1)}, u32[]{:S(2)}, u32[]{:S(2)}) collective-permute-start(bf16[96,512]{1,0:T(8,128)(2,1)S(1)} %slice.23), channel_id=1, source_target_pairs={{0,4},{4,8},{8,12},{12,0},{1,5},{5,9},{9,13},{13,1},{2,6},{6,10},{... | collective-permute-start | bytes 294920 | tf_op jit(solution)/shard_map/ppermute | solution.py:169
  156.1 6.3 %collective-permute-start.9 = (bf16[96,512]{1,0:T(8,128)(2,1)S(1)}, bf16[96,512]{1,0:T(8,128)(2,1)S(1)}, u32[]{:S(2)}, u32[]{:S(2)}) collective-permute-start(bf16[96,512]{1,0:T(8,128)(2,1)S(1)} %slice.24), channel_id=1, source_target_pairs={{0,12},{4,0},{8,4},{12,8},{1,13},{5,1},{9,5},{13,9},{2,14},{6,2},{... | collective-permute-start | bytes 294920 | tf_op jit(solution)/shard_map/ppermute | solution.py:169
  162.5 2.9 %collective-permute-start.4 = (bf16[96,512]{1,0:T(8,128)(2,1)S(1)}, bf16[96,512]{1,0:T(8,128)(2,1)S(1)}, u32[]{:S(2)}, u32[]{:S(2)}) collective-permute-start(bf16[96,512]{1,0:T(8,128)(2,1)S(1)} %slice.21), channel_id=1, source_target_pairs={{0,4},{4,8},{8,12},{12,0},{1,5},{5,9},{9,13},{13,1},{2,6},{6,10},{... | collective-permute-start | bytes 294920 | tf_op jit(solution)/shard_map/ppermute | solution.py:169
  165.3 0.0 collective-permute-done.12
  165.4 6.3 %collective-permute-start.5 = (bf16[96,512]{1,0:T(8,128)(2,1)S(1)}, bf16[96,512]{1,0:T(8,128)(2,1)S(1)}, u32[]{:S(2)}, u32[]{:S(2)}) collective-permute-start(bf16[96,512]{1,0:T(8,128)(2,1)S(1)} %slice.22), channel_id=1, source_target_pairs={{0,12},{4,0},{8,4},{12,8},{1,13},{5,1},{9,5},{13,9},{2,14},{6,2},{... | collective-permute-start | bytes 294920 | tf_op jit(solution)/shard_map/ppermute | solution.py:169
  171.7 0.0 copy-start.7
  171.7 1.8 pad_maximum_fusion.refs_10_
  173.6 0.0 collective-permute-done.8.refs_8_
  173.6 0.0 collective-permute-done.9.refs_9_
  173.6 1.3 collective-permute-done.5.refs_4_
  174.9 2.9 %project.1 = (bf16[768,256]{1,0:T(8,128)(2,1)S(1)}, bf16[768,256]{1,0:T(8,128)(2,1)S(1)}, bf16[768,256]{1,0:T(8,128)(2,1)S(1)}, bf16[768,256]{1,0:T(8,128)(2,1)S(1)}) custom-call(s32[4]{0:T(128)S(1)} %and_select_fusion.order_ref, bf16[192,512]{1,0:T(8,128)(2,1)S(1)} %bitcast.32, bf16[192,512]{1,0:T(8,128)(2,1)S(1)} %collective-permute-done.2.refs_1_, ...), custom_call_target="tpu_custom_call" | custom-call | flops 1610612736 | bytes 5242880 | tf_op jit(solution)/shard_map/project/pallas_call | solution.py:129
  177.9 8.6 %collective-permute-start.14 = (bf16[768,256]{1,0:T(8,128)(2,1)S(1)}, bf16[768,256]{1,0:T(8,128)(2,1)S(1)}, u32[]{:S(2)}, u32[]{:S(2)}) collective-permute-start(bf16[768,256]{1,0:T(8,128)(2,1)S(1)} %get-tuple-element.9), channel_id=1, source_target_pairs={{0,64},{1,65},{2,66},{3,67},{64,128},{65,129},{66,130},{67,131},{1... | collective-permute-start | bytes 1179656 | tf_op jit(solution)/shard_map/ppermute | solution.py:231
  186.5 1.9 collective-permute-start.15
  188.4 2.7 %collective-permute-start.16 = (bf16[768,256]{1,0:T(8,128)(2,1)S(1)}, bf16[768,256]{1,0:T(8,128)(2,1)S(1)}, u32[]{:S(2)}, u32[]{:S(2)}) collective-permute-start(bf16[768,256]{1,0:T(8,128)(2,1)S(1)} %get-tuple-element.11), channel_id=1, source_target_pairs={{0,66},{1,67},{2,64},{3,65},{64,130},{65,131},{66,128},{67,129},{1... | collective-permute-start | bytes 1179656 | tf_op jit(solution)/shard_map/ppermute | solution.py:231
  191.1 1.9 collective-permute-start.17
  193.1 0.1 select_reduce_fusion
  193.2 0.0 collective-permute-start.1
  193.3 5.3 %collective-permute-done.1.order_ref = s32[48]{0:T(128)S(1)} collective-permute-done((s32[48]{0:T(128)S(1)}, s32[48]{0:T(128)S(1)}, u32[]{:S(2)}, u32[]{:S(2)}) %collective-permute-start.1) | collective-permute-done | bytes 224 | tf_op jit(solution)/shard_map/ppermute | solution.py:211
  198.6 0.0 collective-permute-done.14.refs_0_
  198.6 1.4 collective-permute-done.15.refs_1_
  200.0 21.4 %collective-permute-done.16.refs_2_ = bf16[768,256]{1,0:T(8,128)(2,1)S(1)} collective-permute-done((bf16[768,256]{1,0:T(8,128)(2,1)S(1)}, bf16[768,256]{1,0:T(8,128)(2,1)S(1)}, u32[]{:S(2)}, u32[]{:S(2)}) %collective-permute-start.16) | collective-permute-done | bytes 393248 | tf_op jit(solution)/shard_map/ppermute | solution.py:231
  221.4 0.0 collective-permute-done.17.refs_3_
  221.4 0.7 sum_permute.1
  222.2 0.0 copy-start.10
  222.2 38.2 %all_to_all.27 = bf16[16,3,16,256]{3,2,1,0:T(8,128)(2,1)S(1)} all-to-all(bf16[16,3,16,256]{3,2,1,0:T(8,128)(2,1)S(1)} %bitcast.29), channel_id=1, replica_groups=mesh['segment'=8,'x'=4,'zh'=4,'tp'=4] {'x','zh'}, dimensions={0} | all-to-all | bytes 786432 | tf_op jit(solution)/shard_map/all_to_all | solution.py:165
  260.3 0.2 copy.21
  260.5 0.4 reshape.120
  261.0 0.8 add_convert_fusion
  (28 shorter events, 0.2 us)
Async XLA Ops:
  0.0 7.4 %collective-permute-start = (bf16[192,1024]{1,0:T(8,128)(2,1)}, bf16[192,1024]{1,0:T(8,128)(2,1)S(1)}, u32[]{:S(2)}, u32[]{:S(2)}) collective-permute-start(bf16[192,1024]{1,0:T(8,128)(2,1)} %bitcast.38), channel_id=1, source_target_pairs={{0,448},{64,0},{128,64},{192,128},{256,192},{320,256},{384,320},{4... | collective-permute-start | bytes 1179656 | tf_op jit(solution)/shard_map/ppermute | solution.py:189
  7.4 56.2 %copy-start.11 = (s32[1,3,2]{1,2,0:T(2,128)S(1)}, s32[1,3,2]{1,2,0:T(2,128)}, u32[]{:S(2)}) copy-start(s32[1,3,2]{1,2,0:T(2,128)} %param.10) | copy-start | bytes 76
  7.7 84.5 %copy-start = (bf16[1,3,256,1024]{3,2,1,0:T(8,128)(2,1)S(1)}, bf16[1,3,256,1024]{3,2,1,0:T(8,128)(2,1)}, u32[]{:S(2)}) copy-start(bf16[1,3,256,1024]{3,2,1,0:T(8,128)(2,1)} %param.8) | copy-start | bytes 4718596
  7.7 84.4 %copy-start.1 = (bf16[1,3,256,1024]{3,2,1,0:T(8,128)(2,1)S(1)}, bf16[1,3,256,1024]{3,2,1,0:T(8,128)(2,1)}, u32[]{:S(2)}) copy-start(bf16[1,3,256,1024]{3,2,1,0:T(8,128)(2,1)} %param.9) | copy-start | bytes 4718596
  56.2 0.8 copy-start.2
  57.0 1.0 copy-start.3
  58.9 0.7 copy-start.4
  59.6 32.5 %all-to-all-start.1 = ((bf16[16,3,16,256]{3,2,1,0:T(8,128)(2,1)}), bf16[16,3,16,256]{3,2,1,0:T(8,128)(2,1)S(1)}, u32[]{:S(2)}, u32[]{:S(2)}) async-start(bf16[16,3,16,256]{3,2,1,0:T(8,128)(2,1)} %bitcast.28), calls=%async_computation.1 | async-start | bytes 786432 | tf_op jit(solution)/shard_map/all_to_all | solution.py:165
  63.2 35.9 %collective-permute-start.10 = (bf16[1024,256]{1,0:T(8,128)(2,1)}, bf16[1024,256]{1,0:T(8,128)(2,1)}, u32[]{:S(2)}, u32[]{:S(2)}) collective-permute-start(bf16[1024,256]{1,0:T(8,128)(2,1)} %bitcast.37), channel_id=1, source_target_pairs={{0,448},{64,0},{128,64},{192,128},{256,192},{320,256},{384,320},{4... | collective-permute-start | bytes 1572872 | tf_op jit(solution)/shard_map/ppermute | solution.py:201
  94.4 0.7 copy-start.5
  95.1 13.5 %all-to-all-start.3 = ((bf16[4,3,16,512]{3,2,1,0:T(8,128)(2,1)}), bf16[4,3,16,512]{3,2,1,0:T(8,128)(2,1)}, u32[]{:S(2)}, u32[]{:S(2)}) async-start(bf16[4,3,16,512]{3,2,1,0:T(8,128)(2,1)} %copy-done.5), calls=%async_computation.3 | async-start | bytes 393216 | tf_op jit(solution)/shard_map/all_to_all | solution.py:165
  99.1 63.4 %collective-permute-start.11 = (bf16[1024,256]{1,0:T(8,128)(2,1)}, bf16[1024,256]{1,0:T(8,128)(2,1)}, u32[]{:S(2)}, u32[]{:S(2)}) collective-permute-start(bf16[1024,256]{1,0:T(8,128)(2,1)} %collective-permute-done.10), channel_id=1, source_target_pairs={{0,48},{16,0},{32,16},{48,32},{1,49},{17,1},{33,17},{49,33},{2,50}... | collective-permute-start | bytes 1572872 | tf_op jit(solution)/shard_map/ppermute | solution.py:169
  103.6 61.7 %collective-permute-start.12 = (bf16[1024,256]{1,0:T(8,128)(2,1)}, bf16[1024,256]{1,0:T(8,128)(2,1)}, u32[]{:S(2)}, u32[]{:S(2)}) collective-permute-start(bf16[1024,256]{1,0:T(8,128)(2,1)} %collective-permute-done.10), channel_id=1, source_target_pairs={{0,32},{16,48},{32,0},{48,16},{1,33},{17,49},{33,1},{49,17},{2,34}... | collective-permute-start | bytes 1572872 | tf_op jit(solution)/shard_map/ppermute | solution.py:169
  106.1 65.6 %collective-permute-start.13 = (bf16[1024,256]{1,0:T(8,128)(2,1)}, bf16[1024,256]{1,0:T(8,128)(2,1)}, u32[]{:S(2)}, u32[]{:S(2)}) collective-permute-start(bf16[1024,256]{1,0:T(8,128)(2,1)} %collective-permute-done.10), channel_id=1, source_target_pairs={{0,16},{16,32},{32,48},{48,0},{1,17},{17,33},{33,49},{49,1},{2,18}... | collective-permute-start | bytes 1572872 | tf_op jit(solution)/shard_map/ppermute | solution.py:169
  108.6 25.3 %collective-permute-start.6 = (bf16[192,512]{1,0:T(8,128)(2,1)}, bf16[192,512]{1,0:T(8,128)(2,1)S(1)}, u32[]{:S(2)}, u32[]{:S(2)}) collective-permute-start(bf16[192,512]{1,0:T(8,128)(2,1)} %bitcast.9.refs_5_), channel_id=1, source_target_pairs={{0,4},{4,8},{8,12},{12,0},{1,5},{5,9},{9,13},{13,1},{2,6},{6,10},{... | collective-permute-start | bytes 589832 | tf_op jit(solution)/shard_map/ppermute | solution.py:169
  111.4 25.3 %collective-permute-start.7 = (bf16[192,512]{1,0:T(8,128)(2,1)}, bf16[192,512]{1,0:T(8,128)(2,1)S(1)}, u32[]{:S(2)}, u32[]{:S(2)}) collective-permute-start(bf16[192,512]{1,0:T(8,128)(2,1)} %bitcast.9.refs_5_), channel_id=1, source_target_pairs={{0,12},{4,0},{8,4},{12,8},{1,13},{5,1},{9,5},{13,9},{2,14},{6,2},{... | collective-permute-start | bytes 589832 | tf_op jit(solution)/shard_map/ppermute | solution.py:169
  133.9 2.8 %copy-start.6 = (bf16[192,512]{1,0:T(8,128)(2,1)}, bf16[192,512]{1,0:T(8,128)(2,1)S(1)}, u32[]{:S(2)}) copy-start(bf16[192,512]{1,0:T(8,128)(2,1)S(1)} %collective-permute-done.6.refs_6_) | copy-start | bytes 589828
  133.9 19.3 %collective-permute-start.2 = (bf16[192,512]{1,0:T(8,128)(2,1)S(1)}, bf16[192,512]{1,0:T(8,128)(2,1)S(1)}, u32[]{:S(2)}, u32[]{:S(2)}) collective-permute-start(bf16[192,512]{1,0:T(8,128)(2,1)S(1)} %bitcast.30), channel_id=1, source_target_pairs={{0,4},{4,8},{8,12},{12,0},{1,5},{5,9},{9,13},{13,1},{2,6},{6,10},{... | collective-permute-start | bytes 589832 | tf_op jit(solution)/shard_map/ppermute | solution.py:169
  136.7 0.7 copy-start.8
  137.4 18.7 %collective-permute-start.3 = (bf16[192,512]{1,0:T(8,128)(2,1)S(1)}, bf16[192,512]{1,0:T(8,128)(2,1)S(1)}, u32[]{:S(2)}, u32[]{:S(2)}) collective-permute-start(bf16[192,512]{1,0:T(8,128)(2,1)S(1)} %bitcast.31), channel_id=1, source_target_pairs={{0,12},{4,0},{8,4},{12,8},{1,13},{5,1},{9,5},{13,9},{2,14},{6,2},{... | collective-permute-start | bytes 589832 | tf_op jit(solution)/shard_map/ppermute | solution.py:169
  153.2 20.3 %collective-permute-start.8 = (bf16[96,512]{1,0:T(8,128)(2,1)S(1)}, bf16[96,512]{1,0:T(8,128)(2,1)S(1)}, u32[]{:S(2)}, u32[]{:S(2)}) collective-permute-start(bf16[96,512]{1,0:T(8,128)(2,1)S(1)} %slice.23), channel_id=1, source_target_pairs={{0,4},{4,8},{8,12},{12,0},{1,5},{5,9},{9,13},{13,1},{2,6},{6,10},{... | collective-permute-start | bytes 294920 | tf_op jit(solution)/shard_map/ppermute | solution.py:169
  156.1 17.5 %collective-permute-start.9 = (bf16[96,512]{1,0:T(8,128)(2,1)S(1)}, bf16[96,512]{1,0:T(8,128)(2,1)S(1)}, u32[]{:S(2)}, u32[]{:S(2)}) collective-permute-start(bf16[96,512]{1,0:T(8,128)(2,1)S(1)} %slice.24), channel_id=1, source_target_pairs={{0,12},{4,0},{8,4},{12,8},{1,13},{5,1},{9,5},{13,9},{2,14},{6,2},{... | collective-permute-start | bytes 294920 | tf_op jit(solution)/shard_map/ppermute | solution.py:169
  162.5 11.1 %collective-permute-start.4 = (bf16[96,512]{1,0:T(8,128)(2,1)S(1)}, bf16[96,512]{1,0:T(8,128)(2,1)S(1)}, u32[]{:S(2)}, u32[]{:S(2)}) collective-permute-start(bf16[96,512]{1,0:T(8,128)(2,1)S(1)} %slice.21), channel_id=1, source_target_pairs={{0,4},{4,8},{8,12},{12,0},{1,5},{5,9},{9,13},{13,1},{2,6},{6,10},{... | collective-permute-start | bytes 294920 | tf_op jit(solution)/shard_map/ppermute | solution.py:169
  165.4 9.6 %collective-permute-start.5 = (bf16[96,512]{1,0:T(8,128)(2,1)S(1)}, bf16[96,512]{1,0:T(8,128)(2,1)S(1)}, u32[]{:S(2)}, u32[]{:S(2)}) collective-permute-start(bf16[96,512]{1,0:T(8,128)(2,1)S(1)} %slice.22), channel_id=1, source_target_pairs={{0,12},{4,0},{8,4},{12,8},{1,13},{5,1},{9,5},{13,9},{2,14},{6,2},{... | collective-permute-start | bytes 294920 | tf_op jit(solution)/shard_map/ppermute | solution.py:169
  171.7 3.2 %copy-start.7 = (bf16[192,512]{1,0:T(8,128)(2,1)S(1)}, bf16[192,512]{1,0:T(8,128)(2,1)}, u32[]{:S(2)}) copy-start(bf16[192,512]{1,0:T(8,128)(2,1)} %copy-done.6) | copy-start | bytes 589828
  171.7 3.2 %copy-start.9 = (bf16[192,512]{1,0:T(8,128)(2,1)S(1)}, bf16[192,512]{1,0:T(8,128)(2,1)}, u32[]{:S(2)}) copy-start(bf16[192,512]{1,0:T(8,128)(2,1)} %copy-done.8) | copy-start | bytes 589828
  177.9 20.7 %collective-permute-start.14 = (bf16[768,256]{1,0:T(8,128)(2,1)S(1)}, bf16[768,256]{1,0:T(8,128)(2,1)S(1)}, u32[]{:S(2)}, u32[]{:S(2)}) collective-permute-start(bf16[768,256]{1,0:T(8,128)(2,1)S(1)} %get-tuple-element.9), channel_id=1, source_target_pairs={{0,64},{1,65},{2,66},{3,67},{64,128},{65,129},{66,130},{67,131},{1... | collective-permute-start | bytes 1179656 | tf_op jit(solution)/shard_map/ppermute | solution.py:231
  186.5 13.6 %collective-permute-start.15 = (bf16[768,256]{1,0:T(8,128)(2,1)S(1)}, bf16[768,256]{1,0:T(8,128)(2,1)S(1)}, u32[]{:S(2)}, u32[]{:S(2)}) collective-permute-start(bf16[768,256]{1,0:T(8,128)(2,1)S(1)} %get-tuple-element.10), channel_id=1, source_target_pairs={{0,65},{1,66},{2,67},{3,64},{64,129},{65,130},{66,131},{67,128},{1... | collective-permute-start | bytes 1179656 | tf_op jit(solution)/shard_map/ppermute | solution.py:231
  188.4 33.0 %collective-permute-start.16 = (bf16[768,256]{1,0:T(8,128)(2,1)S(1)}, bf16[768,256]{1,0:T(8,128)(2,1)S(1)}, u32[]{:S(2)}, u32[]{:S(2)}) collective-permute-start(bf16[768,256]{1,0:T(8,128)(2,1)S(1)} %get-tuple-element.11), channel_id=1, source_target_pairs={{0,66},{1,67},{2,64},{3,65},{64,130},{65,131},{66,128},{67,129},{1... | collective-permute-start | bytes 1179656 | tf_op jit(solution)/shard_map/ppermute | solution.py:231
  191.1 30.3 %collective-permute-start.17 = (bf16[768,256]{1,0:T(8,128)(2,1)S(1)}, bf16[768,256]{1,0:T(8,128)(2,1)S(1)}, u32[]{:S(2)}, u32[]{:S(2)}) collective-permute-start(bf16[768,256]{1,0:T(8,128)(2,1)S(1)} %get-tuple-element.12), channel_id=1, source_target_pairs={{0,67},{1,64},{2,65},{3,66},{64,131},{65,128},{66,129},{67,130},{1... | collective-permute-start | bytes 1179656 | tf_op jit(solution)/shard_map/ppermute | solution.py:231
  193.2 5.4 %collective-permute-start.1 = (s32[48]{0:T(128)S(1)}, s32[48]{0:T(128)S(1)}, u32[]{:S(2)}, u32[]{:S(2)}) collective-permute-start(s32[48]{0:T(128)S(1)} %select_reduce_fusion), channel_id=1, source_target_pairs={{0,64},{64,128},{128,192},{192,256},{256,320},{320,384},{384,448},... | collective-permute-start | bytes 584 | tf_op jit(solution)/shard_map/ppermute | solution.py:211
  222.2 38.8 %copy-start.10 = (bf16[1,192,1024]{2,1,0:T(8,128)(2,1)S(1)}, bf16[1,192,1024]{2,1,0:T(8,128)(2,1)}, u32[]{:S(2)}) copy-start(bf16[1,192,1024]{2,1,0:T(8,128)(2,1)} %param.13) | copy-start | bytes 1179652

commit v4 on v3

--- a/solution.py
+++ b/solution.py
@@ -18,7 +18,8 @@
 SMEM = pl.BlockSpec(memory_space=pltpu.SMEM)
 PARAMS = pltpu.CompilerParams(vmem_limit_bytes=40 * 1024 * 1024)
 SEQ = ("x", "zh")
-CHUNKS = 2
+CHUNKS = 1
+AHEAD = (2, 3, 1, 0)
 
 
 def cost(flops, moved, trans=0):
@@ -199,7 +200,6 @@
     spread = exchange(pieces, SEQ)
 
     own = lax.ppermute(out_weight[0], "segment", back)
-    weight = jnp.stack([own, turn(own, "x", -1), turn(own, "x", 2), turn(own, "x", 1)])
 
     table = spread[:, per_dev * ROWS, :per_dev].astype(jnp.int32).reshape(count)
     ids = jnp.arange(count, dtype=jnp.int32)
@@ -212,18 +212,21 @@
 
     ordered = permute_blocks(spread, table, per_dev)
     picked = exchange(ordered.reshape(G * G, per_dev, ROWS, part), SEQ)
+    picked, places, own = lax.optimization_barrier((picked, places, own))
     picked = picked.reshape(G, G, per_dev, ROWS, part)
 
     parts = []
     for chunk in range(CHUNKS):
         answer = attend(picked, nb_keys[0], nb_values[0], nb_lengths[0], chunk, CHUNKS)
         banded = exchange(answer, "x")
+        banded, own = lax.optimization_barrier((banded, own))
+        weight = jnp.stack([own, turn(own, "x", -1), turn(own, "x", 2), turn(own, "x", 1)])
         parts.append(gather_ring(banded.reshape(-1, feats // CHUNKS)))
 
-    order = (t + jnp.arange(G, dtype=jnp.int32) - x) % G
+    order = (t + jnp.array(AHEAD, dtype=jnp.int32) - x) % G
     partial = project(parts, weight, order)
     arrived = []
-    for ahead, block in enumerate(partial):
+    for ahead, block in zip(AHEAD, partial):
         moves = []
         for s in range(sections):
             for i in range(G):

time: 263 us -> 240 us (0.913)
  the two profiles are of different devices: /device:TPU:49 before, /device:TPU:57 now
where the time goes in v4:
time: 240 us; the launch traced here: 239 us
  blocking collectives  90.7 us (38%)
  waiting for transfers between devices  80.1 us (33%)
  starting transfers between devices  55.3 us (23%)
  Pallas kernels  7.49 us (3%)
  other arithmetic  3.02 us (1%)
  local copies, waits for them, and re-layouts  2.58 us (1%)
    all_to_all x3, blocking collectives, exchange(): return lax.all_to_all(value, axes, split_axis=0, concat_axis=0, tiled=True)  90.7 us
    ppermute x7, starting transfers between devices, turn(): return lax.ppermute(value, axis, [(i, (i + by) % G) for i in range(G)])  26.2 us
    ppermute x4, waiting for transfers between devices, local(): arrived.append(lax.ppermute(block, ('segment', 'tp'), moves))  26.1 us
    ppermute x4, starting transfers between devices, local(): arrived.append(lax.ppermute(block, ('segment', 'tp'), moves))  21.9 us
    ppermute x7, waiting for transfers between devices, turn(): return lax.ppermute(value, axis, [(i, (i + by) % G) for i in range(G)])  21.6 us
    all_to_all x1, waiting for transfers between devices, exchange(): return lax.all_to_all(value, axes, split_axis=0, concat_axis=0, tiled=True)  18.5 us
    ppermute x1, waiting for transfers between devices, local(): moved = lax.ppermute(queries[0], 'segment', back)  7.28 us
    ppermute x1, waiting for transfers between devices, local(): own = lax.ppermute(out_weight[0], 'segment', back)  6.61 us
  transfers between devices with their start and end apart: 15, of which 8 were waited for; matrix products, arithmetic and copies ran while one was open for 1% of the time, Pallas kernels for 0%

profile of v4, /device:TPU:57, one launch (start us, length us, event | category | flops | bytes accessed | tf_op | source)
XLA Modules:
  0.0 239.4 jit_solution(13304412007564071096)
XLA Ops:
  0.0 0.7 collective-permute-start
  0.7 0.7 convert_element_type.44
  1.3 7.3 %collective-permute-done = bf16[192,1024]{1,0:T(8,128)(2,1)S(1)} collective-permute-done((bf16[192,1024]{1,0:T(8,128)(2,1)}, bf16[192,1024]{1,0:T(8,128)(2,1)S(1)}, u32[]{:S(2)}, u32[]{:S(2)}) %collective-permute-start) | collective-permute-done | bytes 393248 | tf_op jit(solution)/shard_map/ppermute | solution.py:190
  8.6 0.3 reshape.109
  8.9 0.0 copy-start.5
  8.9 0.0 copy-start.3
  8.9 0.0 copy-start
  9.0 46.5 %all_to_all.20.in_ref = bf16[16,56,256]{2,1,0:T(8,128)(2,1)S(1)} all-to-all(bf16[16,56,256]{2,1,0:T(8,128)(2,1)S(1)} %pad_maximum_fusion.1), channel_id=1, replica_groups=mesh['segment'=8,'x'=4,'zh'=4,'tp'=4] {'x','zh'}, dimensions={0} | all-to-all | bytes 917504 | tf_op jit(solution)/shard_map/all_to_all | solution.py:166
  55.6 0.1 reshape.115.order_ref
  55.7 1.5 permute_blocks.1
  57.2 3.6 %all-to-all-start.1 = ((bf16[16,3,16,256]{3,2,1,0:T(8,128)(2,1)}), bf16[16,3,16,256]{3,2,1,0:T(8,128)(2,1)S(1)}, u32[]{:S(2)}, u32[]{:S(2)}) async-start(bf16[16,3,16,256]{3,2,1,0:T(8,128)(2,1)} %bitcast.3), calls=%async_computation.1 | async-start | bytes 786432 | tf_op jit(solution)/shard_map/all_to_all | solution.py:166
  60.8 0.0 copy-done.5
  60.8 0.3 collective-permute-start.2
  61.2 0.1 select_reduce_fusion
  61.3 2.6 %collective-permute-start.1 = (s32[48]{0:T(128)S(1)}, s32[48]{0:T(128)S(1)}, u32[]{:S(2)}, u32[]{:S(2)}) collective-permute-start(s32[48]{0:T(128)S(1)} %select_reduce_fusion), channel_id=1, source_target_pairs={{0,64},{64,128},{128,192},{192,256},{256,320},{320,384},{384,448},... | collective-permute-start | bytes 584 | tf_op jit(solution)/shard_map/ppermute | solution.py:211
  63.9 0.0 copy-done.3
  63.9 0.1 copy.16.len_ref
  64.0 6.6 %collective-permute-done.2 = bf16[1024,256]{1,0:T(8,128)(2,1)S(1)} collective-permute-done((bf16[1024,256]{1,0:T(8,128)(2,1)S(1)}, bf16[1024,256]{1,0:T(8,128)(2,1)S(1)}, u32[]{:S(2)}, u32[]{:S(2)}) %collective-permute-start.2) | collective-permute-done | bytes 524320 | tf_op jit(solution)/shard_map/ppermute | solution.py:202
  70.6 0.0 collective-permute-done.1.order_ref
  70.6 18.5 %all-to-all-done.1 = bf16[16,3,16,256]{3,2,1,0:T(8,128)(2,1)S(1)} async-done(((bf16[16,3,16,256]{3,2,1,0:T(8,128)(2,1)}), bf16[16,3,16,256]{3,2,1,0:T(8,128)(2,1)S(1)}, u32[]{:S(2)}, u32[]{:S(2)}) %all-to-all-start.1) | async-done | bytes 393248 | tf_op jit(solution)/shard_map/all_to_all | solution.py:166
  89.1 0.0 copy-done
  89.1 0.0 copy-start.1
  89.1 1.4 copy-done.1
  90.5 0.0 copy-start.4
  90.5 2.6 %attend.1 = bf16[4,3,16,1024]{3,2,1,0:T(8,128)(2,1)S(1)} custom-call(s32[3,2]{1,0:T(4,128)S(1)} %copy.16.len_ref, bf16[4,4,3,16,256]{4,3,2,1,0:T(8,128)(2,1)S(1)} %bitcast.23, bf16[3,256,1024]{2,1,0:T(8,128)(2,1)S(1)} %bitcast.21, bf16[3,256,1024]{2,1,0:T(8,128)(2,1)S(1)} %bitcast.22), custom_call_target="tpu_custom_call" | custom-call | flops 201326592 | bytes 3145728 | tf_op jit(solution)/shard_map/attend/pallas_call | solution.py:87
  93.1 8.6 %all_to_all.21 = bf16[4,3,16,1024]{3,2,1,0:T(8,128)(2,1)S(1)} all-to-all(bf16[4,3,16,1024]{3,2,1,0:T(8,128)(2,1)S(1)} %attend.1), channel_id=1, replica_groups=mesh['segment'=8,'x'=4,'zh'=4,'tp'=4] {'x'}, dimensions={0} | all-to-all | bytes 786432 | tf_op jit(solution)/shard_map/all_to_all | solution.py:166
  101.7 4.1 %collective-permute-start.3 = (bf16[192,1024]{1,0:T(8,128)(2,1)S(1)}, bf16[192,1024]{1,0:T(8,128)(2,1)S(1)}, u32[]{:S(2)}, u32[]{:S(2)}) collective-permute-start(bf16[192,1024]{1,0:T(8,128)(2,1)S(1)} %bitcast.25), channel_id=1, source_target_pairs={{0,4},{4,8},{8,12},{12,0},{1,5},{5,9},{9,13},{13,1},{2,6},{6,10},{... | collective-permute-start | bytes 1179656 | tf_op jit(solution)/shard_map/ppermute | solution.py:170
  105.8 5.1 %collective-permute-start.4 = (bf16[192,1024]{1,0:T(8,128)(2,1)S(1)}, bf16[192,1024]{1,0:T(8,128)(2,1)S(1)}, u32[]{:S(2)}, u32[]{:S(2)}) collective-permute-start(bf16[192,1024]{1,0:T(8,128)(2,1)S(1)} %bitcast.26), channel_id=1, source_target_pairs={{0,12},{4,0},{8,4},{12,8},{1,13},{5,1},{9,5},{13,9},{2,14},{6,2},{... | collective-permute-start | bytes 1179656 | tf_op jit(solution)/shard_map/ppermute | solution.py:170
  110.9 2.8 %collective-permute-start.7 = (bf16[1024,256]{1,0:T(8,128)(2,1)S(1)}, bf16[1024,256]{1,0:T(8,128)(2,1)S(1)}, u32[]{:S(2)}, u32[]{:S(2)}) collective-permute-start(bf16[1024,256]{1,0:T(8,128)(2,1)S(1)} %collective-permute-done.2), channel_id=1, source_target_pairs={{0,48},{16,0},{32,16},{48,32},{1,49},{17,1},{33,17},{49,33},{2,50}... | collective-permute-start | bytes 1572872 | tf_op jit(solution)/shard_map/ppermute | solution.py:170
  113.7 3.1 %collective-permute-start.8 = (bf16[1024,256]{1,0:T(8,128)(2,1)S(1)}, bf16[1024,256]{1,0:T(8,128)(2,1)S(1)}, u32[]{:S(2)}, u32[]{:S(2)}) collective-permute-start(bf16[1024,256]{1,0:T(8,128)(2,1)S(1)} %collective-permute-done.2), channel_id=1, source_target_pairs={{0,32},{16,48},{32,0},{48,16},{1,33},{17,49},{33,1},{49,17},{2,34}... | collective-permute-start | bytes 1572872 | tf_op jit(solution)/shard_map/ppermute | solution.py:170
  116.8 1.9 collective-permute-start.9
  118.8 16.1 %collective-permute-done.3.refs_1_ = bf16[192,1024]{1,0:T(8,128)(2,1)S(1)} collective-permute-done((bf16[192,1024]{1,0:T(8,128)(2,1)S(1)}, bf16[192,1024]{1,0:T(8,128)(2,1)S(1)}, u32[]{:S(2)}, u32[]{:S(2)}) %collective-permute-start.3) | collective-permute-done | bytes 393248 | tf_op jit(solution)/shard_map/ppermute | solution.py:170
  134.9 2.1 collective-permute-start.5
  137.0 0.0 collective-permute-done.4.refs_2_
  137.0 7.1 %collective-permute-start.6 = (bf16[96,1024]{1,0:T(8,128)(2,1)S(1)}, bf16[96,1024]{1,0:T(8,128)(2,1)S(1)}, u32[]{:S(2)}, u32[]{:S(2)}) collective-permute-start(bf16[96,1024]{1,0:T(8,128)(2,1)S(1)} %slice.14), channel_id=1, source_target_pairs={{0,12},{4,0},{8,4},{12,8},{1,13},{5,1},{9,5},{13,9},{2,14},{6,2},{... | collective-permute-start | bytes 589832 | tf_op jit(solution)/shard_map/ppermute | solution.py:170
  144.1 0.0 copy-done.4
  144.1 0.0 collective-permute-done.7
  144.1 0.0 collective-permute-done.8
  144.2 0.0 collective-permute-done.9
  144.2 1.3 pad_maximum_fusion.refs_5_
  145.5 3.9 %collective-permute-done.5.refs_3_ = bf16[96,1024]{1,0:T(8,128)(2,1)S(1)} collective-permute-done((bf16[96,1024]{1,0:T(8,128)(2,1)S(1)}, bf16[96,1024]{1,0:T(8,128)(2,1)S(1)}, u32[]{:S(2)}, u32[]{:S(2)}) %collective-permute-start.5) | collective-permute-done | bytes 196640 | tf_op jit(solution)/shard_map/ppermute | solution.py:170
  149.4 1.6 collective-permute-done.6.refs_4_
  151.0 2.7 %project.1 = (bf16[768,256]{1,0:T(8,128)(2,1)S(1)}, bf16[768,256]{1,0:T(8,128)(2,1)S(1)}, bf16[768,256]{1,0:T(8,128)(2,1)S(1)}, bf16[768,256]{1,0:T(8,128)(2,1)S(1)}) custom-call(s32[4]{0:T(128)S(1)} %and_select_fusion.order_ref, bf16[192,1024]{1,0:T(8,128)(2,1)S(1)} %bitcast.27, bf16[192,1024]{1,0:T(8,128)(2,1)S(1)} %collective-permute-done.3.refs_1_, ...), custom_call_target="tpu_custom_call" | custom-call | flops 1610612736 | bytes 5242880 | tf_op jit(solution)/shard_map/project/pallas_call | solution.py:130
  153.7 1.9 collective-permute-start.10
  155.6 11.3 %collective-permute-start.11 = (bf16[768,256]{1,0:T(8,128)(2,1)S(1)}, bf16[768,256]{1,0:T(8,128)(2,1)S(1)}, u32[]{:S(2)}, u32[]{:S(2)}) collective-permute-start(bf16[768,256]{1,0:T(8,128)(2,1)S(1)} %get-tuple-element.20), channel_id=1, source_target_pairs={{0,67},{1,64},{2,65},{3,66},{64,131},{65,128},{66,129},{67,130},{1... | collective-permute-start | bytes 1179656 | tf_op jit(solution)/shard_map/ppermute | solution.py:234
  166.9 1.9 collective-permute-start.12
  168.8 6.8 %collective-permute-start.13 = (bf16[768,256]{1,0:T(8,128)(2,1)S(1)}, bf16[768,256]{1,0:T(8,128)(2,1)S(1)}, u32[]{:S(2)}, u32[]{:S(2)}) collective-permute-start(bf16[768,256]{1,0:T(8,128)(2,1)S(1)} %get-tuple-element.22), channel_id=1, source_target_pairs={{0,64},{1,65},{2,66},{3,67},{64,128},{65,129},{66,130},{67,131},{1... | collective-permute-start | bytes 1179656 | tf_op jit(solution)/shard_map/ppermute | solution.py:234
  175.6 3.0 %collective-permute-done.10.refs_0_ = bf16[768,256]{1,0:T(8,128)(2,1)S(1)} collective-permute-done((bf16[768,256]{1,0:T(8,128)(2,1)S(1)}, bf16[768,256]{1,0:T(8,128)(2,1)S(1)}, u32[]{:S(2)}, u32[]{:S(2)}) %collective-permute-start.10) | collective-permute-done | bytes 393248 | tf_op jit(solution)/shard_map/ppermute | solution.py:234
  178.6 23.1 %collective-permute-done.11.refs_1_ = bf16[768,256]{1,0:T(8,128)(2,1)S(1)} collective-permute-done((bf16[768,256]{1,0:T(8,128)(2,1)S(1)}, bf16[768,256]{1,0:T(8,128)(2,1)S(1)}, u32[]{:S(2)}, u32[]{:S(2)}) %collective-permute-start.11) | collective-permute-done | bytes 393248 | tf_op jit(solution)/shard_map/ppermute | solution.py:234
  201.7 0.0 collective-permute-done.12.refs_2_
  201.7 0.0 collective-permute-done.13.refs_3_
  201.7 0.7 sum_permute.1
  202.5 0.0 copy-start.2
  202.5 35.5 %all_to_all.22 = bf16[16,3,16,256]{3,2,1,0:T(8,128)(2,1)S(1)} all-to-all(bf16[16,3,16,256]{3,2,1,0:T(8,128)(2,1)S(1)} %bitcast.24), channel_id=1, replica_groups=mesh['segment'=8,'x'=4,'zh'=4,'tp'=4] {'x','zh'}, dimensions={0} | all-to-all | bytes 786432 | tf_op jit(solution)/shard_map/all_to_all | solution.py:166
  238.0 0.2 copy.19
  238.2 0.4 reshape.116
  238.6 0.0 copy-done.2
  238.6 0.8 add_convert_fusion
  (9 shorter events, 0.2 us)
Async XLA Ops:
  0.0 8.6 %collective-permute-start = (bf16[192,1024]{1,0:T(8,128)(2,1)}, bf16[192,1024]{1,0:T(8,128)(2,1)S(1)}, u32[]{:S(2)}, u32[]{:S(2)}) collective-permute-start(bf16[192,1024]{1,0:T(8,128)(2,1)} %bitcast.36), channel_id=1, source_target_pairs={{0,448},{64,0},{128,64},{192,128},{256,192},{320,256},{384,320},{4... | collective-permute-start | bytes 1179656 | tf_op jit(solution)/shard_map/ppermute | solution.py:190
  8.9 51.9 %copy-start.5 = (bf16[1,1024,256]{2,1,0:T(8,128)(2,1)S(1)}, bf16[1,1024,256]{2,1,0:T(8,128)(2,1)}, u32[]{:S(2)}) copy-start(bf16[1,1024,256]{2,1,0:T(8,128)(2,1)} %param.13) | copy-start | bytes 1572868
  8.9 55.0 %copy-start.3 = (s32[1,3,2]{1,2,0:T(2,128)S(1)}, s32[1,3,2]{1,2,0:T(2,128)}, u32[]{:S(2)}) copy-start(s32[1,3,2]{1,2,0:T(2,128)} %param.11) | copy-start | bytes 76
  8.9 80.2 %copy-start = (bf16[1,3,256,1024]{3,2,1,0:T(8,128)(2,1)S(1)}, bf16[1,3,256,1024]{3,2,1,0:T(8,128)(2,1)}, u32[]{:S(2)}) copy-start(bf16[1,3,256,1024]{3,2,1,0:T(8,128)(2,1)} %param.9) | copy-start | bytes 4718596
  57.2 31.9 %all-to-all-start.1 = ((bf16[16,3,16,256]{3,2,1,0:T(8,128)(2,1)}), bf16[16,3,16,256]{3,2,1,0:T(8,128)(2,1)S(1)}, u32[]{:S(2)}, u32[]{:S(2)}) async-start(bf16[16,3,16,256]{3,2,1,0:T(8,128)(2,1)} %bitcast.3), calls=%async_computation.1 | async-start | bytes 786432 | tf_op jit(solution)/shard_map/all_to_all | solution.py:166
  60.8 9.8 %collective-permute-start.2 = (bf16[1024,256]{1,0:T(8,128)(2,1)S(1)}, bf16[1024,256]{1,0:T(8,128)(2,1)S(1)}, u32[]{:S(2)}, u32[]{:S(2)}) collective-permute-start(bf16[1024,256]{1,0:T(8,128)(2,1)S(1)} %bitcast.35), channel_id=1, source_target_pairs={{0,448},{64,0},{128,64},{192,128},{256,192},{320,256},{384,320},{4... | collective-permute-start | bytes 1572872 | tf_op jit(solution)/shard_map/ppermute | solution.py:202
  61.3 9.3 %collective-permute-start.1 = (s32[48]{0:T(128)S(1)}, s32[48]{0:T(128)S(1)}, u32[]{:S(2)}, u32[]{:S(2)}) collective-permute-start(s32[48]{0:T(128)S(1)} %select_reduce_fusion), channel_id=1, source_target_pairs={{0,64},{64,128},{128,192},{192,256},{256,320},{320,384},{384,448},... | collective-permute-start | bytes 584 | tf_op jit(solution)/shard_map/ppermute | solution.py:211
  89.1 1.4 copy-start.1
  90.5 53.6 %copy-start.4 = (s32[4]{0:T(128)S(1)}, s32[4]{0:T(128)}, u32[]{:S(2)}) copy-start(s32[4]{0:T(128)} %constant.74.clone) | copy-start | bytes 52
  101.7 33.1 %collective-permute-start.3 = (bf16[192,1024]{1,0:T(8,128)(2,1)S(1)}, bf16[192,1024]{1,0:T(8,128)(2,1)S(1)}, u32[]{:S(2)}, u32[]{:S(2)}) collective-permute-start(bf16[192,1024]{1,0:T(8,128)(2,1)S(1)} %bitcast.25), channel_id=1, source_target_pairs={{0,4},{4,8},{8,12},{12,0},{1,5},{5,9},{9,13},{13,1},{2,6},{6,10},{... | collective-permute-start | bytes 1179656 | tf_op jit(solution)/shard_map/ppermute | solution.py:170
  105.8 31.2 %collective-permute-start.4 = (bf16[192,1024]{1,0:T(8,128)(2,1)S(1)}, bf16[192,1024]{1,0:T(8,128)(2,1)S(1)}, u32[]{:S(2)}, u32[]{:S(2)}) collective-permute-start(bf16[192,1024]{1,0:T(8,128)(2,1)S(1)} %bitcast.26), channel_id=1, source_target_pairs={{0,12},{4,0},{8,4},{12,8},{1,13},{5,1},{9,5},{13,9},{2,14},{6,2},{... | collective-permute-start | bytes 1179656 | tf_op jit(solution)/shard_map/ppermute | solution.py:170
  110.9 33.2 %collective-permute-start.7 = (bf16[1024,256]{1,0:T(8,128)(2,1)S(1)}, bf16[1024,256]{1,0:T(8,128)(2,1)S(1)}, u32[]{:S(2)}, u32[]{:S(2)}) collective-permute-start(bf16[1024,256]{1,0:T(8,128)(2,1)S(1)} %collective-permute-done.2), channel_id=1, source_target_pairs={{0,48},{16,0},{32,16},{48,32},{1,49},{17,1},{33,17},{49,33},{2,50}... | collective-permute-start | bytes 1572872 | tf_op jit(solution)/shard_map/ppermute | solution.py:170
  113.7 30.4 %collective-permute-start.8 = (bf16[1024,256]{1,0:T(8,128)(2,1)S(1)}, bf16[1024,256]{1,0:T(8,128)(2,1)S(1)}, u32[]{:S(2)}, u32[]{:S(2)}) collective-permute-start(bf16[1024,256]{1,0:T(8,128)(2,1)S(1)} %collective-permute-done.2), channel_id=1, source_target_pairs={{0,32},{16,48},{32,0},{48,16},{1,33},{17,49},{33,1},{49,17},{2,34}... | collective-permute-start | bytes 1572872 | tf_op jit(solution)/shard_map/ppermute | solution.py:170
  116.8 27.3 %collective-permute-start.9 = (bf16[1024,256]{1,0:T(8,128)(2,1)S(1)}, bf16[1024,256]{1,0:T(8,128)(2,1)}, u32[]{:S(2)}, u32[]{:S(2)}) collective-permute-start(bf16[1024,256]{1,0:T(8,128)(2,1)S(1)} %collective-permute-done.2), channel_id=1, source_target_pairs={{0,16},{16,32},{32,48},{48,0},{1,17},{17,33},{33,49},{49,1},{2,18}... | collective-permute-start | bytes 1572872 | tf_op jit(solution)/shard_map/ppermute | solution.py:170
  134.9 14.5 %collective-permute-start.5 = (bf16[96,1024]{1,0:T(8,128)(2,1)S(1)}, bf16[96,1024]{1,0:T(8,128)(2,1)S(1)}, u32[]{:S(2)}, u32[]{:S(2)}) collective-permute-start(bf16[96,1024]{1,0:T(8,128)(2,1)S(1)} %slice.13), channel_id=1, source_target_pairs={{0,4},{4,8},{8,12},{12,0},{1,5},{5,9},{9,13},{13,1},{2,6},{6,10},{... | collective-permute-start | bytes 589832 | tf_op jit(solution)/shard_map/ppermute | solution.py:170
  137.0 14.0 %collective-permute-start.6 = (bf16[96,1024]{1,0:T(8,128)(2,1)S(1)}, bf16[96,1024]{1,0:T(8,128)(2,1)S(1)}, u32[]{:S(2)}, u32[]{:S(2)}) collective-permute-start(bf16[96,1024]{1,0:T(8,128)(2,1)S(1)} %slice.14), channel_id=1, source_target_pairs={{0,12},{4,0},{8,4},{12,8},{1,13},{5,1},{9,5},{13,9},{2,14},{6,2},{... | collective-permute-start | bytes 589832 | tf_op jit(solution)/shard_map/ppermute | solution.py:170
  153.7 24.9 %collective-permute-start.10 = (bf16[768,256]{1,0:T(8,128)(2,1)S(1)}, bf16[768,256]{1,0:T(8,128)(2,1)S(1)}, u32[]{:S(2)}, u32[]{:S(2)}) collective-permute-start(bf16[768,256]{1,0:T(8,128)(2,1)S(1)} %get-tuple-element.19), channel_id=1, source_target_pairs={{0,66},{1,67},{2,64},{3,65},{64,130},{65,131},{66,128},{67,129},{1... | collective-permute-start | bytes 1179656 | tf_op jit(solution)/shard_map/ppermute | solution.py:234
  155.6 46.1 %collective-permute-start.11 = (bf16[768,256]{1,0:T(8,128)(2,1)S(1)}, bf16[768,256]{1,0:T(8,128)(2,1)S(1)}, u32[]{:S(2)}, u32[]{:S(2)}) collective-permute-start(bf16[768,256]{1,0:T(8,128)(2,1)S(1)} %get-tuple-element.20), channel_id=1, source_target_pairs={{0,67},{1,64},{2,65},{3,66},{64,131},{65,128},{66,129},{67,130},{1... | collective-permute-start | bytes 1179656 | tf_op jit(solution)/shard_map/ppermute | solution.py:234
  166.9 34.8 %collective-permute-start.12 = (bf16[768,256]{1,0:T(8,128)(2,1)S(1)}, bf16[768,256]{1,0:T(8,128)(2,1)S(1)}, u32[]{:S(2)}, u32[]{:S(2)}) collective-permute-start(bf16[768,256]{1,0:T(8,128)(2,1)S(1)} %get-tuple-element.21), channel_id=1, source_target_pairs={{0,65},{1,66},{2,67},{3,64},{64,129},{65,130},{66,131},{67,128},{1... | collective-permute-start | bytes 1179656 | tf_op jit(solution)/shard_map/ppermute | solution.py:234
  168.8 32.9 %collective-permute-start.13 = (bf16[768,256]{1,0:T(8,128)(2,1)S(1)}, bf16[768,256]{1,0:T(8,128)(2,1)S(1)}, u32[]{:S(2)}, u32[]{:S(2)}) collective-permute-start(bf16[768,256]{1,0:T(8,128)(2,1)S(1)} %get-tuple-element.22), channel_id=1, source_target_pairs={{0,64},{1,65},{2,66},{3,67},{64,128},{65,129},{66,130},{67,131},{1... | collective-permute-start | bytes 1179656 | tf_op jit(solution)/shard_map/ppermute | solution.py:234
  202.5 36.1 %copy-start.2 = (bf16[1,192,1024]{2,1,0:T(8,128)(2,1)S(1)}, bf16[1,192,1024]{2,1,0:T(8,128)(2,1)}, u32[]{:S(2)}) copy-start(bf16[1,192,1024]{2,1,0:T(8,128)(2,1)} %param.14) | copy-start | bytes 1179652

commit v5 on v4

--- a/solution.py
+++ b/solution.py
@@ -18,8 +18,9 @@
 SMEM = pl.BlockSpec(memory_space=pltpu.SMEM)
 PARAMS = pltpu.CompilerParams(vmem_limit_bytes=40 * 1024 * 1024)
 SEQ = ("x", "zh")
+NOTE = 8
 CHUNKS = 1
-AHEAD = (2, 3, 1, 0)
+AHEAD = (2, 1, 3, 0)
 
 
 def cost(flops, moved, trans=0):
@@ -29,15 +30,17 @@
 def permute_kernel(per_dev, order_ref, in_ref, out_ref):
     for slot in range(out_ref.shape[0]):
         taken = order_ref[slot]
-        start = pl.multiple_of(lax.rem(taken, per_dev) * ROWS, ROWS)
-        out_ref[slot] = in_ref[lax.div(taken, per_dev), pl.ds(start, ROWS), :]
+        rows = out_ref.shape[1]
+        start = pl.multiple_of(lax.rem(taken, per_dev) * rows, rows)
+        out_ref[slot] = in_ref[lax.div(taken, per_dev), pl.ds(start, rows), :]
 
 
 def permute_blocks(spread, order, per_dev):
-    sources, _, part = spread.shape
+    sources, _, lanes = spread.shape
+    rows = (spread.shape[1] - NOTE) // per_dev
     return pl.pallas_call(
         functools.partial(permute_kernel, per_dev),
-        out_shape=jax.ShapeDtypeStruct((sources * per_dev, ROWS, part), spread.dtype),
+        out_shape=jax.ShapeDtypeStruct((sources * per_dev, rows, lanes), spread.dtype),
         in_specs=[SMEM, VMEM],
         out_specs=VMEM,
         compiler_params=PARAMS,
@@ -58,8 +61,7 @@
     lanes = [slice(head * HD, (head + 1) * HD) for head in range(heads)]
     scores = []
     for head in range(heads):
-        part = slice((head % per_group) * HD, (head % per_group + 1) * HD)
-        q = q_ref[:, head // per_group, 0, :, part].reshape(STRETCH, HD)
+        q = q_ref[:, head // per_group, 0, head % per_group].reshape(STRETCH, HD)
         scores.append(
             lax.dot_general(
                 q,
@@ -90,7 +92,7 @@
         grid=(slots,),
         in_specs=[
             SMEM,
-            pl.BlockSpec((G, groups, 1, ROWS, feats // G), lambda s: (0, chunk, s, 0, 0)),
+            pl.BlockSpec((G, groups, 1, feats // G // HD, ROWS, HD), lambda s: (0, chunk, s, 0, 0, 0)),
             pl.BlockSpec((1, span, wide), lambda s: (s, 0, chunk)),
             pl.BlockSpec((1, span, wide), lambda s: (s, 0, chunk)),
         ],
@@ -162,6 +164,30 @@
     )(order, *parts)
 
 
+def finish_kernel(in_ref, residual_ref, out_ref):
+    _, per_dev, rows, part = in_ref.shape
+    for x in range(G):
+        for zh in range(G):
+            for within in range(per_dev):
+                start = (within * G + x) * rows
+                here = (slice(start, start + rows), slice(zh * part, (zh + 1) * part))
+                total = residual_ref[here].astype(jnp.float32)
+                total = total + in_ref[x * G + zh, within].astype(jnp.float32)
+                out_ref[here] = total.astype(out_ref.dtype)
+
+
+def finish(owned, residual):
+    return pl.pallas_call(
+        finish_kernel,
+        out_shape=jax.ShapeDtypeStruct(residual.shape, residual.dtype),
+        in_specs=[VMEM, VMEM],
+        out_specs=VMEM,
+        compiler_params=PARAMS,
+        cost_estimate=cost(residual.size, 6 * residual.size),
+        name="finish",
+    )(owned, residual)
+
+
 def exchange(value, axes):
     return lax.all_to_all(value, axes, split_axis=0, concat_axis=0, tiled=True)
 
@@ -188,11 +214,12 @@
     x, zh, t = lax.axis_index("x"), lax.axis_index("zh"), lax.axis_index("tp")
 
     moved = lax.ppermute(queries[0], "segment", back)
-    pieces = moved.reshape(per_dev, G, ROWS, G, part).transpose(1, 3, 0, 2, 4)
-    note = jnp.pad(slot_stretch.astype(jnp.bfloat16), ((0, 7), (0, part - per_dev)))
+    pair = part // HD
+    pieces = moved.reshape(per_dev, G, ROWS, G, pair, HD).transpose(1, 3, 0, 4, 2, 5)
+    note = jnp.pad(slot_stretch.astype(jnp.bfloat16), ((0, NOTE - 1), (0, HD - per_dev)))
     pieces = jnp.concatenate(
         [
-            pieces.reshape(G * G, per_dev * ROWS, part),
+            pieces.reshape(G * G, per_dev * pair * ROWS, HD),
             jnp.broadcast_to(note[None], (G * G,) + note.shape),
         ],
         axis=1,
@@ -201,7 +228,7 @@
 
     own = lax.ppermute(out_weight[0], "segment", back)
 
-    table = spread[:, per_dev * ROWS, :per_dev].astype(jnp.int32).reshape(count)
+    table = spread[:, per_dev * pair * ROWS, :per_dev].astype(jnp.int32).reshape(count)
     ids = jnp.arange(count, dtype=jnp.int32)
     holder, within = ids // per_dev, ids % per_dev
     apart = (holder % G - zh) % G
@@ -211,9 +238,9 @@
     places = lax.ppermute(places, "segment", onward)
 
     ordered = permute_blocks(spread, table, per_dev)
-    picked = exchange(ordered.reshape(G * G, per_dev, ROWS, part), SEQ)
+    picked = exchange(ordered.reshape(G * G, per_dev, pair * ROWS, HD), SEQ)
     picked, places, own = lax.optimization_barrier((picked, places, own))
-    picked = picked.reshape(G, G, per_dev, ROWS, part)
+    picked = picked.reshape(G, G, per_dev, pair, ROWS, HD)
 
     parts = []
     for chunk in range(CHUNKS):
@@ -234,9 +261,7 @@
         arrived.append(lax.ppermute(block, ("segment", "tp"), moves))
     summed = sum_permute(arrived, places)
     owned = exchange(summed.reshape(G * G, per_dev, ROWS, part), SEQ)
-    owned = owned.reshape(G, G, per_dev, ROWS, part).transpose(2, 0, 3, 1, 4)
-    projected = owned.reshape(per_dev * STRETCH, feats).astype(jnp.float32)
-    return (residual[0].astype(jnp.float32) + projected).astype(jnp.bfloat16)[None]
+    return finish(owned, residual[0])[None]
 
 
 def solution(mesh):

time: 240 us -> 237 us (0.988)
  the two profiles are of different devices: /device:TPU:57 before, /device:TPU:65 now
where the time goes in v5:
time: 237 us
  blocking collectives  95 us (40%)
  waiting for transfers between devices  66.6 us (28%)
  starting transfers between devices  62.3 us (26%)
  Pallas kernels  8.33 us (4%)
    all_to_all x3, blocking collectives, exchange(): return lax.all_to_all(value, axes, split_axis=0, concat_axis=0, tiled=True)  95 us
    ppermute x7, starting transfers between devices, turn(): return lax.ppermute(value, axis, [(i, (i + by) % G) for i in range(G)])  34.7 us
    ppermute x4, waiting for transfers between devices, local(): arrived.append(lax.ppermute(block, ('segment', 'tp'), moves))  21.7 us
    ppermute x4, starting transfers between devices, local(): arrived.append(lax.ppermute(block, ('segment', 'tp'), moves))  21.5 us
    all_to_all x1, waiting for transfers between devices, exchange(): return lax.all_to_all(value, axes, split_axis=0, concat_axis=0, tiled=True)  17.8 us
    ppermute x7, waiting for transfers between devices, turn(): return lax.ppermute(value, axis, [(i, (i + by) % G) for i in range(G)])  14.3 us
    ppermute x1, waiting for transfers between devices, local(): own = lax.ppermute(out_weight[0], 'segment', back)  6.61 us
    ppermute x1, waiting for transfers between devices, local(): moved = lax.ppermute(queries[0], 'segment', back)  6.18 us
  transfers between devices with their start and end apart: 15, of which 8 were waited for; matrix products, arithmetic and copies ran while one was open for 1% of the time, Pallas kernels for 0%

profile of v5, /device:TPU:65, one launch (start us, length us, event | category | flops | bytes accessed | tf_op | source)
XLA Modules:
  0.0 236.7 jit_solution(449190017087373370)
XLA Ops:
  0.0 0.7 collective-permute-start
  0.7 0.7 convert_element_type.16
  1.3 6.2 %collective-permute-done = bf16[192,1024]{1,0:T(8,128)(2,1)S(1)} collective-permute-done((bf16[192,1024]{1,0:T(8,128)(2,1)}, bf16[192,1024]{1,0:T(8,128)(2,1)S(1)}, u32[]{:S(2)}, u32[]{:S(2)}) %collective-permute-start) | collective-permute-done | bytes 393248 | tf_op jit(solution)/shard_map/ppermute | solution.py:216
  7.5 0.3 reshape.93
  7.8 0.0 copy-start.5
  7.8 0.0 copy-start.3
  7.8 0.0 copy-start
  7.8 0.1 copy.13
  8.0 45.2 %all_to_all.20.in_ref = bf16[16,104,128]{2,1,0:T(8,128)(2,1)S(1)} all-to-all(bf16[16,104,128]{2,1,0:T(8,128)(2,1)S(1)} %pad_maximum_fusion.1), channel_id=1, replica_groups=mesh['segment'=8,'x'=4,'zh'=4,'tp'=4] {'x','zh'}, dimensions={0} | all-to-all | bytes 851968 | tf_op jit(solution)/shard_map/all_to_all | solution.py:192
  53.2 0.1 reshape.99.order_ref
  53.3 1.5 permute_blocks.1
  54.8 3.7 %all-to-all-start.1 = ((bf16[16,3,32,128]{3,2,1,0:T(8,128)(2,1)}), bf16[16,3,32,128]{3,2,1,0:T(8,128)(2,1)S(1)}, u32[]{:S(2)}, u32[]{:S(2)}) async-start(bf16[16,3,32,128]{3,2,1,0:T(8,128)(2,1)} %bitcast.3), calls=%async_computation.1 | async-start | bytes 786432 | tf_op jit(solution)/shard_map/all_to_all | solution.py:192
  58.4 0.0 copy-done.5
  58.4 1.4 collective-permute-start.2
  59.9 0.1 select_reduce_fusion
  60.0 0.3 collective-permute-start.1
  60.4 0.0 copy-done.3
  60.4 0.1 copy.14.len_ref
  60.5 6.6 %collective-permute-done.2 = bf16[1024,256]{1,0:T(8,128)(2,1)S(1)} collective-permute-done((bf16[1024,256]{1,0:T(8,128)(2,1)S(1)}, bf16[1024,256]{1,0:T(8,128)(2,1)S(1)}, u32[]{:S(2)}, u32[]{:S(2)}) %collective-permute-start.2) | collective-permute-done | bytes 524320 | tf_op jit(solution)/shard_map/ppermute | solution.py:229
  67.1 0.0 collective-permute-done.1.order_ref
  67.1 17.8 %all-to-all-done.1 = bf16[16,3,32,128]{3,2,1,0:T(8,128)(2,1)S(1)} async-done(((bf16[16,3,32,128]{3,2,1,0:T(8,128)(2,1)}), bf16[16,3,32,128]{3,2,1,0:T(8,128)(2,1)S(1)}, u32[]{:S(2)}, u32[]{:S(2)}) %all-to-all-start.1) | async-done | bytes 393248 | tf_op jit(solution)/shard_map/all_to_all | solution.py:192
  84.9 0.0 copy-done
  84.9 0.0 copy-start.1
  84.9 1.4 copy-done.1
  86.3 0.0 copy-start.4
  86.3 2.6 %attend.1 = bf16[4,3,16,1024]{3,2,1,0:T(8,128)(2,1)S(1)} custom-call(s32[3,2]{1,0:T(4,128)S(1)} %copy.14.len_ref, bf16[4,4,3,2,16,128]{5,4,3,2,1,0:T(8,128)(2,1)S(1)} %bitcast.20, bf16[3,256,1024]{2,1,0:T(8,128)(2,1)S(1)} %bitcast.18, bf16[3,256,1024]{2,1,0:T(8,128)(2,1)S(1)} %bitcast.19), custom_call_target="tpu_custom_call" | custom-call | flops 201326592 | bytes 3145728 | tf_op jit(solution)/shard_map/attend/pallas_call | solution.py:89
  88.9 10.1 %all_to_all.21 = bf16[4,3,16,1024]{3,2,1,0:T(8,128)(2,1)S(1)} all-to-all(bf16[4,3,16,1024]{3,2,1,0:T(8,128)(2,1)S(1)} %attend.1), channel_id=1, replica_groups=mesh['segment'=8,'x'=4,'zh'=4,'tp'=4] {'x'}, dimensions={0} | all-to-all | bytes 786432 | tf_op jit(solution)/shard_map/all_to_all | solution.py:192
  98.9 1.9 collective-permute-start.3
  100.8 7.3 %collective-permute-start.4 = (bf16[192,1024]{1,0:T(8,128)(2,1)S(1)}, bf16[192,1024]{1,0:T(8,128)(2,1)S(1)}, u32[]{:S(2)}, u32[]{:S(2)}) collective-permute-start(bf16[192,1024]{1,0:T(8,128)(2,1)S(1)} %bitcast.23), channel_id=1, source_target_pairs={{0,12},{4,0},{8,4},{12,8},{1,13},{5,1},{9,5},{13,9},{2,14},{6,2},{... | collective-permute-start | bytes 1179656 | tf_op jit(solution)/shard_map/ppermute | solution.py:196
  108.1 2.8 %collective-permute-start.7 = (bf16[1024,256]{1,0:T(8,128)(2,1)S(1)}, bf16[1024,256]{1,0:T(8,128)(2,1)S(1)}, u32[]{:S(2)}, u32[]{:S(2)}) collective-permute-start(bf16[1024,256]{1,0:T(8,128)(2,1)S(1)} %collective-permute-done.2), channel_id=1, source_target_pairs={{0,48},{16,0},{32,16},{48,32},{1,49},{17,1},{33,17},{49,33},{2,50}... | collective-permute-start | bytes 1572872 | tf_op jit(solution)/shard_map/ppermute | solution.py:196
  110.9 3.1 %collective-permute-start.8 = (bf16[1024,256]{1,0:T(8,128)(2,1)S(1)}, bf16[1024,256]{1,0:T(8,128)(2,1)S(1)}, u32[]{:S(2)}, u32[]{:S(2)}) collective-permute-start(bf16[1024,256]{1,0:T(8,128)(2,1)S(1)} %collective-permute-done.2), channel_id=1, source_target_pairs={{0,32},{16,48},{32,0},{48,16},{1,33},{17,49},{33,1},{49,17},{2,34}... | collective-permute-start | bytes 1572872 | tf_op jit(solution)/shard_map/ppermute | solution.py:196
  114.0 1.9 collective-permute-start.9
  116.0 13.1 %collective-permute-done.3.refs_1_ = bf16[192,1024]{1,0:T(8,128)(2,1)S(1)} collective-permute-done((bf16[192,1024]{1,0:T(8,128)(2,1)S(1)}, bf16[192,1024]{1,0:T(8,128)(2,1)S(1)}, u32[]{:S(2)}, u32[]{:S(2)}) %collective-permute-start.3) | collective-permute-done | bytes 393248 | tf_op jit(solution)/shard_map/ppermute | solution.py:196
  129.1 2.2 collective-permute-start.5
  131.3 0.0 collective-permute-done.4.refs_2_
  131.4 15.5 %collective-permute-start.6 = (bf16[96,1024]{1,0:T(8,128)(2,1)S(1)}, bf16[96,1024]{1,0:T(8,128)(2,1)S(1)}, u32[]{:S(2)}, u32[]{:S(2)}) collective-permute-start(bf16[96,1024]{1,0:T(8,128)(2,1)S(1)} %slice.14), channel_id=1, source_target_pairs={{0,12},{4,0},{8,4},{12,8},{1,13},{5,1},{9,5},{13,9},{2,14},{6,2},{... | collective-permute-start | bytes 589832 | tf_op jit(solution)/shard_map/ppermute | solution.py:196
  146.9 0.0 copy-done.4
  146.9 0.0 collective-permute-done.7
  146.9 0.0 collective-permute-done.8
  146.9 0.0 collective-permute-done.9
  146.9 1.3 pad_maximum_fusion.refs_5_
  148.2 0.0 collective-permute-done.5.refs_3_
  148.3 1.2 collective-permute-done.6.refs_4_
  149.5 2.7 %project.1 = (bf16[768,256]{1,0:T(8,128)(2,1)S(1)}, bf16[768,256]{1,0:T(8,128)(2,1)S(1)}, bf16[768,256]{1,0:T(8,128)(2,1)S(1)}, bf16[768,256]{1,0:T(8,128)(2,1)S(1)}) custom-call(s32[4]{0:T(128)S(1)} %and_select_fusion.order_ref, bf16[192,1024]{1,0:T(8,128)(2,1)S(1)} %bitcast.24, bf16[192,1024]{1,0:T(8,128)(2,1)S(1)} %collective-permute-done.3.refs_1_, ...), custom_call_target="tpu_custom_call" | custom-call | flops 1610612736 | bytes 5242880 | tf_op jit(solution)/shard_map/project/pallas_call | solution.py:132
  152.1 0.0 copy-start.2
  152.1 17.5 %collective-permute-start.10 = (bf16[768,256]{1,0:T(8,128)(2,1)S(1)}, bf16[768,256]{1,0:T(8,128)(2,1)S(1)}, u32[]{:S(2)}, u32[]{:S(2)}) collective-permute-start(bf16[768,256]{1,0:T(8,128)(2,1)S(1)} %get-tuple-element.19), channel_id=1, source_target_pairs={{0,66},{1,67},{2,64},{3,65},{64,130},{65,131},{66,128},{67,129},{1... | collective-permute-start | bytes 1179656 | tf_op jit(solution)/shard_map/ppermute | solution.py:261
  169.6 1.9 collective-permute-start.11
  171.5 1.9 collective-permute-start.12
  173.5 0.2 collective-permute-start.13
  173.6 15.4 %collective-permute-done.10.refs_0_ = bf16[768,256]{1,0:T(8,128)(2,1)S(1)} collective-permute-done((bf16[768,256]{1,0:T(8,128)(2,1)S(1)}, bf16[768,256]{1,0:T(8,128)(2,1)S(1)}, u32[]{:S(2)}, u32[]{:S(2)}) %collective-permute-start.10) | collective-permute-done | bytes 393248 | tf_op jit(solution)/shard_map/ppermute | solution.py:261
  189.0 5.5 %collective-permute-done.11.refs_1_ = bf16[768,256]{1,0:T(8,128)(2,1)S(1)} collective-permute-done((bf16[768,256]{1,0:T(8,128)(2,1)S(1)}, bf16[768,256]{1,0:T(8,128)(2,1)S(1)}, u32[]{:S(2)}, u32[]{:S(2)}) %collective-permute-start.11) | collective-permute-done | bytes 393248 | tf_op jit(solution)/shard_map/ppermute | solution.py:261
  194.5 0.8 collective-permute-done.12.refs_2_
  195.3 0.0 collective-permute-done.13.refs_3_
  195.3 0.7 sum_permute.1
  196.0 39.8 %all_to_all.22.in_ref = bf16[16,3,16,256]{3,2,1,0:T(8,128)(2,1)S(1)} all-to-all(bf16[16,3,16,256]{3,2,1,0:T(8,128)(2,1)S(1)} %bitcast.21), channel_id=1, replica_groups=mesh['segment'=8,'x'=4,'zh'=4,'tp'=4] {'x','zh'}, dimensions={0} | all-to-all | bytes 786432 | tf_op jit(solution)/shard_map/all_to_all | solution.py:192
  235.8 0.0 copy-done.2
  235.8 0.8 finish.1
  (8 shorter events, 0.2 us)
Async XLA Ops:
  0.0 7.5 %collective-permute-start = (bf16[192,1024]{1,0:T(8,128)(2,1)}, bf16[192,1024]{1,0:T(8,128)(2,1)S(1)}, u32[]{:S(2)}, u32[]{:S(2)}) collective-permute-start(bf16[192,1024]{1,0:T(8,128)(2,1)} %bitcast.32), channel_id=1, source_target_pairs={{0,448},{64,0},{128,64},{192,128},{256,192},{320,256},{384,320},{4... | collective-permute-start | bytes 1179656 | tf_op jit(solution)/shard_map/ppermute | solution.py:216
  7.8 50.6 %copy-start.5 = (bf16[1,1024,256]{2,1,0:T(8,128)(2,1)S(1)}, bf16[1,1024,256]{2,1,0:T(8,128)(2,1)}, u32[]{:S(2)}) copy-start(bf16[1,1024,256]{2,1,0:T(8,128)(2,1)} %param.13) | copy-start | bytes 1572868
  7.8 52.5 %copy-start.3 = (s32[1,3,2]{1,2,0:T(2,128)S(1)}, s32[1,3,2]{1,2,0:T(2,128)}, u32[]{:S(2)}) copy-start(s32[1,3,2]{1,2,0:T(2,128)} %param.11) | copy-start | bytes 76
  7.8 77.1 %copy-start = (bf16[1,3,256,1024]{3,2,1,0:T(8,128)(2,1)S(1)}, bf16[1,3,256,1024]{3,2,1,0:T(8,128)(2,1)}, u32[]{:S(2)}) copy-start(bf16[1,3,256,1024]{3,2,1,0:T(8,128)(2,1)} %param.9) | copy-start | bytes 4718596
  54.8 30.1 %all-to-all-start.1 = ((bf16[16,3,32,128]{3,2,1,0:T(8,128)(2,1)}), bf16[16,3,32,128]{3,2,1,0:T(8,128)(2,1)S(1)}, u32[]{:S(2)}, u32[]{:S(2)}) async-start(bf16[16,3,32,128]{3,2,1,0:T(8,128)(2,1)} %bitcast.3), calls=%async_computation.1 | async-start | bytes 786432 | tf_op jit(solution)/shard_map/all_to_all | solution.py:192
  58.4 8.6 %collective-permute-start.2 = (bf16[1024,256]{1,0:T(8,128)(2,1)S(1)}, bf16[1024,256]{1,0:T(8,128)(2,1)S(1)}, u32[]{:S(2)}, u32[]{:S(2)}) collective-permute-start(bf16[1024,256]{1,0:T(8,128)(2,1)S(1)} %bitcast.31), channel_id=1, source_target_pairs={{0,448},{64,0},{128,64},{192,128},{256,192},{320,256},{384,320},{4... | collective-permute-start | bytes 1572872 | tf_op jit(solution)/shard_map/ppermute | solution.py:229
  60.0 7.0 %collective-permute-start.1 = (s32[48]{0:T(128)S(1)}, s32[48]{0:T(128)S(1)}, u32[]{:S(2)}, u32[]{:S(2)}) collective-permute-start(s32[48]{0:T(128)S(1)} %select_reduce_fusion), channel_id=1, source_target_pairs={{0,64},{64,128},{128,192},{192,256},{256,320},{320,384},{384,448},... | collective-permute-start | bytes 584 | tf_op jit(solution)/shard_map/ppermute | solution.py:238
  84.9 1.4 copy-start.1
  86.3 60.6 %copy-start.4 = (s32[4]{0:T(128)S(1)}, s32[4]{0:T(128)}, u32[]{:S(2)}) copy-start(s32[4]{0:T(128)} %constant.74.clone) | copy-start | bytes 52
  98.9 30.1 %collective-permute-start.3 = (bf16[192,1024]{1,0:T(8,128)(2,1)S(1)}, bf16[192,1024]{1,0:T(8,128)(2,1)S(1)}, u32[]{:S(2)}, u32[]{:S(2)}) collective-permute-start(bf16[192,1024]{1,0:T(8,128)(2,1)S(1)} %bitcast.22), channel_id=1, source_target_pairs={{0,4},{4,8},{8,12},{12,0},{1,5},{5,9},{9,13},{13,1},{2,6},{6,10},{... | collective-permute-start | bytes 1179656 | tf_op jit(solution)/shard_map/ppermute | solution.py:196
  100.8 30.5 %collective-permute-start.4 = (bf16[192,1024]{1,0:T(8,128)(2,1)S(1)}, bf16[192,1024]{1,0:T(8,128)(2,1)S(1)}, u32[]{:S(2)}, u32[]{:S(2)}) collective-permute-start(bf16[192,1024]{1,0:T(8,128)(2,1)S(1)} %bitcast.23), channel_id=1, source_target_pairs={{0,12},{4,0},{8,4},{12,8},{1,13},{5,1},{9,5},{13,9},{2,14},{6,2},{... | collective-permute-start | bytes 1179656 | tf_op jit(solution)/shard_map/ppermute | solution.py:196
  108.1 38.8 %collective-permute-start.7 = (bf16[1024,256]{1,0:T(8,128)(2,1)S(1)}, bf16[1024,256]{1,0:T(8,128)(2,1)S(1)}, u32[]{:S(2)}, u32[]{:S(2)}) collective-permute-start(bf16[1024,256]{1,0:T(8,128)(2,1)S(1)} %collective-permute-done.2), channel_id=1, source_target_pairs={{0,48},{16,0},{32,16},{48,32},{1,49},{17,1},{33,17},{49,33},{2,50}... | collective-permute-start | bytes 1572872 | tf_op jit(solution)/shard_map/ppermute | solution.py:196
  110.9 36.0 %collective-permute-start.8 = (bf16[1024,256]{1,0:T(8,128)(2,1)S(1)}, bf16[1024,256]{1,0:T(8,128)(2,1)S(1)}, u32[]{:S(2)}, u32[]{:S(2)}) collective-permute-start(bf16[1024,256]{1,0:T(8,128)(2,1)S(1)} %collective-permute-done.2), channel_id=1, source_target_pairs={{0,32},{16,48},{32,0},{48,16},{1,33},{17,49},{33,1},{49,17},{2,34}... | collective-permute-start | bytes 1572872 | tf_op jit(solution)/shard_map/ppermute | solution.py:196
  114.0 32.9 %collective-permute-start.9 = (bf16[1024,256]{1,0:T(8,128)(2,1)S(1)}, bf16[1024,256]{1,0:T(8,128)(2,1)}, u32[]{:S(2)}, u32[]{:S(2)}) collective-permute-start(bf16[1024,256]{1,0:T(8,128)(2,1)S(1)} %collective-permute-done.2), channel_id=1, source_target_pairs={{0,16},{16,32},{32,48},{48,0},{1,17},{17,33},{33,49},{49,1},{2,18}... | collective-permute-start | bytes 1572872 | tf_op jit(solution)/shard_map/ppermute | solution.py:196
  129.1 19.2 %collective-permute-start.5 = (bf16[96,1024]{1,0:T(8,128)(2,1)S(1)}, bf16[96,1024]{1,0:T(8,128)(2,1)S(1)}, u32[]{:S(2)}, u32[]{:S(2)}) collective-permute-start(bf16[96,1024]{1,0:T(8,128)(2,1)S(1)} %slice.13), channel_id=1, source_target_pairs={{0,4},{4,8},{8,12},{12,0},{1,5},{5,9},{9,13},{13,1},{2,6},{6,10},{... | collective-permute-start | bytes 589832 | tf_op jit(solution)/shard_map/ppermute | solution.py:196
  131.4 18.1 %collective-permute-start.6 = (bf16[96,1024]{1,0:T(8,128)(2,1)S(1)}, bf16[96,1024]{1,0:T(8,128)(2,1)S(1)}, u32[]{:S(2)}, u32[]{:S(2)}) collective-permute-start(bf16[96,1024]{1,0:T(8,128)(2,1)S(1)} %slice.14), channel_id=1, source_target_pairs={{0,12},{4,0},{8,4},{12,8},{1,13},{5,1},{9,5},{13,9},{2,14},{6,2},{... | collective-permute-start | bytes 589832 | tf_op jit(solution)/shard_map/ppermute | solution.py:196
  152.1 83.7 %copy-start.2 = (bf16[1,192,1024]{2,1,0:T(8,128)(2,1)S(1)}, bf16[1,192,1024]{2,1,0:T(8,128)(2,1)}, u32[]{:S(2)}) copy-start(bf16[1,192,1024]{2,1,0:T(8,128)(2,1)} %param.14) | copy-start | bytes 1179652
  152.1 36.9 %collective-permute-start.10 = (bf16[768,256]{1,0:T(8,128)(2,1)S(1)}, bf16[768,256]{1,0:T(8,128)(2,1)S(1)}, u32[]{:S(2)}, u32[]{:S(2)}) collective-permute-start(bf16[768,256]{1,0:T(8,128)(2,1)S(1)} %get-tuple-element.19), channel_id=1, source_target_pairs={{0,66},{1,67},{2,64},{3,65},{64,130},{65,131},{66,128},{67,129},{1... | collective-permute-start | bytes 1179656 | tf_op jit(solution)/shard_map/ppermute | solution.py:261
  169.6 24.9 %collective-permute-start.11 = (bf16[768,256]{1,0:T(8,128)(2,1)S(1)}, bf16[768,256]{1,0:T(8,128)(2,1)S(1)}, u32[]{:S(2)}, u32[]{:S(2)}) collective-permute-start(bf16[768,256]{1,0:T(8,128)(2,1)S(1)} %get-tuple-element.20), channel_id=1, source_target_pairs={{0,65},{1,66},{2,67},{3,64},{64,129},{65,130},{66,131},{67,128},{1... | collective-permute-start | bytes 1179656 | tf_op jit(solution)/shard_map/ppermute | solution.py:261
  171.5 23.8 %collective-permute-start.12 = (bf16[768,256]{1,0:T(8,128)(2,1)S(1)}, bf16[768,256]{1,0:T(8,128)(2,1)S(1)}, u32[]{:S(2)}, u32[]{:S(2)}) collective-permute-start(bf16[768,256]{1,0:T(8,128)(2,1)S(1)} %get-tuple-element.21), channel_id=1, source_target_pairs={{0,67},{1,64},{2,65},{3,66},{64,131},{65,128},{66,129},{67,130},{1... | collective-permute-start | bytes 1179656 | tf_op jit(solution)/shard_map/ppermute | solution.py:261
  173.5 21.8 %collective-permute-start.13 = (bf16[768,256]{1,0:T(8,128)(2,1)S(1)}, bf16[768,256]{1,0:T(8,128)(2,1)S(1)}, u32[]{:S(2)}, u32[]{:S(2)}) collective-permute-start(bf16[768,256]{1,0:T(8,128)(2,1)S(1)} %get-tuple-element.22), channel_id=1, source_target_pairs={{0,64},{1,65},{2,66},{3,67},{64,128},{65,129},{66,130},{67,131},{1... | collective-permute-start | bytes 1179656 | tf_op jit(solution)/shard_map/ppermute | solution.py:261

commit v6 on v5

--- a/solution.py
+++ b/solution.py
@@ -21,6 +21,7 @@
 NOTE = 8
 CHUNKS = 1
 AHEAD = (2, 1, 3, 0)
+FORWARD = 16
 
 
 def cost(flops, moved, trans=0):
@@ -103,41 +104,33 @@
     )(lengths, picked, keys, values)
 
 
-def project_kernel(chunks, order_ref, *refs):
-    parts = len(refs[:-G - 1]) // chunks
-    w_ref, outs = refs[-G - 1], refs[-G:]
-    wide = refs[0].shape[1]
-    for out, group in zip(outs, range(G)):
-        taken = order_ref[group]
+def project_kernel(order_ref, *refs):
+    blocks, weights, outs = refs[: -2 * G], refs[-2 * G : -G], refs[-G:]
+
+    def fill(out, w_ref):
         start = 0
-        for part in range(parts):
-            rows = refs[part].shape[0]
-            total = None
-            for chunk in range(chunks):
-                product = jnp.dot(
-                    refs[chunk * parts + part][...],
-                    w_ref[taken, chunk * wide : (chunk + 1) * wide, :],
-                    preferred_element_type=jnp.float32,
-                )
-                total = product if total is None else total + product
-            out[start : start + rows, :] = total.astype(jnp.bfloat16)
-            start += rows
-
-
-def project(parts, weight, order):
-    chunks = len(parts)
-    m = sum(p.shape[0] for p in parts[0])
-    _, k, n = weight.shape
-    flat = [p for chunk in parts for p in chunk]
-    return pl.pallas_call(
-        functools.partial(project_kernel, chunks),
+        for ref in blocks:
+            product = jnp.dot(ref[...], w_ref[...], preferred_element_type=jnp.float32)
+            out[start : start + ref.shape[0], :] = product.astype(jnp.bfloat16)
+            start += ref.shape[0]
+
+    for group, out in enumerate(outs):
+        for distance, w_ref in enumerate(weights):
+            pl.when(order_ref[group] == distance)(functools.partial(fill, out, w_ref))
+
+
+def project(blocks, weights, order):
+    m = sum(block.shape[0] for block in blocks)
+    k, n = weights[0].shape
+    return pl.pallas_call(
+        project_kernel,
         out_shape=[jax.ShapeDtypeStruct((m, n), jnp.bfloat16)] * G,
-        in_specs=[SMEM] + [VMEM] * (len(flat) + 1),
+        in_specs=[SMEM] + [VMEM] * (len(blocks) + G),
         out_specs=[VMEM] * G,
         compiler_params=PARAMS,
         cost_estimate=cost(2 * m * n * k * G, 2 * (m * k + G * n * k + G * m * n)),
         name="project",
-    )(order, *flat, weight)
+    )(order, *blocks, *weights)
 
 
 def sum_permute_kernel(order_ref, *refs):
@@ -197,7 +190,7 @@
 
 
 def gather_ring(value):
-    half = value.shape[0] // 2
+    half = value.shape[0] // 2 + FORWARD
     below = turn(value, "zh", 1)
     above = turn(value, "zh", -1)
     return [value, below, above, turn(below[:half], "zh", 1), turn(above[half:], "zh", -1)]
@@ -247,11 +240,11 @@
         answer = attend(picked, nb_keys[0], nb_values[0], nb_lengths[0], chunk, CHUNKS)
         banded = exchange(answer, "x")
         banded, own = lax.optimization_barrier((banded, own))
-        weight = jnp.stack([own, turn(own, "x", -1), turn(own, "x", 2), turn(own, "x", 1)])
+        weight = [own, turn(own, "x", -1), turn(own, "x", 2), turn(own, "x", 1)]
         parts.append(gather_ring(banded.reshape(-1, feats // CHUNKS)))
 
     order = (t + jnp.array(AHEAD, dtype=jnp.int32) - x) % G
-    partial = project(parts, weight, order)
+    partial = project(parts[0], weight, order)
     arrived = []
     for ahead, block in zip(AHEAD, partial):
         moves = []

time: 237 us -> 237 us (level)
  the two profiles are of different devices: /device:TPU:65 before, /device:TPU:73 now
where the time goes in v6:
time: 237 us; the launch traced here: 236 us
  blocking collectives  91.6 us (39%)
  waiting for transfers between devices  85.2 us (36%)
  starting transfers between devices  46.8 us (20%)
  Pallas kernels  9.28 us (4%)
    all_to_all x3, blocking collectives, exchange(): return lax.all_to_all(value, axes, split_axis=0, concat_axis=0, tiled=True)  91.6 us
    ppermute x7, waiting for transfers between devices, turn(): return lax.ppermute(value, axis, [(i, (i + by) % G) for i in range(G)])  27.6 us
    ppermute x7, starting transfers between devices, turn(): return lax.ppermute(value, axis, [(i, (i + by) % G) for i in range(G)])  26.8 us
    ppermute x4, waiting for transfers between devices, local(): arrived.append(lax.ppermute(block, ('segment', 'tp'), moves))  24.7 us
    all_to_all x1, waiting for transfers between devices, exchange(): return lax.all_to_all(value, axes, split_axis=0, concat_axis=0, tiled=True)  20.2 us
    ppermute x4, starting transfers between devices, local(): arrived.append(lax.ppermute(block, ('segment', 'tp'), moves))  14 us
    ppermute x1, waiting for transfers between devices, local(): own = lax.ppermute(out_weight[0], 'segment', back)  6.61 us
    ppermute x1, waiting for transfers between devices, local(): moved = lax.ppermute(queries[0], 'segment', back)  6.18 us
  transfers between devices with their start and end apart: 15, of which 9 were waited for; matrix products, arithmetic and copies ran while one was open for 0% of the time, Pallas kernels for 0%

profile of v6, /device:TPU:73, one launch (start us, length us, event | category | flops | bytes accessed | tf_op | source)
XLA Modules:
  0.0 236.0 jit_solution(13965323041729511549)
XLA Ops:
  0.0 0.7 collective-permute-start
  0.7 0.7 convert_element_type.16
  1.3 6.2 %collective-permute-done = bf16[192,1024]{1,0:T(8,128)(2,1)S(1)} collective-permute-done((bf16[192,1024]{1,0:T(8,128)(2,1)}, bf16[192,1024]{1,0:T(8,128)(2,1)S(1)}, u32[]{:S(2)}, u32[]{:S(2)}) %collective-permute-start) | collective-permute-done | bytes 393248 | tf_op jit(solution)/shard_map/ppermute | solution.py:209
  7.5 0.3 reshape.93
  7.8 0.1 copy.13
  7.9 0.0 copy-start.5
  7.9 0.0 copy-start.3
  7.9 0.0 copy-start
  8.0 45.3 %all_to_all.20.in_ref = bf16[16,104,128]{2,1,0:T(8,128)(2,1)S(1)} all-to-all(bf16[16,104,128]{2,1,0:T(8,128)(2,1)S(1)} %pad_maximum_fusion), channel_id=1, replica_groups=mesh['segment'=8,'x'=4,'zh'=4,'tp'=4] {'x','zh'}, dimensions={0} | all-to-all | bytes 851968 | tf_op jit(solution)/shard_map/all_to_all | solution.py:185
  53.3 0.1 reshape.99.order_ref
  53.4 1.5 permute_blocks.1
  54.9 3.6 %all-to-all-start.1 = ((bf16[16,3,32,128]{3,2,1,0:T(8,128)(2,1)}), bf16[16,3,32,128]{3,2,1,0:T(8,128)(2,1)S(1)}, u32[]{:S(2)}, u32[]{:S(2)}) async-start(bf16[16,3,32,128]{3,2,1,0:T(8,128)(2,1)} %bitcast.3), calls=%async_computation.1 | async-start | bytes 786432 | tf_op jit(solution)/shard_map/all_to_all | solution.py:185
  58.5 0.0 copy-done.5
  58.5 0.4 collective-permute-start.2
  58.9 0.1 select_reduce_fusion
  59.0 1.4 collective-permute-start.1
  60.4 0.0 copy-done.3
  60.4 0.1 copy.14.len_ref
  60.5 6.6 %collective-permute-done.2.refs_5_ = bf16[1024,256]{1,0:T(8,128)(2,1)S(1)} collective-permute-done((bf16[1024,256]{1,0:T(8,128)(2,1)S(1)}, bf16[1024,256]{1,0:T(8,128)(2,1)S(1)}, u32[]{:S(2)}, u32[]{:S(2)}) %collective-permute-start.2) | collective-permute-done | bytes 524320 | tf_op jit(solution)/shard_map/ppermute | solution.py:222
  67.1 0.0 collective-permute-done.1.order_ref
  67.1 20.2 %all-to-all-done.1 = bf16[16,3,32,128]{3,2,1,0:T(8,128)(2,1)S(1)} async-done(((bf16[16,3,32,128]{3,2,1,0:T(8,128)(2,1)}), bf16[16,3,32,128]{3,2,1,0:T(8,128)(2,1)S(1)}, u32[]{:S(2)}, u32[]{:S(2)}) %all-to-all-start.1) | async-done | bytes 393248 | tf_op jit(solution)/shard_map/all_to_all | solution.py:185
  87.3 0.0 copy-done
  87.3 0.0 copy-start.1
  87.3 1.4 copy-done.1
  88.7 2.6 %attend.1 = bf16[4,3,16,1024]{3,2,1,0:T(8,128)(2,1)S(1)} custom-call(s32[3,2]{1,0:T(4,128)S(1)} %copy.14.len_ref, bf16[4,4,3,2,16,128]{5,4,3,2,1,0:T(8,128)(2,1)S(1)} %bitcast.16, bf16[3,256,1024]{2,1,0:T(8,128)(2,1)S(1)} %bitcast.14, bf16[3,256,1024]{2,1,0:T(8,128)(2,1)S(1)} %bitcast.15), custom_call_target="tpu_custom_call" | custom-call | flops 201326592 | bytes 3145728 | tf_op jit(solution)/shard_map/attend/pallas_call | solution.py:90
  91.3 0.0 copy-start.4
  91.3 9.4 %all_to_all.21 = bf16[4,3,16,1024]{3,2,1,0:T(8,128)(2,1)S(1)} all-to-all(bf16[4,3,16,1024]{3,2,1,0:T(8,128)(2,1)S(1)} %attend.1), channel_id=1, replica_groups=mesh['segment'=8,'x'=4,'zh'=4,'tp'=4] {'x'}, dimensions={0} | all-to-all | bytes 786432 | tf_op jit(solution)/shard_map/all_to_all | solution.py:185
  100.7 1.9 collective-permute-start.3
  102.6 7.3 %collective-permute-start.4 = (bf16[192,1024]{1,0:T(8,128)(2,1)S(1)}, bf16[192,1024]{1,0:T(8,128)(2,1)S(1)}, u32[]{:S(2)}, u32[]{:S(2)}) collective-permute-start(bf16[192,1024]{1,0:T(8,128)(2,1)S(1)} %bitcast.19), channel_id=1, source_target_pairs={{0,12},{4,0},{8,4},{12,8},{1,13},{5,1},{9,5},{13,9},{2,14},{6,2},{... | collective-permute-start | bytes 1179656 | tf_op jit(solution)/shard_map/ppermute | solution.py:189
  109.9 2.2 collective-permute-start.9
  112.1 3.7 %collective-permute-start.8 = (bf16[1024,256]{1,0:T(8,128)(2,1)S(1)}, bf16[1024,256]{1,0:T(8,128)(2,1)S(1)}, u32[]{:S(2)}, u32[]{:S(2)}) collective-permute-start(bf16[1024,256]{1,0:T(8,128)(2,1)S(1)} %collective-permute-done.2.refs_5_), channel_id=1, source_target_pairs={{0,32},{16,48},{32,0},{48,16},{1,33},{17,49},{33,1},{49,17},{2,34}... | collective-permute-start | bytes 1572872 | tf_op jit(solution)/shard_map/ppermute | solution.py:189
  115.8 2.5 %collective-permute-start.7 = (bf16[1024,256]{1,0:T(8,128)(2,1)S(1)}, bf16[1024,256]{1,0:T(8,128)(2,1)}, u32[]{:S(2)}, u32[]{:S(2)}) collective-permute-start(bf16[1024,256]{1,0:T(8,128)(2,1)S(1)} %collective-permute-done.2.refs_5_), channel_id=1, source_target_pairs={{0,48},{16,0},{32,16},{48,32},{1,49},{17,1},{33,17},{49,33},{2,50}... | collective-permute-start | bytes 1572872 | tf_op jit(solution)/shard_map/ppermute | solution.py:189
  118.3 17.7 %collective-permute-done.3.refs_1_ = bf16[192,1024]{1,0:T(8,128)(2,1)S(1)} collective-permute-done((bf16[192,1024]{1,0:T(8,128)(2,1)S(1)}, bf16[192,1024]{1,0:T(8,128)(2,1)S(1)}, u32[]{:S(2)}, u32[]{:S(2)}) %collective-permute-start.3) | collective-permute-done | bytes 393248 | tf_op jit(solution)/shard_map/ppermute | solution.py:189
  136.1 3.4 %collective-permute-start.5 = (bf16[112,1024]{1,0:T(8,128)(2,1)S(1)}, bf16[112,1024]{1,0:T(8,128)(2,1)S(1)}, u32[]{:S(2)}, u32[]{:S(2)}) collective-permute-start(bf16[112,1024]{1,0:T(8,128)(2,1)S(1)} %slice.13), channel_id=1, source_target_pairs={{0,4},{4,8},{8,12},{12,0},{1,5},{5,9},{9,13},{13,1},{2,6},{6,10},{... | collective-permute-start | bytes 688136 | tf_op jit(solution)/shard_map/ppermute | solution.py:189
  139.4 0.0 collective-permute-done.4.refs_2_
  139.5 5.8 %collective-permute-start.6 = (bf16[80,1024]{1,0:T(8,128)(2,1)S(1)}, bf16[80,1024]{1,0:T(8,128)(2,1)S(1)}, u32[]{:S(2)}, u32[]{:S(2)}) collective-permute-start(bf16[80,1024]{1,0:T(8,128)(2,1)S(1)} %slice.14), channel_id=1, source_target_pairs={{0,12},{4,0},{8,4},{12,8},{1,13},{5,1},{9,5},{13,9},{2,14},{6,2},{... | collective-permute-start | bytes 491528 | tf_op jit(solution)/shard_map/ppermute | solution.py:189
  145.3 0.0 copy-done.4
  145.3 0.0 collective-permute-done.9.refs_8_
  145.3 0.0 collective-permute-done.8.refs_7_
  145.3 0.0 collective-permute-done.7.refs_6_
  145.4 4.8 %collective-permute-done.6.refs_4_ = bf16[80,1024]{1,0:T(8,128)(2,1)S(1)} collective-permute-done((bf16[80,1024]{1,0:T(8,128)(2,1)S(1)}, bf16[80,1024]{1,0:T(8,128)(2,1)S(1)}, u32[]{:S(2)}, u32[]{:S(2)}) %collective-permute-start.6) | collective-permute-done | bytes 163872 | tf_op jit(solution)/shard_map/ppermute | solution.py:189
  150.2 5.0 %collective-permute-done.5.refs_3_ = bf16[112,1024]{1,0:T(8,128)(2,1)S(1)} collective-permute-done((bf16[112,1024]{1,0:T(8,128)(2,1)S(1)}, bf16[112,1024]{1,0:T(8,128)(2,1)S(1)}, u32[]{:S(2)}, u32[]{:S(2)}) %collective-permute-start.5) | collective-permute-done | bytes 229408 | tf_op jit(solution)/shard_map/ppermute | solution.py:189
  155.2 3.6 %project.1 = (bf16[768,256]{1,0:T(8,128)(2,1)S(1)}, bf16[768,256]{1,0:T(8,128)(2,1)S(1)}, bf16[768,256]{1,0:T(8,128)(2,1)S(1)}, bf16[768,256]{1,0:T(8,128)(2,1)S(1)}) custom-call(s32[4]{0:T(128)S(1)} %and_select_fusion.order_ref, bf16[192,1024]{1,0:T(8,128)(2,1)S(1)} %bitcast.20, bf16[192,1024]{1,0:T(8,128)(2,1)S(1)} %collective-permute-done.3.refs_1_, ...), custom_call_target="tpu_custom_call" | custom-call | flops 1610612736 | bytes 5242880 | tf_op jit(solution)/shard_map/project/pallas_call | solution.py:125
  158.8 0.0 copy-start.2
  158.9 8.0 %collective-permute-start.10 = (bf16[768,256]{1,0:T(8,128)(2,1)S(1)}, bf16[768,256]{1,0:T(8,128)(2,1)S(1)}, u32[]{:S(2)}, u32[]{:S(2)}) collective-permute-start(bf16[768,256]{1,0:T(8,128)(2,1)S(1)} %get-tuple-element.19), channel_id=1, source_target_pairs={{0,66},{1,67},{2,64},{3,65},{64,130},{65,131},{66,128},{67,129},{1... | collective-permute-start | bytes 1179656 | tf_op jit(solution)/shard_map/ppermute | solution.py:254
  166.9 1.9 collective-permute-start.11
  168.8 1.9 collective-permute-start.12
  170.7 2.2 collective-permute-start.13
  172.9 16.3 %collective-permute-done.10.refs_0_ = bf16[768,256]{1,0:T(8,128)(2,1)S(1)} collective-permute-done((bf16[768,256]{1,0:T(8,128)(2,1)S(1)}, bf16[768,256]{1,0:T(8,128)(2,1)S(1)}, u32[]{:S(2)}, u32[]{:S(2)}) %collective-permute-start.10) | collective-permute-done | bytes 393248 | tf_op jit(solution)/shard_map/ppermute | solution.py:254
  189.1 7.4 %collective-permute-done.11.refs_1_ = bf16[768,256]{1,0:T(8,128)(2,1)S(1)} collective-permute-done((bf16[768,256]{1,0:T(8,128)(2,1)S(1)}, bf16[768,256]{1,0:T(8,128)(2,1)S(1)}, u32[]{:S(2)}, u32[]{:S(2)}) %collective-permute-start.11) | collective-permute-done | bytes 393248 | tf_op jit(solution)/shard_map/ppermute | solution.py:254
  196.5 1.0 collective-permute-done.12.refs_2_
  197.6 0.0 collective-permute-done.13.refs_3_
  197.6 0.7 sum_permute.1
  198.3 36.8 %all_to_all.22.in_ref = bf16[16,3,16,256]{3,2,1,0:T(8,128)(2,1)S(1)} all-to-all(bf16[16,3,16,256]{3,2,1,0:T(8,128)(2,1)S(1)} %bitcast.17), channel_id=1, replica_groups=mesh['segment'=8,'x'=4,'zh'=4,'tp'=4] {'x','zh'}, dimensions={0} | all-to-all | bytes 786432 | tf_op jit(solution)/shard_map/all_to_all | solution.py:185
  235.1 0.0 copy-done.2
  235.1 0.8 finish.1
  (8 shorter events, 0.2 us)
Async XLA Ops:
  0.0 7.5 %collective-permute-start = (bf16[192,1024]{1,0:T(8,128)(2,1)}, bf16[192,1024]{1,0:T(8,128)(2,1)S(1)}, u32[]{:S(2)}, u32[]{:S(2)}) collective-permute-start(bf16[192,1024]{1,0:T(8,128)(2,1)} %bitcast.25), channel_id=1, source_target_pairs={{0,448},{64,0},{128,64},{192,128},{256,192},{320,256},{384,320},{4... | collective-permute-start | bytes 1179656 | tf_op jit(solution)/shard_map/ppermute | solution.py:209
  7.9 50.6 %copy-start.5 = (bf16[1,1024,256]{2,1,0:T(8,128)(2,1)S(1)}, bf16[1,1024,256]{2,1,0:T(8,128)(2,1)}, u32[]{:S(2)}) copy-start(bf16[1,1024,256]{2,1,0:T(8,128)(2,1)} %param.13) | copy-start | bytes 1572868
  7.9 52.5 %copy-start.3 = (s32[1,3,2]{1,2,0:T(2,128)S(1)}, s32[1,3,2]{1,2,0:T(2,128)}, u32[]{:S(2)}) copy-start(s32[1,3,2]{1,2,0:T(2,128)} %param.11) | copy-start | bytes 76
  7.9 79.4 %copy-start = (bf16[1,3,256,1024]{3,2,1,0:T(8,128)(2,1)S(1)}, bf16[1,3,256,1024]{3,2,1,0:T(8,128)(2,1)}, u32[]{:S(2)}) copy-start(bf16[1,3,256,1024]{3,2,1,0:T(8,128)(2,1)} %param.9) | copy-start | bytes 4718596
  54.9 32.4 %all-to-all-start.1 = ((bf16[16,3,32,128]{3,2,1,0:T(8,128)(2,1)}), bf16[16,3,32,128]{3,2,1,0:T(8,128)(2,1)S(1)}, u32[]{:S(2)}, u32[]{:S(2)}) async-start(bf16[16,3,32,128]{3,2,1,0:T(8,128)(2,1)} %bitcast.3), calls=%async_computation.1 | async-start | bytes 786432 | tf_op jit(solution)/shard_map/all_to_all | solution.py:185
  58.5 8.6 %collective-permute-start.2 = (bf16[1024,256]{1,0:T(8,128)(2,1)S(1)}, bf16[1024,256]{1,0:T(8,128)(2,1)S(1)}, u32[]{:S(2)}, u32[]{:S(2)}) collective-permute-start(bf16[1024,256]{1,0:T(8,128)(2,1)S(1)} %bitcast.24), channel_id=1, source_target_pairs={{0,448},{64,0},{128,64},{192,128},{256,192},{320,256},{384,320},{4... | collective-permute-start | bytes 1572872 | tf_op jit(solution)/shard_map/ppermute | solution.py:222
  59.0 8.1 %collective-permute-start.1 = (s32[48]{0:T(128)S(1)}, s32[48]{0:T(128)S(1)}, u32[]{:S(2)}, u32[]{:S(2)}) collective-permute-start(s32[48]{0:T(128)S(1)} %select_reduce_fusion), channel_id=1, source_target_pairs={{0,64},{64,128},{128,192},{192,256},{256,320},{320,384},{384,448},... | collective-permute-start | bytes 584 | tf_op jit(solution)/shard_map/ppermute | solution.py:231
  87.3 1.4 copy-start.1
  91.3 54.0 %copy-start.4 = (s32[4]{0:T(128)S(1)}, s32[4]{0:T(128)}, u32[]{:S(2)}) copy-start(s32[4]{0:T(128)} %constant.74.clone) | copy-start | bytes 52
  100.7 35.3 %collective-permute-start.3 = (bf16[192,1024]{1,0:T(8,128)(2,1)S(1)}, bf16[192,1024]{1,0:T(8,128)(2,1)S(1)}, u32[]{:S(2)}, u32[]{:S(2)}) collective-permute-start(bf16[192,1024]{1,0:T(8,128)(2,1)S(1)} %bitcast.18), channel_id=1, source_target_pairs={{0,4},{4,8},{8,12},{12,0},{1,5},{5,9},{9,13},{13,1},{2,6},{6,10},{... | collective-permute-start | bytes 1179656 | tf_op jit(solution)/shard_map/ppermute | solution.py:189
  102.6 36.8 %collective-permute-start.4 = (bf16[192,1024]{1,0:T(8,128)(2,1)S(1)}, bf16[192,1024]{1,0:T(8,128)(2,1)S(1)}, u32[]{:S(2)}, u32[]{:S(2)}) collective-permute-start(bf16[192,1024]{1,0:T(8,128)(2,1)S(1)} %bitcast.19), channel_id=1, source_target_pairs={{0,12},{4,0},{8,4},{12,8},{1,13},{5,1},{9,5},{13,9},{2,14},{6,2},{... | collective-permute-start | bytes 1179656 | tf_op jit(solution)/shard_map/ppermute | solution.py:189
  109.9 35.4 %collective-permute-start.9 = (bf16[1024,256]{1,0:T(8,128)(2,1)S(1)}, bf16[1024,256]{1,0:T(8,128)(2,1)S(1)}, u32[]{:S(2)}, u32[]{:S(2)}) collective-permute-start(bf16[1024,256]{1,0:T(8,128)(2,1)S(1)} %collective-permute-done.2.refs_5_), channel_id=1, source_target_pairs={{0,16},{16,32},{32,48},{48,0},{1,17},{17,33},{33,49},{49,1},{2,18}... | collective-permute-start | bytes 1572872 | tf_op jit(solution)/shard_map/ppermute | solution.py:189
  112.1 33.2 %collective-permute-start.8 = (bf16[1024,256]{1,0:T(8,128)(2,1)S(1)}, bf16[1024,256]{1,0:T(8,128)(2,1)S(1)}, u32[]{:S(2)}, u32[]{:S(2)}) collective-permute-start(bf16[1024,256]{1,0:T(8,128)(2,1)S(1)} %collective-permute-done.2.refs_5_), channel_id=1, source_target_pairs={{0,32},{16,48},{32,0},{48,16},{1,33},{17,49},{33,1},{49,17},{2,34}... | collective-permute-start | bytes 1572872 | tf_op jit(solution)/shard_map/ppermute | solution.py:189
  115.8 29.5 %collective-permute-start.7 = (bf16[1024,256]{1,0:T(8,128)(2,1)S(1)}, bf16[1024,256]{1,0:T(8,128)(2,1)}, u32[]{:S(2)}, u32[]{:S(2)}) collective-permute-start(bf16[1024,256]{1,0:T(8,128)(2,1)S(1)} %collective-permute-done.2.refs_5_), channel_id=1, source_target_pairs={{0,48},{16,0},{32,16},{48,32},{1,49},{17,1},{33,17},{49,33},{2,50}... | collective-permute-start | bytes 1572872 | tf_op jit(solution)/shard_map/ppermute | solution.py:189
  136.1 19.2 %collective-permute-start.5 = (bf16[112,1024]{1,0:T(8,128)(2,1)S(1)}, bf16[112,1024]{1,0:T(8,128)(2,1)S(1)}, u32[]{:S(2)}, u32[]{:S(2)}) collective-permute-start(bf16[112,1024]{1,0:T(8,128)(2,1)S(1)} %slice.13), channel_id=1, source_target_pairs={{0,4},{4,8},{8,12},{12,0},{1,5},{5,9},{9,13},{13,1},{2,6},{6,10},{... | collective-permute-start | bytes 688136 | tf_op jit(solution)/shard_map/ppermute | solution.py:189
  139.5 10.7 %collective-permute-start.6 = (bf16[80,1024]{1,0:T(8,128)(2,1)S(1)}, bf16[80,1024]{1,0:T(8,128)(2,1)S(1)}, u32[]{:S(2)}, u32[]{:S(2)}) collective-permute-start(bf16[80,1024]{1,0:T(8,128)(2,1)S(1)} %slice.14), channel_id=1, source_target_pairs={{0,12},{4,0},{8,4},{12,8},{1,13},{5,1},{9,5},{13,9},{2,14},{6,2},{... | collective-permute-start | bytes 491528 | tf_op jit(solution)/shard_map/ppermute | solution.py:189
  158.8 76.3 %copy-start.2 = (bf16[1,192,1024]{2,1,0:T(8,128)(2,1)S(1)}, bf16[1,192,1024]{2,1,0:T(8,128)(2,1)}, u32[]{:S(2)}) copy-start(bf16[1,192,1024]{2,1,0:T(8,128)(2,1)} %param.14) | copy-start | bytes 1179652
  158.9 30.3 %collective-permute-start.10 = (bf16[768,256]{1,0:T(8,128)(2,1)S(1)}, bf16[768,256]{1,0:T(8,128)(2,1)S(1)}, u32[]{:S(2)}, u32[]{:S(2)}) collective-permute-start(bf16[768,256]{1,0:T(8,128)(2,1)S(1)} %get-tuple-element.19), channel_id=1, source_target_pairs={{0,66},{1,67},{2,64},{3,65},{64,130},{65,131},{66,128},{67,129},{1... | collective-permute-start | bytes 1179656 | tf_op jit(solution)/shard_map/ppermute | solution.py:254
  166.9 29.7 %collective-permute-start.11 = (bf16[768,256]{1,0:T(8,128)(2,1)S(1)}, bf16[768,256]{1,0:T(8,128)(2,1)S(1)}, u32[]{:S(2)}, u32[]{:S(2)}) collective-permute-start(bf16[768,256]{1,0:T(8,128)(2,1)S(1)} %get-tuple-element.20), channel_id=1, source_target_pairs={{0,65},{1,66},{2,67},{3,64},{64,129},{65,130},{66,131},{67,128},{1... | collective-permute-start | bytes 1179656 | tf_op jit(solution)/shard_map/ppermute | solution.py:254
  168.8 28.8 %collective-permute-start.12 = (bf16[768,256]{1,0:T(8,128)(2,1)S(1)}, bf16[768,256]{1,0:T(8,128)(2,1)S(1)}, u32[]{:S(2)}, u32[]{:S(2)}) collective-permute-start(bf16[768,256]{1,0:T(8,128)(2,1)S(1)} %get-tuple-element.21), channel_id=1, source_target_pairs={{0,67},{1,64},{2,65},{3,66},{64,131},{65,128},{66,129},{67,130},{1... | collective-permute-start | bytes 1179656 | tf_op jit(solution)/shard_map/ppermute | solution.py:254
  170.7 26.8 %collective-permute-start.13 = (bf16[768,256]{1,0:T(8,128)(2,1)S(1)}, bf16[768,256]{1,0:T(8,128)(2,1)S(1)}, u32[]{:S(2)}, u32[]{:S(2)}) collective-permute-start(bf16[768,256]{1,0:T(8,128)(2,1)S(1)} %get-tuple-element.22), channel_id=1, source_target_pairs={{0,64},{1,65},{2,66},{3,67},{64,128},{65,129},{66,130},{67,131},{1... | collective-permute-start | bytes 1179656 | tf_op jit(solution)/shard_map/ppermute | solution.py:254

commit v7 on v6

--- a/solution.py
+++ b/solution.py
@@ -50,8 +50,15 @@
     )(order, spread)
 
 
-def attend_kernel(len_ref, q_ref, k_ref, v_ref, out_ref):
+def attend_kernel(len_ref, q_ref, k_ref, values_ref, out_ref, held_ref, sem):
     slot = pl.program_id(0)
+    slots = held_ref.shape[0]
+
+    @pl.when(slot == 0)
+    def _():
+        for each in range(slots):
+            pltpu.make_async_copy(values_ref.at[each], held_ref.at[each], sem.at[each]).start()
+
     span = k_ref.shape[1]
     heads = k_ref.shape[2] // HD
     groups = q_ref.shape[1]
@@ -76,9 +83,10 @@
         masked = jnp.where(valid, scores[head] * (1.0 / math.sqrt(HD)), -1e30)
         expo = jnp.exp(masked - jnp.max(masked, axis=-1, keepdims=True))
         weights.append((expo / jnp.sum(expo, axis=-1, keepdims=True)).astype(jnp.bfloat16))
+    pltpu.make_async_copy(values_ref.at[slot], held_ref.at[slot], sem.at[slot]).wait()
     for head in range(heads):
         mixed = jnp.dot(
-            weights[head], v_ref[0, :, lanes[head]], preferred_element_type=jnp.float32
+            weights[head], held_ref[slot, :, lanes[head]], preferred_element_type=jnp.float32
         )
         out_ref[:, 0, :, lanes[head]] = mixed.astype(jnp.bfloat16).reshape(G, ROWS, HD)
 
@@ -95,9 +103,13 @@
             SMEM,
             pl.BlockSpec((G, groups, 1, feats // G // HD, ROWS, HD), lambda s: (0, chunk, s, 0, 0, 0)),
             pl.BlockSpec((1, span, wide), lambda s: (s, 0, chunk)),
-            pl.BlockSpec((1, span, wide), lambda s: (s, 0, chunk)),
+            pl.BlockSpec(memory_space=pltpu.HBM),
         ],
         out_specs=pl.BlockSpec((G, 1, ROWS, wide), lambda s: (0, s, 0, 0)),
+        scratch_shapes=[
+            pltpu.VMEM((slots, span, wide), values.dtype),
+            pltpu.SemaphoreType.DMA((slots,)),
+        ],
         compiler_params=PARAMS,
         cost_estimate=cost(4 * slots * STRETCH * span * wide, 4 * slots * span * wide),
         name="attend",

time: 237 us -> 237 us (level)
  no operation moved by 1% of the time
where the time goes in v7:
time: 237 us
  blocking collectives  91.9 us (39%)
  waiting for transfers between devices  85.3 us (36%)
  starting transfers between devices  46.8 us (20%)
  Pallas kernels  9.67 us (4%)
    all_to_all x3, blocking collectives, exchange(): return lax.all_to_all(value, axes, split_axis=0, concat_axis=0, tiled=True)  91.9 us
    ppermute x7, waiting for transfers between devices, turn(): return lax.ppermute(value, axis, [(i, (i + by) % G) for i in range(G)])  27.6 us
    ppermute x7, starting transfers between devices, turn(): return lax.ppermute(value, axis, [(i, (i + by) % G) for i in range(G)])  26.8 us
    ppermute x4, waiting for transfers between devices, local(): arrived.append(lax.ppermute(block, ('segment', 'tp'), moves))  24.7 us
    all_to_all x1, waiting for transfers between devices, exchange(): return lax.all_to_all(value, axes, split_axis=0, concat_axis=0, tiled=True)  20.2 us
    ppermute x4, starting transfers between devices, local(): arrived.append(lax.ppermute(block, ('segment', 'tp'), moves))  14 us
    ppermute x1, waiting for transfers between devices, local(): own = lax.ppermute(out_weight[0], 'segment', back)  6.61 us
    ppermute x1, waiting for transfers between devices, local(): moved = lax.ppermute(queries[0], 'segment', back)  6.18 us
  transfers between devices with their start and end apart: 15, of which 9 were waited for; matrix products, arithmetic and copies ran while one was open for 0% of the time, Pallas kernels for 0%

profile of v7, /device:TPU:73, one launch (start us, length us, event | category | flops | bytes accessed | tf_op | source)
XLA Modules:
  0.0 236.7 jit_solution(2943882021273398353)
XLA Ops:
  0.0 0.7 collective-permute-start
  0.7 0.7 convert_element_type.16
  1.3 6.2 %collective-permute-done = bf16[192,1024]{1,0:T(8,128)(2,1)S(1)} collective-permute-done((bf16[192,1024]{1,0:T(8,128)(2,1)}, bf16[192,1024]{1,0:T(8,128)(2,1)S(1)}, u32[]{:S(2)}, u32[]{:S(2)}) %collective-permute-start) | collective-permute-done | bytes 393248 | tf_op jit(solution)/shard_map/ppermute | solution.py:221
  7.5 0.3 reshape.93
  7.8 0.1 copy.13
  7.9 0.0 copy-start.5
  7.9 0.0 copy-start.3
  7.9 0.0 copy-start
  8.0 45.3 %all_to_all.20.in_ref = bf16[16,104,128]{2,1,0:T(8,128)(2,1)S(1)} all-to-all(bf16[16,104,128]{2,1,0:T(8,128)(2,1)S(1)} %pad_maximum_fusion), channel_id=1, replica_groups=mesh['segment'=8,'x'=4,'zh'=4,'tp'=4] {'x','zh'}, dimensions={0} | all-to-all | bytes 851968 | tf_op jit(solution)/shard_map/all_to_all | solution.py:197
  53.3 0.1 reshape.99.order_ref
  53.4 1.5 permute_blocks.1
  54.9 3.6 %all-to-all-start.1 = ((bf16[16,3,32,128]{3,2,1,0:T(8,128)(2,1)}), bf16[16,3,32,128]{3,2,1,0:T(8,128)(2,1)S(1)}, u32[]{:S(2)}, u32[]{:S(2)}) async-start(bf16[16,3,32,128]{3,2,1,0:T(8,128)(2,1)} %bitcast.3), calls=%async_computation.1 | async-start | bytes 786432 | tf_op jit(solution)/shard_map/all_to_all | solution.py:197
  58.5 0.0 copy-done.5
  58.5 0.4 collective-permute-start.2
  58.9 0.1 select_reduce_fusion
  59.0 1.4 collective-permute-start.1
  60.4 0.0 copy-done.3
  60.4 0.1 copy.14.len_ref
  60.5 6.6 %collective-permute-done.2.refs_5_ = bf16[1024,256]{1,0:T(8,128)(2,1)S(1)} collective-permute-done((bf16[1024,256]{1,0:T(8,128)(2,1)S(1)}, bf16[1024,256]{1,0:T(8,128)(2,1)S(1)}, u32[]{:S(2)}, u32[]{:S(2)}) %collective-permute-start.2) | collective-permute-done | bytes 524320 | tf_op jit(solution)/shard_map/ppermute | solution.py:234
  67.1 0.0 collective-permute-done.1.order_ref
  67.1 20.2 %all-to-all-done.1 = bf16[16,3,32,128]{3,2,1,0:T(8,128)(2,1)S(1)} async-done(((bf16[16,3,32,128]{3,2,1,0:T(8,128)(2,1)}), bf16[16,3,32,128]{3,2,1,0:T(8,128)(2,1)S(1)}, u32[]{:S(2)}, u32[]{:S(2)}) %all-to-all-start.1) | async-done | bytes 393248 | tf_op jit(solution)/shard_map/all_to_all | solution.py:197
  87.3 0.0 copy-done
  87.3 0.0 copy-start.1
  87.3 1.4 copy-done.1
  88.7 3.0 %attend.1 = bf16[4,3,16,1024]{3,2,1,0:T(8,128)(2,1)S(1)} custom-call(s32[3,2]{1,0:T(4,128)S(1)} %copy.14.len_ref, bf16[4,4,3,2,16,128]{5,4,3,2,1,0:T(8,128)(2,1)S(1)} %bitcast.16, bf16[3,256,1024]{2,1,0:T(8,128)(2,1)S(1)} %bitcast.14, bf16[3,256,1024]{2,1,0:T(8,128)(2,1)S(1)} %bitcast.15), custom_call_target="tpu_custom_call" | custom-call | flops 201326592 | bytes 3145728 | tf_op jit(solution)/shard_map/attend/pallas_call | solution.py:98
  91.6 0.0 copy-start.4
  91.7 9.4 %all_to_all.21 = bf16[4,3,16,1024]{3,2,1,0:T(8,128)(2,1)S(1)} all-to-all(bf16[4,3,16,1024]{3,2,1,0:T(8,128)(2,1)S(1)} %attend.1), channel_id=1, replica_groups=mesh['segment'=8,'x'=4,'zh'=4,'tp'=4] {'x'}, dimensions={0} | all-to-all | bytes 786432 | tf_op jit(solution)/shard_map/all_to_all | solution.py:197
  101.1 1.9 collective-permute-start.3
  103.0 7.3 %collective-permute-start.4 = (bf16[192,1024]{1,0:T(8,128)(2,1)S(1)}, bf16[192,1024]{1,0:T(8,128)(2,1)S(1)}, u32[]{:S(2)}, u32[]{:S(2)}) collective-permute-start(bf16[192,1024]{1,0:T(8,128)(2,1)S(1)} %bitcast.19), channel_id=1, source_target_pairs={{0,12},{4,0},{8,4},{12,8},{1,13},{5,1},{9,5},{13,9},{2,14},{6,2},{... | collective-permute-start | bytes 1179656 | tf_op jit(solution)/shard_map/ppermute | solution.py:201
  110.3 2.2 collective-permute-start.9
  112.5 3.7 %collective-permute-start.8 = (bf16[1024,256]{1,0:T(8,128)(2,1)S(1)}, bf16[1024,256]{1,0:T(8,128)(2,1)S(1)}, u32[]{:S(2)}, u32[]{:S(2)}) collective-permute-start(bf16[1024,256]{1,0:T(8,128)(2,1)S(1)} %collective-permute-done.2.refs_5_), channel_id=1, source_target_pairs={{0,32},{16,48},{32,0},{48,16},{1,33},{17,49},{33,1},{49,17},{2,34}... | collective-permute-start | bytes 1572872 | tf_op jit(solution)/shard_map/ppermute | solution.py:201
  116.2 2.5 %collective-permute-start.7 = (bf16[1024,256]{1,0:T(8,128)(2,1)S(1)}, bf16[1024,256]{1,0:T(8,128)(2,1)}, u32[]{:S(2)}, u32[]{:S(2)}) collective-permute-start(bf16[1024,256]{1,0:T(8,128)(2,1)S(1)} %collective-permute-done.2.refs_5_), channel_id=1, source_target_pairs={{0,48},{16,0},{32,16},{48,32},{1,49},{17,1},{33,17},{49,33},{2,50}... | collective-permute-start | bytes 1572872 | tf_op jit(solution)/shard_map/ppermute | solution.py:201
  118.7 17.9 %collective-permute-done.3.refs_1_ = bf16[192,1024]{1,0:T(8,128)(2,1)S(1)} collective-permute-done((bf16[192,1024]{1,0:T(8,128)(2,1)S(1)}, bf16[192,1024]{1,0:T(8,128)(2,1)S(1)}, u32[]{:S(2)}, u32[]{:S(2)}) %collective-permute-start.3) | collective-permute-done | bytes 393248 | tf_op jit(solution)/shard_map/ppermute | solution.py:201
  136.7 3.3 %collective-permute-start.5 = (bf16[112,1024]{1,0:T(8,128)(2,1)S(1)}, bf16[112,1024]{1,0:T(8,128)(2,1)S(1)}, u32[]{:S(2)}, u32[]{:S(2)}) collective-permute-start(bf16[112,1024]{1,0:T(8,128)(2,1)S(1)} %slice.13), channel_id=1, source_target_pairs={{0,4},{4,8},{8,12},{12,0},{1,5},{5,9},{9,13},{13,1},{2,6},{6,10},{... | collective-permute-start | bytes 688136 | tf_op jit(solution)/shard_map/ppermute | solution.py:201
  140.0 0.0 collective-permute-done.4.refs_2_
  140.0 5.9 %collective-permute-start.6 = (bf16[80,1024]{1,0:T(8,128)(2,1)S(1)}, bf16[80,1024]{1,0:T(8,128)(2,1)S(1)}, u32[]{:S(2)}, u32[]{:S(2)}) collective-permute-start(bf16[80,1024]{1,0:T(8,128)(2,1)S(1)} %slice.14), channel_id=1, source_target_pairs={{0,12},{4,0},{8,4},{12,8},{1,13},{5,1},{9,5},{13,9},{2,14},{6,2},{... | collective-permute-start | bytes 491528 | tf_op jit(solution)/shard_map/ppermute | solution.py:201
  145.9 0.0 copy-done.4
  145.9 0.0 collective-permute-done.9.refs_8_
  145.9 0.0 collective-permute-done.8.refs_7_
  145.9 0.0 collective-permute-done.7.refs_6_
  146.0 4.8 %collective-permute-done.6.refs_4_ = bf16[80,1024]{1,0:T(8,128)(2,1)S(1)} collective-permute-done((bf16[80,1024]{1,0:T(8,128)(2,1)S(1)}, bf16[80,1024]{1,0:T(8,128)(2,1)S(1)}, u32[]{:S(2)}, u32[]{:S(2)}) %collective-permute-start.6) | collective-permute-done | bytes 163872 | tf_op jit(solution)/shard_map/ppermute | solution.py:201
  150.8 4.9 %collective-permute-done.5.refs_3_ = bf16[112,1024]{1,0:T(8,128)(2,1)S(1)} collective-permute-done((bf16[112,1024]{1,0:T(8,128)(2,1)S(1)}, bf16[112,1024]{1,0:T(8,128)(2,1)S(1)}, u32[]{:S(2)}, u32[]{:S(2)}) %collective-permute-start.5) | collective-permute-done | bytes 229408 | tf_op jit(solution)/shard_map/ppermute | solution.py:201
  155.6 3.6 %project.1 = (bf16[768,256]{1,0:T(8,128)(2,1)S(1)}, bf16[768,256]{1,0:T(8,128)(2,1)S(1)}, bf16[768,256]{1,0:T(8,128)(2,1)S(1)}, bf16[768,256]{1,0:T(8,128)(2,1)S(1)}) custom-call(s32[4]{0:T(128)S(1)} %and_select_fusion.order_ref, bf16[192,1024]{1,0:T(8,128)(2,1)S(1)} %bitcast.20, bf16[192,1024]{1,0:T(8,128)(2,1)S(1)} %collective-permute-done.3.refs_1_, ...), custom_call_target="tpu_custom_call" | custom-call | flops 1610612736 | bytes 5242880 | tf_op jit(solution)/shard_map/project/pallas_call | solution.py:137
  159.2 0.0 copy-start.2
  159.2 7.3 %collective-permute-start.10 = (bf16[768,256]{1,0:T(8,128)(2,1)S(1)}, bf16[768,256]{1,0:T(8,128)(2,1)S(1)}, u32[]{:S(2)}, u32[]{:S(2)}) collective-permute-start(bf16[768,256]{1,0:T(8,128)(2,1)S(1)} %get-tuple-element.19), channel_id=1, source_target_pairs={{0,66},{1,67},{2,64},{3,65},{64,130},{65,131},{66,128},{67,129},{1... | collective-permute-start | bytes 1179656 | tf_op jit(solution)/shard_map/ppermute | solution.py:266
  166.5 1.9 collective-permute-start.11
  168.5 1.9 collective-permute-start.12
  170.4 2.9 %collective-permute-start.13 = (bf16[768,256]{1,0:T(8,128)(2,1)S(1)}, bf16[768,256]{1,0:T(8,128)(2,1)S(1)}, u32[]{:S(2)}, u32[]{:S(2)}) collective-permute-start(bf16[768,256]{1,0:T(8,128)(2,1)S(1)} %get-tuple-element.22), channel_id=1, source_target_pairs={{0,64},{1,65},{2,66},{3,67},{64,128},{65,129},{66,130},{67,131},{1... | collective-permute-start | bytes 1179656 | tf_op jit(solution)/shard_map/ppermute | solution.py:266
  173.3 16.3 %collective-permute-done.10.refs_0_ = bf16[768,256]{1,0:T(8,128)(2,1)S(1)} collective-permute-done((bf16[768,256]{1,0:T(8,128)(2,1)S(1)}, bf16[768,256]{1,0:T(8,128)(2,1)S(1)}, u32[]{:S(2)}, u32[]{:S(2)}) %collective-permute-start.10) | collective-permute-done | bytes 393248 | tf_op jit(solution)/shard_map/ppermute | solution.py:266
  189.6 7.5 %collective-permute-done.11.refs_1_ = bf16[768,256]{1,0:T(8,128)(2,1)S(1)} collective-permute-done((bf16[768,256]{1,0:T(8,128)(2,1)S(1)}, bf16[768,256]{1,0:T(8,128)(2,1)S(1)}, u32[]{:S(2)}, u32[]{:S(2)}) %collective-permute-start.11) | collective-permute-done | bytes 393248 | tf_op jit(solution)/shard_map/ppermute | solution.py:266
  197.1 0.9 collective-permute-done.12.refs_2_
  198.0 0.0 collective-permute-done.13.refs_3_
  198.0 0.7 sum_permute.1
  198.7 37.2 %all_to_all.22.in_ref = bf16[16,3,16,256]{3,2,1,0:T(8,128)(2,1)S(1)} all-to-all(bf16[16,3,16,256]{3,2,1,0:T(8,128)(2,1)S(1)} %bitcast.17), channel_id=1, replica_groups=mesh['segment'=8,'x'=4,'zh'=4,'tp'=4] {'x','zh'}, dimensions={0} | all-to-all | bytes 786432 | tf_op jit(solution)/shard_map/all_to_all | solution.py:197
  235.9 0.0 copy-done.2
  235.9 0.8 finish.1
  (8 shorter events, 0.2 us)
Async XLA Ops:
  0.0 7.5 %collective-permute-start = (bf16[192,1024]{1,0:T(8,128)(2,1)}, bf16[192,1024]{1,0:T(8,128)(2,1)S(1)}, u32[]{:S(2)}, u32[]{:S(2)}) collective-permute-start(bf16[192,1024]{1,0:T(8,128)(2,1)} %bitcast.25), channel_id=1, source_target_pairs={{0,448},{64,0},{128,64},{192,128},{256,192},{320,256},{384,320},{4... | collective-permute-start | bytes 1179656 | tf_op jit(solution)/shard_map/ppermute | solution.py:221
  7.9 50.6 %copy-start.5 = (bf16[1,1024,256]{2,1,0:T(8,128)(2,1)S(1)}, bf16[1,1024,256]{2,1,0:T(8,128)(2,1)}, u32[]{:S(2)}) copy-start(bf16[1,1024,256]{2,1,0:T(8,128)(2,1)} %param.13) | copy-start | bytes 1572868
  7.9 52.5 %copy-start.3 = (s32[1,3,2]{1,2,0:T(2,128)S(1)}, s32[1,3,2]{1,2,0:T(2,128)}, u32[]{:S(2)}) copy-start(s32[1,3,2]{1,2,0:T(2,128)} %param.11) | copy-start | bytes 76
  7.9 79.4 %copy-start = (bf16[1,3,256,1024]{3,2,1,0:T(8,128)(2,1)S(1)}, bf16[1,3,256,1024]{3,2,1,0:T(8,128)(2,1)}, u32[]{:S(2)}) copy-start(bf16[1,3,256,1024]{3,2,1,0:T(8,128)(2,1)} %param.9) | copy-start | bytes 4718596
  54.9 32.4 %all-to-all-start.1 = ((bf16[16,3,32,128]{3,2,1,0:T(8,128)(2,1)}), bf16[16,3,32,128]{3,2,1,0:T(8,128)(2,1)S(1)}, u32[]{:S(2)}, u32[]{:S(2)}) async-start(bf16[16,3,32,128]{3,2,1,0:T(8,128)(2,1)} %bitcast.3), calls=%async_computation.1 | async-start | bytes 786432 | tf_op jit(solution)/shard_map/all_to_all | solution.py:197
  58.5 8.6 %collective-permute-start.2 = (bf16[1024,256]{1,0:T(8,128)(2,1)S(1)}, bf16[1024,256]{1,0:T(8,128)(2,1)S(1)}, u32[]{:S(2)}, u32[]{:S(2)}) collective-permute-start(bf16[1024,256]{1,0:T(8,128)(2,1)S(1)} %bitcast.24), channel_id=1, source_target_pairs={{0,448},{64,0},{128,64},{192,128},{256,192},{320,256},{384,320},{4... | collective-permute-start | bytes 1572872 | tf_op jit(solution)/shard_map/ppermute | solution.py:234
  59.0 8.1 %collective-permute-start.1 = (s32[48]{0:T(128)S(1)}, s32[48]{0:T(128)S(1)}, u32[]{:S(2)}, u32[]{:S(2)}) collective-permute-start(s32[48]{0:T(128)S(1)} %select_reduce_fusion), channel_id=1, source_target_pairs={{0,64},{64,128},{128,192},{192,256},{256,320},{320,384},{384,448},... | collective-permute-start | bytes 584 | tf_op jit(solution)/shard_map/ppermute | solution.py:243
  87.3 1.4 copy-start.1
  91.6 54.3 %copy-start.4 = (s32[4]{0:T(128)S(1)}, s32[4]{0:T(128)}, u32[]{:S(2)}) copy-start(s32[4]{0:T(128)} %constant.74.clone) | copy-start | bytes 52
  101.1 35.5 %collective-permute-start.3 = (bf16[192,1024]{1,0:T(8,128)(2,1)S(1)}, bf16[192,1024]{1,0:T(8,128)(2,1)S(1)}, u32[]{:S(2)}, u32[]{:S(2)}) collective-permute-start(bf16[192,1024]{1,0:T(8,128)(2,1)S(1)} %bitcast.18), channel_id=1, source_target_pairs={{0,4},{4,8},{8,12},{12,0},{1,5},{5,9},{9,13},{13,1},{2,6},{6,10},{... | collective-permute-start | bytes 1179656 | tf_op jit(solution)/shard_map/ppermute | solution.py:201
  103.0 37.0 %collective-permute-start.4 = (bf16[192,1024]{1,0:T(8,128)(2,1)S(1)}, bf16[192,1024]{1,0:T(8,128)(2,1)S(1)}, u32[]{:S(2)}, u32[]{:S(2)}) collective-permute-start(bf16[192,1024]{1,0:T(8,128)(2,1)S(1)} %bitcast.19), channel_id=1, source_target_pairs={{0,12},{4,0},{8,4},{12,8},{1,13},{5,1},{9,5},{13,9},{2,14},{6,2},{... | collective-permute-start | bytes 1179656 | tf_op jit(solution)/shard_map/ppermute | solution.py:201
  110.3 35.6 %collective-permute-start.9 = (bf16[1024,256]{1,0:T(8,128)(2,1)S(1)}, bf16[1024,256]{1,0:T(8,128)(2,1)S(1)}, u32[]{:S(2)}, u32[]{:S(2)}) collective-permute-start(bf16[1024,256]{1,0:T(8,128)(2,1)S(1)} %collective-permute-done.2.refs_5_), channel_id=1, source_target_pairs={{0,16},{16,32},{32,48},{48,0},{1,17},{17,33},{33,49},{49,1},{2,18}... | collective-permute-start | bytes 1572872 | tf_op jit(solution)/shard_map/ppermute | solution.py:201
  112.5 33.4 %collective-permute-start.8 = (bf16[1024,256]{1,0:T(8,128)(2,1)S(1)}, bf16[1024,256]{1,0:T(8,128)(2,1)S(1)}, u32[]{:S(2)}, u32[]{:S(2)}) collective-permute-start(bf16[1024,256]{1,0:T(8,128)(2,1)S(1)} %collective-permute-done.2.refs_5_), channel_id=1, source_target_pairs={{0,32},{16,48},{32,0},{48,16},{1,33},{17,49},{33,1},{49,17},{2,34}... | collective-permute-start | bytes 1572872 | tf_op jit(solution)/shard_map/ppermute | solution.py:201
  116.2 29.8 %collective-permute-start.7 = (bf16[1024,256]{1,0:T(8,128)(2,1)S(1)}, bf16[1024,256]{1,0:T(8,128)(2,1)}, u32[]{:S(2)}, u32[]{:S(2)}) collective-permute-start(bf16[1024,256]{1,0:T(8,128)(2,1)S(1)} %collective-permute-done.2.refs_5_), channel_id=1, source_target_pairs={{0,48},{16,0},{32,16},{48,32},{1,49},{17,1},{33,17},{49,33},{2,50}... | collective-permute-start | bytes 1572872 | tf_op jit(solution)/shard_map/ppermute | solution.py:201
  136.7 19.0 %collective-permute-start.5 = (bf16[112,1024]{1,0:T(8,128)(2,1)S(1)}, bf16[112,1024]{1,0:T(8,128)(2,1)S(1)}, u32[]{:S(2)}, u32[]{:S(2)}) collective-permute-start(bf16[112,1024]{1,0:T(8,128)(2,1)S(1)} %slice.13), channel_id=1, source_target_pairs={{0,4},{4,8},{8,12},{12,0},{1,5},{5,9},{9,13},{13,1},{2,6},{6,10},{... | collective-permute-start | bytes 688136 | tf_op jit(solution)/shard_map/ppermute | solution.py:201
  140.0 10.7 %collective-permute-start.6 = (bf16[80,1024]{1,0:T(8,128)(2,1)S(1)}, bf16[80,1024]{1,0:T(8,128)(2,1)S(1)}, u32[]{:S(2)}, u32[]{:S(2)}) collective-permute-start(bf16[80,1024]{1,0:T(8,128)(2,1)S(1)} %slice.14), channel_id=1, source_target_pairs={{0,12},{4,0},{8,4},{12,8},{1,13},{5,1},{9,5},{13,9},{2,14},{6,2},{... | collective-permute-start | bytes 491528 | tf_op jit(solution)/shard_map/ppermute | solution.py:201
  159.2 76.7 %copy-start.2 = (bf16[1,192,1024]{2,1,0:T(8,128)(2,1)S(1)}, bf16[1,192,1024]{2,1,0:T(8,128)(2,1)}, u32[]{:S(2)}) copy-start(bf16[1,192,1024]{2,1,0:T(8,128)(2,1)} %param.14) | copy-start | bytes 1179652
  159.2 30.3 %collective-permute-start.10 = (bf16[768,256]{1,0:T(8,128)(2,1)S(1)}, bf16[768,256]{1,0:T(8,128)(2,1)S(1)}, u32[]{:S(2)}, u32[]{:S(2)}) collective-permute-start(bf16[768,256]{1,0:T(8,128)(2,1)S(1)} %get-tuple-element.19), channel_id=1, source_target_pairs={{0,66},{1,67},{2,64},{3,65},{64,130},{65,131},{66,128},{67,129},{1... | collective-permute-start | bytes 1179656 | tf_op jit(solution)/shard_map/ppermute | solution.py:266
  166.5 30.5 %collective-permute-start.11 = (bf16[768,256]{1,0:T(8,128)(2,1)S(1)}, bf16[768,256]{1,0:T(8,128)(2,1)S(1)}, u32[]{:S(2)}, u32[]{:S(2)}) collective-permute-start(bf16[768,256]{1,0:T(8,128)(2,1)S(1)} %get-tuple-element.20), channel_id=1, source_target_pairs={{0,65},{1,66},{2,67},{3,64},{64,129},{65,130},{66,131},{67,128},{1... | collective-permute-start | bytes 1179656 | tf_op jit(solution)/shard_map/ppermute | solution.py:266
  168.5 29.5 %collective-permute-start.12 = (bf16[768,256]{1,0:T(8,128)(2,1)S(1)}, bf16[768,256]{1,0:T(8,128)(2,1)S(1)}, u32[]{:S(2)}, u32[]{:S(2)}) collective-permute-start(bf16[768,256]{1,0:T(8,128)(2,1)S(1)} %get-tuple-element.21), channel_id=1, source_target_pairs={{0,67},{1,64},{2,65},{3,66},{64,131},{65,128},{66,129},{67,130},{1... | collective-permute-start | bytes 1179656 | tf_op jit(solution)/shard_map/ppermute | solution.py:266
  170.4 27.6 %collective-permute-start.13 = (bf16[768,256]{1,0:T(8,128)(2,1)S(1)}, bf16[768,256]{1,0:T(8,128)(2,1)S(1)}, u32[]{:S(2)}, u32[]{:S(2)}) collective-permute-start(bf16[768,256]{1,0:T(8,128)(2,1)S(1)} %get-tuple-element.22), channel_id=1, source_target_pairs={{0,64},{1,65},{2,66},{3,67},{64,128},{65,129},{66,130},{67,131},{1... | collective-permute-start | bytes 1179656 | tf_op jit(solution)/shard_map/ppermute | solution.py:266
